TPU v7x, 32 devices: a whole 2x2x4 slice. The times are simulated.
32 devices in a mesh: dp: 16 (over z, x, core), seq: 2 (over y).
Axes of the slice: x: 2, y: 2, z: 4, core: 2. Of those that a mesh axis runs over, the one named last changes fastest.
Arguments:
- tokens: float32 [32, 2048, 512], P('dp', 'seq'), may hold values from -6 to 6
- lengths: int32 [32], P('dp'), may hold values from 512 to 2048, as said below
- joint_weight: float32 [512, 1536], P(('dp', 'seq')), may hold values from -0.375 to 0.375
- joint_bias: float32 [1024], P(('dp', 'seq')), may hold values from -2 to 2
- out_weight: float32 [512, 512], P(('dp', 'seq')), may hold values from -1 to 1
- out_bias: float32 [512], P(('dp', 'seq')), may hold values from -2 to 2
- gain_first: float32 [512], P(('dp', 'seq')), may hold values from 0.5 to 1.5
- shift_first: float32 [512], P(('dp', 'seq')), may hold values from -2 to 2
- up_weight: float32 [512, 2048], P(('dp', 'seq')), may hold values from -0.25 to 0.25
- up_bias: float32 [2048], P(('dp', 'seq')), may hold values from -2 to 2
- down_weight: float32 [2048, 512], P(('dp', 'seq')), may hold values from -0.1875 to 0.1875
- down_bias: float32 [512], P(('dp', 'seq')), may hold values from -2 to 2
- gain_second: float32 [512], P(('dp', 'seq')), may hold values from 0.5 to 1.5
- shift_second: float32 [512], P(('dp', 'seq')), may hold values from -2 to 2
- cotangent: float32 [32, 2048, 512], P('dp', 'seq'), may hold values from -6 to 6
Outputs:
- layer_output: float32 [32, 2048, 512], P('dp', 'seq')
- input_grad: float32 [32, 2048, 512], P('dp', 'seq')
- joint_weight_grad: float32 [512, 1536], P(('dp', 'seq'))
- joint_bias_grad: float32 [1024], P(('dp', 'seq'))
- out_weight_grad: float32 [512, 512], P(('dp', 'seq'))
- out_bias_grad: float32 [512], P(('dp', 'seq'))
- gain_first_grad: float32 [512], P(('dp', 'seq'))
- shift_first_grad: float32 [512], P(('dp', 'seq'))
- up_weight_grad: float32 [512, 2048], P(('dp', 'seq'))
- up_bias_grad: float32 [2048], P(('dp', 'seq'))
- down_weight_grad: float32 [2048, 512], P(('dp', 'seq'))
- down_bias_grad: float32 [512], P(('dp', 'seq'))
- gain_second_grad: float32 [512], P(('dp', 'seq'))
- shift_second_grad: float32 [512], P(('dp', 'seq'))
Inputs may be any that keep to these rules, and one draw needn't show every extreme that they name: `lengths`: in each aligned block of 2 sequences (those of one index of dp) one sequence has the full length 2048.
All inputs are finite; a program needn't handle non-finite values.
Results may differ from a plain program's by a relative error of at most 0.013.
The roundings to bfloat16 on the way count: a program that leaves them out, or rounds other values in their place, can miss the bound.
Values may be sent and summed in bfloat16 or wider, within the bound.
A program may use at most 256 MiB of HBM per device.

v0:
```python
import math

import jax
import jax.numpy as jnp
from jax import lax
from jax.sharding import PartitionSpec as P

H = 8
HEAD = 64


def norm_parts(value):
    centred = value - jnp.mean(value, axis=-1, keepdims=True)
    inverse = lax.rsqrt(jnp.mean(centred * centred, axis=-1, keepdims=True) + 1e-05)
    return (centred * inverse, inverse)


def norm_back(grad_norm, normal, inverse):
    return inverse * (
        grad_norm
        - jnp.mean(grad_norm, axis=-1, keepdims=True)
        - normal * jnp.mean(grad_norm * normal, axis=-1, keepdims=True)
    )


def per_device(
    tokens,
    lengths,
    joint_weight,
    joint_bias,
    out_weight,
    out_bias,
    gain_first,
    shift_first,
    up_weight,
    up_bias,
    down_weight,
    down_bias,
    gain_second,
    shift_second,
    cotangent,
):
    gathered = (
        lax.all_gather(joint_weight.astype(jnp.bfloat16), ("dp", "seq"), axis=0, tiled=True),
        lax.all_gather(joint_bias.astype(jnp.bfloat16), ("dp", "seq"), axis=0, tiled=True),
        lax.all_gather(out_weight.astype(jnp.bfloat16), ("dp", "seq"), axis=0, tiled=True),
        lax.all_gather(out_bias.astype(jnp.bfloat16), ("dp", "seq"), axis=0, tiled=True),
        lax.all_gather(gain_first.astype(jnp.bfloat16), ("dp", "seq"), axis=0, tiled=True),
        lax.all_gather(shift_first.astype(jnp.bfloat16), ("dp", "seq"), axis=0, tiled=True),
        lax.all_gather(up_weight.astype(jnp.bfloat16), ("dp", "seq"), axis=0, tiled=True),
        lax.all_gather(up_bias.astype(jnp.bfloat16), ("dp", "seq"), axis=0, tiled=True),
        lax.all_gather(down_weight.astype(jnp.bfloat16), ("dp", "seq"), axis=0, tiled=True),
        lax.all_gather(down_bias.astype(jnp.bfloat16), ("dp", "seq"), axis=0, tiled=True),
        lax.all_gather(gain_second.astype(jnp.bfloat16), ("dp", "seq"), axis=0, tiled=True),
        lax.all_gather(shift_second.astype(jnp.bfloat16), ("dp", "seq"), axis=0, tiled=True),
    )
    (
        joint_full,
        pair_full,
        out_full,
        out_shift,
        first_gain,
        first_shift,
        up_full,
        up_shift,
        down_full,
        down_shift,
        second_gain,
        second_shift,
    ) = gathered
    groups, local_len, width = tokens.shape
    seq_parts = lax.axis_size("seq")
    head_dim = HEAD
    heads_here = H // seq_parts
    seq_len = local_len * seq_parts
    block_rows = min(512, seq_len)
    blocks = seq_len // block_rows
    scaling = 1.0 / math.sqrt(head_dim)
    all_rows = groups * local_len
    flat_rows = tokens.reshape(all_rows, width)
    flat_low = flat_rows.astype(jnp.bfloat16)
    bias_pair = pair_full.astype(jnp.float32).reshape(H, 2, head_dim)
    bias_full = jnp.stack(
        [bias_pair[:, 0], jnp.zeros_like(bias_pair[:, 0]), bias_pair[:, 1]], axis=1
    ).reshape(3 * width)
    joint = jnp.dot(flat_low, joint_full, preferred_element_type=jnp.float32) + bias_full
    joint_sent = joint.astype(jnp.bfloat16).reshape(
        groups, local_len, seq_parts, 3 * width // seq_parts
    )
    arrived = lax.all_to_all(joint_sent, "seq", split_axis=2, concat_axis=1, tiled=True)
    arrived = arrived.reshape(groups, seq_len, heads_here, 3, head_dim)
    query_all = arrived[:, :, :, 0]
    keys_all = arrived[:, :, :, 1]
    values_all = arrived[:, :, :, 2]
    key_valid = lax.broadcasted_iota(jnp.int32, (groups, seq_len), 1) < lengths[:, None]

    def forward_block(index):
        group = index // blocks
        offset = index % blocks * block_rows
        query_group = lax.dynamic_index_in_dim(query_all, group, 0, keepdims=False)
        keys_group = lax.dynamic_index_in_dim(keys_all, group, 0, keepdims=False)
        values_group = lax.dynamic_index_in_dim(values_all, group, 0, keepdims=False)
        valid_group = lax.dynamic_index_in_dim(key_valid, group, 0, keepdims=False)
        picked = lax.dynamic_slice_in_dim(query_group, offset, block_rows, 0)
        scores = (
            jnp.einsum("qhd,khd->hqk", picked, keys_group, preferred_element_type=jnp.float32)
            * scaling
        )
        scores = jnp.where(valid_group[None, None, :], scores, -1e30)
        largest = jnp.max(scores, axis=-1, keepdims=True)
        log_total = largest + jnp.log(jnp.sum(jnp.exp(scores - largest), axis=-1, keepdims=True))
        weights = jnp.exp(scores - log_total).astype(jnp.bfloat16)
        block_out = jnp.einsum(
            "hqk,khd->qhd", weights, values_group, preferred_element_type=jnp.float32
        )
        return (block_out, log_total[..., 0])

    mixed_out, log_totals = lax.map(forward_block, jnp.arange(groups * blocks, dtype=jnp.int32))
    heads_low = mixed_out.astype(jnp.bfloat16).reshape(groups, seq_len, 1, heads_here * head_dim)
    returned = lax.all_to_all(heads_low, "seq", split_axis=1, concat_axis=2, tiled=True).reshape(
        all_rows, width
    )
    attn_out = jnp.dot(returned, out_full, preferred_element_type=jnp.float32) + out_shift.astype(
        jnp.float32
    )
    hidden = flat_rows + attn_out
    norm_first, inverse_first = norm_parts(hidden)
    normal_one = norm_first * first_gain.astype(jnp.float32) + first_shift.astype(jnp.float32)
    normal_low = normal_one.astype(jnp.bfloat16)
    inner_pre = jnp.dot(normal_low, up_full, preferred_element_type=jnp.float32) + up_shift.astype(
        jnp.float32
    )
    active = jax.nn.gelu(inner_pre).astype(jnp.bfloat16)
    branch = jnp.dot(active, down_full, preferred_element_type=jnp.float32) + down_shift.astype(
        jnp.float32
    )
    norm_second, inverse_second = norm_parts(normal_one + branch + flat_rows)
    result = norm_second * second_gain.astype(jnp.float32) + second_shift.astype(jnp.float32)
    grad_out = cotangent.reshape(all_rows, width)
    gain_second_grad = jnp.sum(grad_out * norm_second, axis=0)
    shift_second_grad = jnp.sum(grad_out, axis=0)
    back_sum = norm_back(grad_out * second_gain.astype(jnp.float32), norm_second, inverse_second)
    branch_grad = back_sum.astype(jnp.bfloat16)
    down_weight_grad = jnp.dot(active.T, branch_grad, preferred_element_type=jnp.float32)
    down_bias_grad = jnp.sum(branch_grad.astype(jnp.float32), axis=0)
    active_grad = jnp.dot(branch_grad, down_full.T, preferred_element_type=jnp.float32)
    gelu_value, gelu_pull = jax.vjp(jax.nn.gelu, inner_pre)
    inner_grad = gelu_pull(active_grad)[0].astype(jnp.bfloat16)
    up_weight_grad = jnp.dot(normal_low.T, inner_grad, preferred_element_type=jnp.float32)
    up_bias_grad = jnp.sum(inner_grad.astype(jnp.float32), axis=0)
    norm_grad = back_sum + jnp.dot(inner_grad, up_full.T, preferred_element_type=jnp.float32)
    gain_first_grad = jnp.sum(norm_grad * norm_first, axis=0)
    shift_first_grad = jnp.sum(norm_grad, axis=0)
    hidden_grad = norm_back(norm_grad * first_gain.astype(jnp.float32), norm_first, inverse_first)
    attn_grad = hidden_grad.astype(jnp.bfloat16)
    out_weight_grad = jnp.dot(returned.T, attn_grad, preferred_element_type=jnp.float32)
    out_bias_grad = jnp.sum(attn_grad.astype(jnp.float32), axis=0)
    heads_grad = jnp.dot(attn_grad, out_full.T, preferred_element_type=jnp.float32).astype(
        jnp.bfloat16
    )
    heads_grad = heads_grad.reshape(groups, local_len, seq_parts, width // seq_parts)
    grad_mixed = lax.all_to_all(heads_grad, "seq", split_axis=2, concat_axis=1, tiled=True)
    grad_mixed = grad_mixed.reshape(groups, blocks, block_rows, heads_here, head_dim)
    query_blocks = query_all.reshape(groups, blocks, block_rows, heads_here, head_dim)
    log_blocks = log_totals.reshape(groups, blocks, heads_here, block_rows)

    def backward_group(pieces):
        query_split, keys_group, values_group, grad_split, log_split, valid_group = pieces

        def one_block(carried, inputs_block):
            grad_keys, grad_values = carried
            picked, grad_picked, log_picked = inputs_block
            scores = (
                jnp.einsum("qhd,khd->hqk", picked, keys_group, preferred_element_type=jnp.float32)
                * scaling
            )
            scores = jnp.where(valid_group[None, None, :], scores, -1e30)
            weights = jnp.exp(scores - log_picked[..., None])
            grad_values = grad_values + jnp.einsum(
                "hqk,qhd->khd",
                weights.astype(jnp.bfloat16),
                grad_picked,
                preferred_element_type=jnp.float32,
            )
            pulled = jnp.einsum(
                "qhd,khd->hqk", grad_picked, values_group, preferred_element_type=jnp.float32
            )
            centre = jnp.sum(pulled * weights, axis=-1, keepdims=True)
            score_grad = (weights * (pulled - centre)).astype(jnp.bfloat16)
            grad_query = (
                jnp.einsum(
                    "hqk,khd->qhd", score_grad, keys_group, preferred_element_type=jnp.float32
                )
                * scaling
            )
            grad_keys = (
                grad_keys
                + jnp.einsum("hqk,qhd->khd", score_grad, picked, preferred_element_type=jnp.float32)
                * scaling
            )
            return ((grad_keys, grad_values), grad_query)

        empty_grad = jnp.zeros((seq_len, heads_here, head_dim), jnp.float32)
        (grad_keys, grad_values), grad_query = lax.scan(
            one_block, (empty_grad, empty_grad), (query_split, grad_split, log_split)
        )
        return (grad_query.reshape(seq_len, heads_here, head_dim), grad_keys, grad_values)

    grad_query, grad_keys, grad_values = lax.map(
        backward_group, (query_blocks, keys_all, values_all, grad_mixed, log_blocks, key_valid)
    )
    joint_grad = jnp.stack([grad_query, grad_keys, grad_values], axis=3).astype(jnp.bfloat16)
    joint_grad = joint_grad.reshape(groups, seq_len, 1, 3 * width // seq_parts)
    grad_back = lax.all_to_all(joint_grad, "seq", split_axis=1, concat_axis=2, tiled=True).reshape(
        all_rows, 3 * width
    )
    joint_weight_grad = jnp.dot(flat_low.T, grad_back, preferred_element_type=jnp.float32)
    column_sums = jnp.sum(grad_back.astype(jnp.float32), axis=0).reshape(H, 3, head_dim)
    joint_bias_grad = jnp.stack([column_sums[:, 0], column_sums[:, 2]], axis=1).reshape(2 * width)
    input_grad = (
        back_sum
        + hidden_grad
        + jnp.dot(grad_back, joint_full.T, preferred_element_type=jnp.float32)
    )
    summed = (
        lax.psum_scatter(joint_weight_grad, ("dp", "seq"), scatter_dimension=0, tiled=True),
        lax.psum_scatter(joint_bias_grad, ("dp", "seq"), scatter_dimension=0, tiled=True),
        lax.psum_scatter(out_weight_grad, ("dp", "seq"), scatter_dimension=0, tiled=True),
        lax.psum_scatter(out_bias_grad, ("dp", "seq"), scatter_dimension=0, tiled=True),
        lax.psum_scatter(gain_first_grad, ("dp", "seq"), scatter_dimension=0, tiled=True),
        lax.psum_scatter(shift_first_grad, ("dp", "seq"), scatter_dimension=0, tiled=True),
        lax.psum_scatter(up_weight_grad, ("dp", "seq"), scatter_dimension=0, tiled=True),
        lax.psum_scatter(up_bias_grad, ("dp", "seq"), scatter_dimension=0, tiled=True),
        lax.psum_scatter(down_weight_grad, ("dp", "seq"), scatter_dimension=0, tiled=True),
        lax.psum_scatter(down_bias_grad, ("dp", "seq"), scatter_dimension=0, tiled=True),
        lax.psum_scatter(gain_second_grad, ("dp", "seq"), scatter_dimension=0, tiled=True),
        lax.psum_scatter(shift_second_grad, ("dp", "seq"), scatter_dimension=0, tiled=True),
    )
    return (
        result.reshape(groups, local_len, width),
        input_grad.reshape(groups, local_len, width),
        summed[0],
        summed[1],
        summed[2],
        summed[3],
        summed[4],
        summed[5],
        summed[6],
        summed[7],
        summed[8],
        summed[9],
        summed[10],
        summed[11],
    )


def solution(mesh):
    placed = (
        P("dp", "seq", None),
        P("dp"),
        P(("dp", "seq"), None),
        P(("dp", "seq")),
        P(("dp", "seq"), None),
        P(("dp", "seq")),
        P(("dp", "seq")),
        P(("dp", "seq")),
        P(("dp", "seq"), None),
        P(("dp", "seq")),
        P(("dp", "seq"), None),
        P(("dp", "seq")),
        P(("dp", "seq")),
        P(("dp", "seq")),
        P("dp", "seq", None),
    )
    return jax.shard_map(
        per_device,
        mesh=mesh,
        in_specs=placed,
        out_specs=(
            P("dp", "seq", None),
            P("dp", "seq", None),
            P(("dp", "seq"), None),
            P(("dp", "seq")),
            P(("dp", "seq"), None),
            P(("dp", "seq")),
            P(("dp", "seq")),
            P(("dp", "seq")),
            P(("dp", "seq"), None),
            P(("dp", "seq")),
            P(("dp", "seq"), None),
            P(("dp", "seq")),
            P(("dp", "seq")),
            P(("dp", "seq")),
        ),
        check_vma=False,
    )
```

profile of v0, /device:TPU:0, one launch (start us, length us, event | category | flops | bytes accessed | tf_op | source)
XLA Modules:
  0.0 1514.9 jit_solution(5746477486238127279)
XLA Ops:
  17.4 42.2 %all-reduce.17 = (bf16[1024]{0:T(1024)(128)(2,1)S(1)}, bf16[512]{0:T(512)(128)(2,1)S(1)}, bf16[512]{0:T(512)(128)(2,1)S(1)}, bf16[512]{0:T(512)(128)(2,1)S(1)}, ...) all-reduce(bf16[1024]{0:T(1024)(128)(2,1)S(1)} %dynamic-update-slic, ...), channel_id=1, replica_groups=mesh['dp'=16,'seq'=2] {'dp','seq'}, use_global_device_ids=true, to_apply=%add | all-reduce | flops 6144 | bytes 24576
  76.1 13.6 reshape.208
  89.6 16.2 %copy.67 = bf16[2,1024,2,768]{1,3,0,2:T(8,128)(2,1)} copy(bf16[2,1024,2,768]{3,2,1,0:T(2,128)(2,1)} %reshape.208) | data formatting | bytes 12582912 | tf_op jit(solution)/shard_map/reshape | solution.py:87
  113.2 78.4 %all-to-all-done = bf16[2,1024,2,768]{1,3,0,2:T(8,128)(2,1)} async-done(((bf16[2,1024,2,768]{1,3,0,2:T(8,128)(2,1)}), bf16[2,1024,2,768]{1,3,0,2:T(8,128)(2,1)}, u32[]{:S(2)}, u32[]{:S(2)}) %all-to-all-start) | async-done | bytes 6291488 | tf_op jit(solution)/shard_map/all_to_all | solution.py:90
  191.6 12.7 copy.68
  204.2 11.1 reshape.209
  222.1 138.7 %while.44 = (s32[]{:T(128)}, bf16[8,512,4,64]{1,3,2,0:T(8,128)(2,1)}, f32[8,4,512]{2,1,0:T(4,128)}, s32[8]{0:T(128)S(1)}, bf16[2,2048,4,64]{1,3,2,0:T(8,128)(2,1...) while((s32[]{:T(128)}, ...), condition=%wide.region_3.4_spmd, body=%wide.region_0.3_spmd.sunk | while | flops 1119877120 | bytes 53291512 | solution.py:118
  381.6 81.9 %all_gather.38 = bf16[512,512]{1,0:T(8,128)(2,1)S(1)} all-gather(bf16[16,512]{1,0:T(8,128)(2,1)S(1)} %convert_element_type.134), channel_id=1, replica_groups=mesh['dp'=16,'seq'=2] {'dp','seq'}, dimensions={0}, use_global_device_ids=true | all-gather | bytes 540672 | tf_op jit(solution)/shard_map/all_gather | solution.py:46
  470.9 13.3 fusion.63
  484.2 13.7 fusion.71
  506.8 20.5 %convert_reduce_fusion = (f32[2048]{0:T(1024)}, bf16[2048,2048]{1,0:T(8,128)(2,1)}) fusion(f32[2048,2048]{1,0:T(8,128)} %fusion.63, f32[2048]{0:T(1024)S(1)} %convert_element_type.144, bf16[2048,512]{1,0:T(8,128)(2,1)} %all-gather.8.cloned.1.call-done, f32[2048,512]{1,0:T(8,128)S(1)} %get-tuple-element.475), kind=kOutput, calls=%fused_computation.73 | convolution fusion | flops 4392482816 | bytes 31473664 | tf_op jit(solution)/shard_map/dot_general | solution.py:146
  559.6 19.9 %all-to-all-done.2 = bf16[2,1024,2,256]{1,3,0,2:T(8,128)(2,1)} async-done(((bf16[2,1024,2,256]{1,3,0,2:T(8,128)(2,1)}), bf16[2,1024,2,256]{1,3,0,2:T(8,128)(2,1)}, u32[]{:S(2)}, u32[]{:S(2)}) %all-to-all-start.2) | async-done | bytes 2097184 | tf_op jit(solution)/shard_map/all_to_all | solution.py:162
  585.4 364.4 %while.46 = (s32[]{:T(128)}, bf16[2,2048,4,64]{1,3,2,0:T(8,128)(2,1)}, bf16[2,2048,4,64]{1,3,2,0:T(8,128)(2,1)}, bf16[2,2048,4,64]{1,3,2,0:T(8,128)(2,1)}, bf16[...) while((s32[]{:T(128)}, ...), condition=%wide.region_16.17_spmd, body=%wide.region_12.16_spmd.sunk | while | flops 2750019584 | bytes 225086048 | solution.py:209
  593.0 163.0 %while.47 = (s32[]{:T(128)}, f32[2048,4,64]{0,2,1:T(8,128)}, f32[2048,4,64]{0,2,1:T(8,128)}, bf16[4,512,4,64]{1,3,2,0:T(8,128)(2,1)}, bf16[4,512,4,64]{1,3,2,0:T...) while((s32[]{:T(128)}, f32[2048,4,64]{0,2,1:T(8,128)}, ...), condition=%wide.region_15.15_spmd.clone, body=%wide.region_13.14_spmd.clone.sunk | while | flops 2750019584 | bytes 172554416 | solution.py:204
  774.9 163.0 %while.47 = (s32[]{:T(128)}, f32[2048,4,64]{0,2,1:T(8,128)}, f32[2048,4,64]{0,2,1:T(8,128)}, bf16[4,512,4,64]{1,3,2,0:T(8,128)(2,1)}, bf16[4,512,4,64]{1,3,2,0:T...) while((s32[]{:T(128)}, f32[2048,4,64]{0,2,1:T(8,128)}, ...), condition=%wide.region_15.15_spmd.clone, body=%wide.region_13.14_spmd.clone.sunk | while | flops 2750019584 | bytes 172554416 | solution.py:204
  956.0 16.3 %copy.80 = bf16[2,2048,1,768]{3,0,2,1:T(2,128)(2,1)} copy(bf16[2,2048,1,768]{1,3,0,2:T(8,128)(2,1)} %bitcast.220) | data formatting | bytes 12582912 | tf_op jit(solution)/shard_map/convert_element_type | solution.py:212
  983.3 74.0 %all-to-all-done.3 = bf16[2,2048,1,768]{3,0,2,1:T(2,128)(2,1)} async-done(((bf16[2,2048,1,768]{3,0,2,1:T(2,128)(2,1)}), bf16[2,2048,1,768]{3,0,2,1:T(2,128)(2,1)}, u32[]{:S(2)}, u32[]{:S(2)}) %all-to-all-start.3) | async-done | bytes 6291488 | tf_op jit(solution)/shard_map/all_to_all | solution.py:214
  1060.9 45.6 %copy.82 = bf16[2,1024,2,1,768]{4,2,1,0,3:T(2,128)(2,1)S(1)} copy(bf16[2,1024,2,1,768]{4,1,2,0,3:T(8,128)(2,1)S(1)} %bitcast.218) | data formatting | bytes 12582912 | tf_op jit(solution)/shard_map/all_to_all | solution.py:214
  1116.5 13.8 fusion.58
  1131.0 11.6 fusion.61
  1146.8 38.6 %all-reduce.16 = (f32[1024]{0:T(1024)S(1)}, f32[512]{0:T(512)S(1)}, f32[512]{0:T(512)S(1)}, f32[512]{0:T(512)S(1)}, f32[2048]{0:T(1024)S(1)}, /*index=5*/f32[512]{0:T(512)S(1)}, f32[512]{0:T(512)S(1)}, f32[512]{0:T(512)S(1)}) all-reduce(f32[1024]{0:T(1024)S(1)} %reshape.220, ...), channel_id=3, replica_groups=mesh['dp'=16,'seq'=2] {'dp','seq'}, use_global_device_ids=true, to_apply=%region_19.20.clone | all-reduce | flops 6144 | bytes 49152
  1199.2 23.0 %reduce-scatter.13.cloned.1.call-done = f32[16,1536]{1,0:T(8,128)} async-done(((f32[512,1536]{1,0:T(8,128)}), f32[16,1536]{1,0:T(8,128)}) %reduce-scatter.13.cloned.1.call-update) | async-done | bytes 98320
  1222.2 143.9 %reduce-scatter.11.cloned.1.call-done = f32[64,512]{1,0:T(8,128)} async-done(((f32[2048,512]{1,0:T(8,128)}), f32[64,512]{1,0:T(8,128)}) %reduce-scatter.11.cloned.1.call-update) | async-done | bytes 131088 | tf_op jit(solution)/shard_map/reduce_scatter | solution.py:234
  1366.1 141.7 %reduce-scatter.9.cloned.1.call-done = f32[16,2048]{1,0:T(8,128)} async-done(((f32[512,2048]{1,0:T(8,128)}), f32[16,2048]{1,0:T(8,128)}) %reduce-scatter.9.cloned.1.call-update) | async-done | bytes 131088 | tf_op jit(solution)/shard_map/reduce_scatter | solution.py:232
  (357 shorter events, 646.2 us)
Async XLA Ops:
  7.2 62.2 %all-gather.4.cloned.1.call-start = ((), (), s32[]{:S(2)}) async-start(), calls=%async_computation.8 | async-start | bytes 1622016 | tf_op jit(solution)/shard_map/all_gather | solution.py:44
  8.8 462.1 %all-gather.6.cloned.1.call-start = ((), (), s32[]{:S(2)}) async-start(), calls=%async_computation.9 | async-start | bytes 2162688 | tf_op jit(solution)/shard_map/all_gather | solution.py:50
  105.8 7.3 copy-start.37
  105.8 85.8 %all-to-all-start = ((bf16[2,1024,2,768]{1,3,0,2:T(8,128)(2,1)}), bf16[2,1024,2,768]{1,3,0,2:T(8,128)(2,1)}, u32[]{:S(2)}, u32[]{:S(2)}) async-start(bf16[2,1024,2,768]{1,3,0,2:T(8,128)(2,1)} %copy.67), calls=%async_computation | async-start | bytes 12582912 | tf_op jit(solution)/shard_map/all_to_all | solution.py:90
  112.2 372.0 %all-gather.8.cloned.1.call-start = ((), (), s32[]{:S(2)}) async-start(), calls=%async_computation.10 | async-start | bytes 2162688 | tf_op jit(solution)/shard_map/all_gather | solution.py:52
  374.3 89.3 %all-to-all-start.1 = ((bf16[2,2048,1,256]{3,0,2,1:T(2,128)(2,1)}), bf16[2,2048,1,256]{3,0,2,1:T(2,128)(2,1)S(1)}, u32[]{:S(2)}, u32[]{:S(2)}) async-start(bf16[2,2048,1,256]{3,0,2,1:T(2,128)(2,1)} %copy.70), calls=%async_computation.1 | async-start | bytes 4194304 | tf_op jit(solution)/shard_map/all_to_all | solution.py:120
  378.2 159.9 %copy-start.28 = (f32[512]{0:T(512)}, f32[512]{0:T(512)S(1)}, u32[]{:S(2)}) copy-start(f32[512]{0:T(512)S(1)} %convert_element_type.138) | copy-start | bytes 6148
  378.2 106.0 %copy-start.35 = (f32[512]{0:T(512)}, f32[512]{0:T(512)S(1)}, u32[]{:S(2)}) copy-start(f32[512]{0:T(512)S(1)} %convert_element_type.140) | copy-start | bytes 6148
  378.3 128.6 %copy-start.31 = (f32[2048]{0:T(1024)}, f32[2048]{0:T(1024)S(1)}, u32[]{:S(2)}) copy-start(f32[2048]{0:T(1024)S(1)} %convert_element_type.144) | copy-start | bytes 24580
  468.0 70.1 %copy-start.19 = (f32[2048]{0:T(1024)}, f32[2048]{0:T(1024)S(1)}, u32[]{:S(2)}) copy-start(f32[2048]{0:T(1024)S(1)} %broadcast_multiply_fusion.4) | copy-start | bytes 24580
  470.9 67.2 %copy-start.22 = (f32[2048]{0:T(1024)}, f32[2048]{0:T(1024)S(1)}, u32[]{:S(2)}) copy-start(f32[2048]{0:T(1024)S(1)} %add_rsqrt_fusion.1) | copy-start | bytes 24580
  506.8 20.5 %copy-start.14 = (f32[2048,512]{1,0:T(8,128)}, f32[2048,512]{1,0:T(8,128)S(1)}, u32[]{:S(2)}) copy-start(f32[2048,512]{1,0:T(8,128)S(1)} %get-tuple-element.475) | copy-start | bytes 12582916
  506.8 20.5 %copy-start.6 = (f32[2048,512]{1,0:T(8,128)S(1)}, f32[2048,512]{1,0:T(8,128)}, u32[]{:S(2)}) copy-start(f32[2048,512]{1,0:T(8,128)} %copy-done.5) | copy-start | bytes 12582916
  545.7 11.1 copy-start.12
  552.0 27.6 %all-to-all-start.2 = ((bf16[2,1024,2,256]{1,3,0,2:T(8,128)(2,1)}), bf16[2,1024,2,256]{1,3,0,2:T(8,128)(2,1)}, u32[]{:S(2)}, u32[]{:S(2)}) async-start(bf16[2,1024,2,256]{1,3,0,2:T(8,128)(2,1)} %copy.73), calls=%async_computation.2 | async-start | bytes 4194304 | tf_op jit(solution)/shard_map/all_to_all | solution.py:162
  756.0 8.2 copy-start.1
  937.9 8.3 copy-start.1
  972.3 85.0 %all-to-all-start.3 = ((bf16[2,2048,1,768]{3,0,2,1:T(2,128)(2,1)}), bf16[2,2048,1,768]{3,0,2,1:T(2,128)(2,1)}, u32[]{:S(2)}, u32[]{:S(2)}) async-start(bf16[2,2048,1,768]{3,0,2,1:T(2,128)(2,1)} %copy.80), calls=%async_computation.3 | async-start | bytes 12582912 | tf_op jit(solution)/shard_map/all_to_all | solution.py:214
  978.7 220.6 %reduce-scatter.7.cloned.1.call-start = ((), (), s32[]{:S(2)}) async-start(), calls=%async_computation.11 | async-start | bytes 1081344 | tf_op jit(solution)/shard_map/reduce_scatter | solution.py:228
  983.2 239.0 %reduce-scatter.13.cloned.1.call-start = ((), (), s32[]{:S(2)}) async-start(), calls=%async_computation.14 | async-start | bytes 3244032
  1060.9 45.6 %copy-start.2 = (bf16[2,2048,1,768]{3,1,0,2:T(8,128)(2,1)}, bf16[2,2048,1,768]{3,1,0,2:T(8,128)(2,1)S(1)}, u32[]{:S(2)}) copy-start(bf16[2,2048,1,768]{3,1,0,2:T(8,128)(2,1)S(1)} %copy.81) | copy-start | bytes 18874372
  1116.4 249.7 %reduce-scatter.11.cloned.1.call-start = ((), (), s32[]{:S(2)}) async-start(), calls=%async_computation.13 | async-start | bytes 4325376 | tf_op jit(solution)/shard_map/reduce_scatter | solution.py:234
  1130.3 377.5 %reduce-scatter.9.cloned.1.call-start = ((), (), s32[]{:S(2)}) async-start(), calls=%async_computation.12 | async-start | bytes 4325376 | tf_op jit(solution)/shard_map/reduce_scatter | solution.py:232
  1142.6 47.5 %copy-start.38 = (bf16[512,1536]{1,0:T(8,128)(2,1)S(1)}, bf16[512,1536]{1,0:T(8,128)(2,1)}, u32[]{:S(2)}) copy-start(bf16[512,1536]{1,0:T(8,128)(2,1)} %all-gather.4.cloned.1.call-done) | copy-start | bytes 4718596
  (38 other events, 152.1 us)
Sparse Core Ops, SparseCore 0:
  11.5 57.8 all-gather.3
  73.1 57.8 all-gather.5
  134.6 58.6 all-gather.7
  983.3 134.0 reduce-scatter.6
  1124.1 98.0 reduce-scatter.12
  1225.0 141.0 reduce-scatter.10
  1369.1 138.7 reduce-scatter.8
where the time goes:
time: 1520 us; the launch traced here: 1510 us
  waiting for transfers between devices  485 us (32%)
  matrix products  429 us (28%)
  local copies, waits for them, and re-layouts  221 us (15%)
  blocking collectives  163 us (11%)
  other arithmetic  158 us (10%)
  starting transfers between devices  22.1 us (1%)
  loops' own time  21.8 us (1%)
    reduce_scatter x1, waiting for transfers between devices, per_device(): lax.psum_scatter(down_weight_grad, ('dp', 'seq'), scatter_dimension=0, ti...  144 us
    reduce_scatter x1, waiting for transfers between devices, per_device(): lax.psum_scatter(up_weight_grad, ('dp', 'seq'), scatter_dimension=0, tile...  142 us
    convert_element_type x8, other arithmetic, one_block(): score_grad = (weights * (pulled - centre)).astype(jnp.bfloat16)  84.7 us
    all_gather x1, blocking collectives, per_device(): lax.all_gather(out_weight.astype(jnp.bfloat16), ('dp', 'seq'), axis=0, ti...  81.9 us
    unnamed x2, blocking collectives  80.8 us
    all_to_all x1, waiting for transfers between devices, per_device(): lax.all_to_all(joint_sent, 'seq', split_axis=2, concat_axis=1, tiled=True)  78.4 us
    dot_general x8, matrix products, one_block(): jnp.einsum('qhd,khd->hqk', grad_picked, values_group, preferred_element_t...  74.8 us
    all_to_all x1, waiting for transfers between devices, per_device(): lax.all_to_all(joint_grad, 'seq', split_axis=1, concat_axis=2, tiled=True)  74 us
  transfers between devices with their start and end apart: 11, of which 7 were waited for; matrix products, arithmetic and copies ran while one was open for 23% of the time, Pallas kernels for 0%

commit v1 on v0

v1 whole, which is shorter than its diff:
```python
import functools
import math

import jax
import jax.numpy as jnp
from jax import lax
from jax.experimental import pallas as pl
from jax.experimental.pallas import tpu as pltpu
from jax.sharding import PartitionSpec as P

H = 8
HEAD = 64
PAIRS = H // 2
WIDE = 2 * HEAD
BF = jnp.bfloat16
F32 = jnp.float32
EPS = 1e-05
SCALE = 1.0 / math.sqrt(HEAD)
LOG2E = math.log2(math.e)
GELU_A = math.sqrt(2.0 / math.pi)
GELU_B = 0.044715
MESH = pl.DeviceIdType.MESH
MIB = 2**20
FORMS = {
    "nn": (((1,), (0,)), ((), ())),
    "nt": (((1,), (1,)), ((), ())),
    "tn": (((0,), (0,)), ((), ())),
}


def dot(left, right, form="nn"):
    return lax.dot_general(left, right, FORMS[form], preferred_element_type=F32)


def params(limit, steps):
    return pltpu.CompilerParams(
        vmem_limit_bytes=limit * MIB, dimension_semantics=("arbitrary",) * steps
    )


def log2(size):
    return size.bit_length() - 1


def gather_kernel(orders, bits_dp, bits_seq, *refs):
    count = len(orders)
    shards, fulls = refs[:count], refs[count : 2 * count]
    own_sem, send_sem, recv_sem = refs[2 * count :]
    dp, seq = lax.axis_index("dp"), lax.axis_index("seq")
    bits = bits_dp + bits_seq
    mine = [lax.rem(dp // 2 ** (bits_dp - 1 - b), 2) for b in range(bits_dp)]
    mine += [lax.rem(seq // 2 ** (bits_seq - 1 - b), 2) for b in range(bits_seq)]

    def partner(bit):
        if bit < bits_dp:
            return (dp + (1 - 2 * mine[bit]) * 2 ** (bits_dp - 1 - bit), seq)
        return (dp, seq + (1 - 2 * mine[bit]) * 2 ** (bits - 1 - bit))

    barrier = pltpu.get_barrier_semaphore()
    for bit in range(bits):
        pl.semaphore_signal(barrier, inc=1, device_id=partner(bit), device_id_type=MESH)
    local = [
        pltpu.make_async_copy(shard, full.at[tuple(mine)], own_sem.at[i])
        for i, (shard, full) in enumerate(zip(shards, fulls))
    ]
    for copy in local:
        copy.start()
    for copy in local:
        copy.wait()
    pl.semaphore_wait(barrier, bits)
    for stage in range(bits):
        copies = []
        for i, full in enumerate(fulls):
            done = orders[i][:stage]
            place = tuple(slice(None) if b in done else mine[b] for b in range(bits))
            copies.append(
                pltpu.make_async_remote_copy(
                    src_ref=full.at[place],
                    dst_ref=full.at[place],
                    send_sem=send_sem.at[stage, i],
                    recv_sem=recv_sem.at[stage, i],
                    device_id=partner(orders[i][stage]),
                    device_id_type=MESH,
                )
            )
        for copy in copies:
            copy.start()
        for copy in copies:
            copy.wait()


def gather_weights(shards, first):
    bits_dp, bits_seq = log2(lax.axis_size("dp")), log2(lax.axis_size("seq"))
    bits = bits_dp + bits_seq
    upper = list(range(bits_dp - 1))
    beside = list(range(bits_dp, bits))
    plans = (upper + beside + [bits_dp - 1], upper[:-1] + beside + upper[-1:] + [bits_dp - 1])
    orders = tuple(tuple(plans[p]) for p in first)
    count = len(shards)
    fulls = pl.pallas_call(
        functools.partial(gather_kernel, orders, bits_dp, bits_seq),
        out_shape=[jax.ShapeDtypeStruct((2,) * bits + s.shape, s.dtype) for s in shards],
        in_specs=[pl.BlockSpec(memory_space=pl.ANY)] * count,
        out_specs=[pl.BlockSpec(memory_space=pl.ANY)] * count,
        scratch_shapes=[
            pltpu.SemaphoreType.DMA((count,)),
            pltpu.SemaphoreType.DMA((bits, count)),
            pltpu.SemaphoreType.DMA((bits, count)),
        ],
        compiler_params=pltpu.CompilerParams(collective_id=0, has_side_effects=True),
        name="gather_weights",
    )(*shards)
    return [f.reshape((2**bits * s.shape[0],) + s.shape[1:]) for f, s in zip(fulls, shards)]


def owner_sums(arrays):
    size_dp, size_seq = lax.axis_size("dp"), lax.axis_size("seq")
    bits_dp, bits_seq = log2(size_dp), log2(size_seq)
    bits = bits_dp + bits_seq
    dp, seq = lax.axis_index("dp"), lax.axis_index("seq")
    rows = [a.shape[0] // (size_dp * size_seq) for a in arrays]
    arrays = [
        a.reshape((2,) * bits + (r,) + a.shape[1:]) for a, r in zip(arrays, rows)
    ]
    left = list(range(bits))
    order = [bits_dp - 1] + list(range(bits_dp, bits)) + list(range(bits_dp - 2, -1, -1))
    for bit in order:
        axis = left.index(bit)
        left.remove(bit)
        if bit < bits_dp:
            name, size, step, me = "dp", size_dp, 2 ** (bits_dp - 1 - bit), dp
        else:
            name, size, step, me = "seq", size_seq, 2 ** (bits - 1 - bit), seq
        mine = me // step % 2
        pairs = [(i, i ^ step) for i in range(size)]
        sent = [
            lax.dynamic_index_in_dim(a, 1 - mine, axis, keepdims=False).astype(BF) for a in arrays
        ]
        kept = [lax.dynamic_index_in_dim(a, mine, axis, keepdims=False) for a in arrays]
        arrived = [lax.ppermute(s, name, pairs) for s in sent]
        arrays = [k + a.astype(F32) for k, a in zip(kept, arrived)]
    return arrays


def attend_kernel(
    parts,
    groups,
    info,
    query,
    keys_own,
    values_own,
    keys_rest,
    values_rest,
    e_own,
    e_rest,
    mixed,
    mixed_t,
    inverse,
    k_ext,
    v_ext,
):
    local = keys_own.shape[1]
    block = query.shape[1]

    @pl.when(pl.program_id(2) == 0)
    def prepare():
        length = info[pl.program_id(0)]
        for part in range(parts):
            rows = slice(part * local, (part + 1) * local)
            if part == 0:
                keys, values = keys_own[0], values_own[0]
            else:
                inside = slice((part - 1) * local, part * local)
                keys, values = keys_rest[0, inside], values_rest[0, inside]
            k_ext[rows, :WIDE] = keys
            place = lax.broadcasted_iota(jnp.int32, (local, WIDE), 0) + info[groups + part]
            k_ext[rows, WIDE:] = jnp.where(place < length, 0.0, -1e30).astype(BF)
            turned = values.T
            v_ext[0, :HEAD, rows] = turned[:HEAD]
            v_ext[1, :HEAD, rows] = turned[HEAD:]
            v_ext[:, HEAD:, rows] = jnp.ones((2, HEAD, local), BF)

    turned = query[0].T
    zero = jnp.zeros((HEAD, block), BF)
    one = (lax.broadcasted_iota(jnp.int32, (WIDE, block), 0) == 0).astype(F32).astype(BF)
    heads = []
    for head in range(2):
        if head == 0:
            picked = jnp.concatenate([turned[:HEAD], zero, one], axis=0)
        else:
            picked = jnp.concatenate([zero, turned[HEAD:], one], axis=0)
        scores = dot(k_ext[...], picked)
        largest = jnp.max(scores, axis=0, keepdims=True)
        e = jnp.exp2((scores - largest) * (SCALE * LOG2E)).astype(BF)
        e_own[0, head] = e[:local]
        e_rest[0, head] = e[local:]
        out = dot(v_ext[head], e)
        inv = 1.0 / out[HEAD : HEAD + 1]
        inverse[0, 0, head : head + 1] = inv
        heads.append(out[:HEAD] * inv)
    both = jnp.concatenate(heads, axis=0).astype(BF)
    mixed_t[0] = both
    mixed[0] = both.T


def attend(info, joint_own, joint_rest, parts):
    groups, local, _ = joint_own.shape
    rest = joint_rest.shape[1]
    block = min(256, local)
    width = H * HEAD
    grid = (groups, PAIRS, local // block)
    return pl.pallas_call(
        functools.partial(attend_kernel, parts, groups),
        grid=grid,
        in_specs=[
            pl.BlockSpec(memory_space=pltpu.SMEM),
            pl.BlockSpec((1, block, WIDE), lambda g, p, b: (g, b, p)),
            pl.BlockSpec((1, local, WIDE), lambda g, p, b: (g, 0, PAIRS + p)),
            pl.BlockSpec((1, local, WIDE), lambda g, p, b: (g, 0, 2 * PAIRS + p)),
            pl.BlockSpec((1, rest, WIDE), lambda g, p, b: (g, 0, p)),
            pl.BlockSpec((1, rest, WIDE), lambda g, p, b: (g, 0, PAIRS + p)),
        ],
        out_specs=[
            pl.BlockSpec((1, 2, local, block), lambda g, p, b: (g, p, 0, b)),
            pl.BlockSpec((1, 2, rest, block), lambda g, p, b: (g, p, 0, b)),
            pl.BlockSpec((1, block, WIDE), lambda g, p, b: (g, b, p)),
            pl.BlockSpec((1, WIDE, block), lambda g, p, b: (g, p, b)),
            pl.BlockSpec((1, 1, 2, block), lambda g, p, b: (g, p, 0, b)),
        ],
        out_shape=[
            jax.ShapeDtypeStruct((groups, H, local, local), BF),
            jax.ShapeDtypeStruct((groups, H, rest, local), BF),
            jax.ShapeDtypeStruct((groups, local, width), BF),
            jax.ShapeDtypeStruct((groups, width, local), BF),
            jax.ShapeDtypeStruct((groups, PAIRS, 2, local), F32),
        ],
        scratch_shapes=[
            pltpu.VMEM((local + rest, 2 * WIDE), BF),
            pltpu.VMEM((2, WIDE, local + rest), BF),
        ],
        compiler_params=params(56, 3),
        name="attend",
    )(info, joint_own, joint_own, joint_own, joint_rest, joint_rest)


def middle_kernel(
    tokens,
    cotangent,
    mixed,
    out_w,
    up_w,
    down_w,
    rows,
    up_bias,
    result,
    partial,
    mixed_grad,
    out_wg,
    up_wg,
    down_wg,
    row_sums,
    up_bias_sum,
):
    first = pl.program_id(0) == 0

    @pl.when(first)
    def clear():
        out_wg[...] = jnp.zeros_like(out_wg)
        up_wg[...] = jnp.zeros_like(up_wg)
        down_wg[...] = jnp.zeros_like(down_wg)
        row_sums[...] = jnp.zeros_like(row_sums)
        up_bias_sum[...] = jnp.zeros_like(up_bias_sum)

    out_bias, gain_one, shift_one = rows[0:1], rows[1:2], rows[2:3]
    down_bias, gain_two, shift_two = rows[3:4], rows[4:5], rows[5:6]

    def mean(v):
        return jnp.mean(v, axis=-1, keepdims=True)

    def total(v):
        return jnp.sum(v, axis=0, keepdims=True)

    x = tokens[...]
    heads = mixed[...]
    hidden = x + (dot(heads, out_w[...]) + out_bias)
    centred = hidden - mean(hidden)
    r_one = lax.rsqrt(mean(centred * centred) + EPS)
    n_one = centred * r_one
    normal = n_one * gain_one + shift_one
    normal_low = normal.astype(BF)
    inner = dot(normal_low, up_w[...]) + up_bias[...]
    square = inner * inner
    tanh = jnp.tanh(inner * (GELU_A + (GELU_A * GELU_B) * square))
    half = 0.5 + 0.5 * tanh
    active = (inner * half).astype(BF)
    slope = half + (0.5 * inner) * (1.0 - tanh * tanh) * (
        GELU_A + (3.0 * GELU_A * GELU_B) * square
    )
    branch = dot(active, down_w[...]) + down_bias
    last = normal + branch + x
    centred = last - mean(last)
    r_two = lax.rsqrt(mean(centred * centred) + EPS)
    n_two = centred * r_two
    result[...] = n_two * gain_two + shift_two
    grad = cotangent[...]
    e_two = grad * gain_two
    back = r_two * (e_two - mean(e_two) - n_two * mean(e_two * n_two))
    branch_grad = back.astype(BF)
    down_wg[...] += dot(active, branch_grad, "tn")
    inner_grad_wide = slope * dot(branch_grad, down_w[...], "nt")
    inner_grad = inner_grad_wide.astype(BF)
    up_wg[...] += dot(normal_low, inner_grad, "tn")
    up_bias_sum[...] += total(inner_grad.astype(F32))
    norm_grad = back + dot(inner_grad, up_w[...], "nt")
    e_one = norm_grad * gain_one
    hidden_grad = r_one * (e_one - mean(e_one) - n_one * mean(e_one * n_one))
    attn_grad = hidden_grad.astype(BF)
    partial[...] = back + hidden_grad
    out_wg[...] += dot(heads, attn_grad, "tn")
    mixed_grad[...] = dot(attn_grad, out_w[...], "nt").astype(BF)
    row_sums[0:1] += total(attn_grad.astype(F32))
    row_sums[1:2] += total(norm_grad * n_one)
    row_sums[2:3] += total(norm_grad)
    row_sums[3:4] += total(branch_grad.astype(F32))
    row_sums[4:5] += total(grad * n_two)
    row_sums[5:6] += total(grad)


def middle(tokens, cotangent, mixed, out_w, up_w, down_w, rows, up_bias):
    count, width = tokens.shape
    hidden = up_w.shape[1]
    block = min(256, count)

    def moving(columns=width):
        return pl.BlockSpec((block, columns), lambda b: (b, 0))

    def still(*shape):
        return pl.BlockSpec(shape, lambda b: (0, 0), pipeline_mode=pl.Buffered(1))

    return pl.pallas_call(
        middle_kernel,
        grid=(count // block,),
        in_specs=[
            moving(),
            moving(),
            moving(),
            still(width, width),
            still(width, hidden),
            still(hidden, width),
            still(8, width),
            still(1, hidden),
        ],
        out_specs=[
            moving(),
            moving(),
            moving(),
            still(width, width),
            still(width, hidden),
            still(hidden, width),
            still(8, width),
            still(1, hidden),
        ],
        out_shape=[
            jax.ShapeDtypeStruct((count, width), F32),
            jax.ShapeDtypeStruct((count, width), F32),
            jax.ShapeDtypeStruct((count, width), BF),
            jax.ShapeDtypeStruct((width, width), F32),
            jax.ShapeDtypeStruct((width, hidden), F32),
            jax.ShapeDtypeStruct((hidden, width), F32),
            jax.ShapeDtypeStruct((8, width), F32),
            jax.ShapeDtypeStruct((1, hidden), F32),
        ],
        compiler_params=params(58, 1),
        name="middle",
    )(tokens, cotangent, mixed, out_w, up_w, down_w, rows, up_bias)


def pull_kernel(
    own,
    e_part,
    query,
    keys,
    values,
    mixed_grad,
    mixed_t,
    inverse,
    tokens_low,
    weight,
    *rest,
):
    if own:
        partial, dq_before, share, weight_grad, bias_grad, dkv, d_scores, dq_all = rest
    else:
        share, dq_out, weight_grad, bias_grad, dkv, d_scores = rest
    group, pair = pl.program_id(0), pl.program_id(1)
    span = keys.shape[1]
    local = query.shape[1]
    block = min(256, local)
    width = H * HEAD
    turned = mixed_grad[0].astype(F32).T
    heads = mixed_t[0].astype(F32)
    keys_t = keys[0].T
    query_now = query[0]
    lane = lax.broadcasted_iota(jnp.int32, (local, WIDE), 1)
    zero = jnp.zeros((HEAD, local), BF)
    key_sum = jnp.zeros((span, WIDE), F32)
    value_sum = jnp.zeros((span, WIDE), F32)
    query_parts = []
    for head in range(2):
        side = slice(head * HEAD, (head + 1) * HEAD)
        inv = inverse[0, 0, head : head + 1]
        centre = inv * jnp.sum(turned[side] * heads[side], axis=0, keepdims=True)
        scaled = (turned[side] * inv).astype(BF)
        grad_t = jnp.concatenate([scaled, zero] if head == 0 else [zero, scaled], axis=0)
        grad = grad_t.T
        for at in range(0, local, block):
            columns = slice(at, at + block)
            pulled = dot(values[0], grad_t[:, columns])
            e = e_part[0, head, :, columns].astype(F32)
            d_scores[head, :, columns] = (e * (pulled - centre[:, columns])).astype(BF)
            dq = dot(keys_t, d_scores[head, :, columns])[side]
            if own:
                query_parts.append((head, columns, dq))
            else:
                dq_out[0, side, columns] = dq
        kept = lane < HEAD if head == 0 else lane >= HEAD
        query_head = jnp.where(kept, query_now, jnp.zeros_like(query_now))
        key_sum += dot(d_scores[head], query_head)
        value_sum += dot(e_part[0, head], grad)
    at_keys = pl.ds(pl.multiple_of(pair * WIDE, WIDE), WIDE)
    at_values = pl.ds(pl.multiple_of(width + pair * WIDE, WIDE), WIDE)
    dkv[:, at_keys] = (key_sum * SCALE).astype(BF)
    dkv[:, at_values] = value_sum.astype(BF)
    if own:
        for head, columns, dq in query_parts:
            side = slice(head * HEAD, (head + 1) * HEAD)
            row = pl.ds(pl.multiple_of(pair * WIDE + head * HEAD, HEAD), HEAD)
            dq_all[row, columns] = (dq + dq_before[0, side, columns]) * SCALE

    @pl.when(jnp.logical_and(group == 0, pair == 0))
    def clear():
        weight_grad[...] = jnp.zeros_like(weight_grad)
        bias_grad[...] = jnp.zeros_like(bias_grad)

    @pl.when(pair == PAIRS - 1)
    def finish():
        if own:
            dq = dq_all[...].T.astype(BF)
            weight_grad[:, :width] += dot(tokens_low[0], dq, "tn")
            bias_grad[0:1] += jnp.sum(dq.astype(F32), axis=0, keepdims=True)
            share[0] = (
                partial[0]
                + dot(dq, weight[:, :width], "nt")
                + dot(dkv[...], weight[:, width:], "nt")
            )
            weight_grad[:, width:] += dot(tokens_low[0], dkv[...], "tn")
        else:
            share[0] = dot(dkv[...], weight[:, width:], "nt").astype(BF)
            weight_grad[...] += dot(tokens_low[0], dkv[...], "tn")
        bias_grad[1:2] += jnp.sum(dkv[:, width:].astype(F32), axis=0, keepdims=True)


def pull(e_part, joint_own, joint_part, mixed_grad, mixed_t, inverse, tokens_low, weight, extra):
    own = extra is not None
    groups, _, span, local = e_part.shape
    width = H * HEAD
    first = PAIRS if own else 0
    grid = (groups, PAIRS)
    columns = 3 * width if own else 2 * width

    def still(*shape):
        return pl.BlockSpec(shape, lambda g, p: (0,) * len(shape), pipeline_mode=pl.Buffered(1))

    in_specs = [
        pl.BlockSpec((1, 2, span, local), lambda g, p: (g, p, 0, 0)),
        pl.BlockSpec((1, local, WIDE), lambda g, p: (g, 0, p)),
        pl.BlockSpec((1, span, WIDE), lambda g, p: (g, 0, first + p)),
        pl.BlockSpec((1, span, WIDE), lambda g, p: (g, 0, first + PAIRS + p)),
        pl.BlockSpec((1, local, WIDE), lambda g, p: (g, 0, p)),
        pl.BlockSpec((1, WIDE, local), lambda g, p: (g, p, 0)),
        pl.BlockSpec((1, 1, 2, local), lambda g, p: (g, p, 0, 0)),
        pl.BlockSpec((1, span, width), lambda g, p: (g, 0, 0), pipeline_mode=pl.Buffered(1)),
        still(width, 3 * width),
    ]
    scratch = [
        pltpu.VMEM((span, 2 * width), BF),
        pltpu.VMEM((2, span, local), BF),
    ]
    out_specs = [
        pl.BlockSpec((1, span, width), lambda g, p: (g, 0, 0), pipeline_mode=pl.Buffered(1))
    ]
    out_shape = [jax.ShapeDtypeStruct((groups, span, width), F32 if own else BF)]
    if own:
        in_specs += [
            pl.BlockSpec((1, local, width), lambda g, p: (g, 0, 0), pipeline_mode=pl.Buffered(1)),
            pl.BlockSpec((1, WIDE, local), lambda g, p: (g, p, 0)),
        ]
        scratch += [pltpu.VMEM((width, local), F32)]
    else:
        out_specs += [pl.BlockSpec((1, WIDE, local), lambda g, p: (g, p, 0))]
        out_shape += [jax.ShapeDtypeStruct((groups, width, local), F32)]
    out_specs += [still(width, columns), still(8, width)]
    out_shape += [
        jax.ShapeDtypeStruct((width, columns), F32),
        jax.ShapeDtypeStruct((8, width), F32),
    ]
    return pl.pallas_call(
        functools.partial(pull_kernel, own),
        grid=grid,
        in_specs=in_specs,
        out_specs=out_specs,
        out_shape=out_shape,
        scratch_shapes=scratch,
        compiler_params=params(58, 2),
        name="pull_own" if own else "pull_rest",
    )(
        e_part,
        joint_own,
        joint_part,
        joint_part,
        mixed_grad,
        mixed_t,
        inverse,
        tokens_low,
        weight,
        *(extra or ()),
    )


def per_device(
    tokens,
    lengths,
    joint_weight,
    joint_bias,
    out_weight,
    out_bias,
    gain_first,
    shift_first,
    up_weight,
    up_bias,
    down_weight,
    down_bias,
    gain_second,
    shift_second,
    cotangent,
):
    groups, local, width = tokens.shape
    parts = lax.axis_size("seq")
    devices = lax.axis_size("dp") * parts
    me = lax.axis_index("seq")
    rows = groups * local
    tokens_low = tokens.astype(BF)
    others = [
        lax.ppermute(tokens_low, "seq", [(i, (i - shift) % parts) for i in range(parts)])
        for shift in range(1, parts)
    ]
    tokens_rest = others[0] if parts == 2 else jnp.concatenate(others, axis=1)

    own_rows = joint_weight.shape[0]
    joint_shard = (
        joint_weight.astype(BF)
        .reshape(own_rows, H, 3, HEAD)
        .transpose(0, 2, 1, 3)
        .reshape(own_rows, 3 * width)
    )
    vectors = [
        joint_bias,
        out_bias,
        gain_first,
        shift_first,
        up_bias,
        down_bias,
        gain_second,
        shift_second,
    ]
    lens = [v.shape[0] for v in vectors]
    packed = jnp.concatenate([v.astype(BF) for v in vectors])
    room = -packed.shape[0] % 128
    packed = jnp.pad(packed, (0, room)).reshape(1, -1)
    packed = jnp.broadcast_to(packed, (16, packed.shape[1]))
    joint_w, out_w, up_w, down_w, packed = gather_weights(
        [
            joint_shard,
            out_weight.astype(BF),
            up_weight.astype(BF),
            down_weight.astype(BF),
            packed,
        ],
        (0, 1, 0, 1, 1),
    )
    packed = packed.reshape(devices, 16, -1)[:, 0].astype(F32)
    full, at = [], 0
    for size in lens:
        full.append(packed[:, at : at + size].reshape(devices * size))
        at += size
    pair_full, out_b, gain_1, shift_1, up_b, down_b, gain_2, shift_2 = full
    pair_full = pair_full.reshape(H, 2, HEAD)
    bias_kv = jnp.concatenate([jnp.zeros(width, F32), pair_full[:, 1].reshape(width)])
    bias_all = jnp.concatenate([pair_full[:, 0].reshape(width), bias_kv])
    blank = jnp.zeros(width, F32)
    row_stack = jnp.stack([out_b, gain_1, shift_1, down_b, gain_2, shift_2, blank, blank])

    joint_own = (
        jnp.dot(tokens_low.reshape(rows, width), joint_w, preferred_element_type=F32) + bias_all
    )
    joint_own = joint_own.astype(BF).reshape(groups, local, 3 * width)
    joint_rest = (
        jnp.dot(
            tokens_rest.reshape(-1, width), joint_w[:, width:], preferred_element_type=F32
        )
        + bias_kv
    )
    joint_rest = joint_rest.astype(BF).reshape(groups, (parts - 1) * local, 2 * width)

    places = (me + jnp.arange(parts, dtype=jnp.int32)) % parts * local
    info = jnp.concatenate([lengths, places.astype(jnp.int32)])
    e_own, e_rest, mixed, mixed_t, inverse = attend(info, joint_own, joint_rest, parts)

    result, partial, mixed_grad, out_wg, up_wg, down_wg, row_sums, up_bias_sum = middle(
        tokens.reshape(rows, width),
        cotangent.reshape(rows, width),
        mixed.reshape(rows, width),
        out_w,
        up_w,
        down_w,
        row_stack,
        up_b.reshape(1, -1),
    )
    mixed_grad = mixed_grad.reshape(groups, local, width)
    out_sum, up_sum, down_sum = owner_sums([out_wg, up_wg, down_wg])

    share_rest, dq_rest, joint_wg_rest, bias_rest = pull(
        e_rest, joint_own, joint_rest, mixed_grad, mixed_t, inverse, tokens_rest, joint_w, None
    )
    returned = [
        lax.ppermute(
            share_rest[:, (shift - 1) * local : shift * local],
            "seq",
            [(i, (i + shift) % parts) for i in range(parts)],
        )
        for shift in range(1, parts)
    ]
    input_grad, joint_wg, bias_own = pull(
        e_own,
        joint_own,
        joint_own,
        mixed_grad,
        mixed_t,
        inverse,
        tokens_low,
        joint_w,
        (partial.reshape(groups, local, width), dq_rest),
    )
    for piece in returned:
        input_grad = input_grad + piece.astype(F32)
    joint_wg = jnp.concatenate([joint_wg[:, :width], joint_wg[:, width:] + joint_wg_rest], axis=1)

    pair_grad = jnp.stack(
        [
            bias_own[0].reshape(H, HEAD),
            (bias_own[1] + bias_rest[1]).reshape(H, HEAD),
        ],
        axis=1,
    ).reshape(2 * width)
    sums = [
        pair_grad,
        row_sums[0],
        row_sums[1],
        row_sums[2],
        up_bias_sum[0],
        row_sums[3],
        row_sums[4],
        row_sums[5],
    ]
    vec = jnp.concatenate([s.reshape(devices, -1) for s in sums], axis=1)
    joint_sum, vec = owner_sums([joint_wg, vec])
    joint_sum = joint_sum.reshape(own_rows, 3, H, HEAD).transpose(0, 2, 1, 3)
    joint_sum = joint_sum.reshape(own_rows, 3 * width)
    vec = vec.reshape(-1)
    small, at = [], 0
    for size in lens:
        small.append(vec[at : at + size])
        at += size
    return (
        result.reshape(groups, local, width),
        input_grad,
        joint_sum,
        small[0],
        out_sum,
        small[1],
        small[2],
        small[3],
        up_sum,
        small[4],
        down_sum,
        small[5],
        small[6],
        small[7],
    )


def solution(mesh):
    both = ("dp", "seq")
    matrix, vector, whole = P(both, None), P(both), P("dp", "seq", None)
    return jax.shard_map(
        per_device,
        mesh=mesh,
        in_specs=(
            whole,
            P("dp"),
            matrix,
            vector,
            matrix,
            vector,
            vector,
            vector,
            matrix,
            vector,
            matrix,
            vector,
            vector,
            vector,
            whole,
        ),
        out_specs=(
            whole,
            whole,
            matrix,
            vector,
            matrix,
            vector,
            vector,
            vector,
            matrix,
            vector,
            matrix,
            vector,
            vector,
            vector,
        ),
        check_vma=False,
    )
```

time: 1520 us -> 547 us (0.36)
  matrix products: 429 us -> 14 us
  waiting for transfers between devices: 485 us -> 75.1 us
  Pallas kernels: 0 us -> 355 us
  local copies, waits for them, and re-layouts: 221 us -> 34.6 us
  blocking collectives: 163 us -> 0 us
  other arithmetic: 158 us -> 23.2 us
  loops' own time: 21.8 us -> 0 us
    dot_general x68 -> x2, matrix products: 429 us -> 14 us  [the longest x1 7.39 us: per_device(): jnp.dot(tokens_low.reshape(rows, width), joint_w, preferred_element_type=...]
    pallas_call x0 -> x5, Pallas kernels: none -> 355 us  [the longest x2 127 us: pull(): pl.pallas_call(functools.partial(pull_kernel, own), grid=grid, in_specs=i...]
    reduce_scatter x3 -> x0, waiting for transfers between devices: 286 us -> none  [the longest x1 144 us: per_device(): lax.psum_scatter(down_weight_grad, ('dp', 'seq'), scatter_dimension=0, ti...]
    all_to_all x4 -> x0, waiting for transfers between devices: 172 us -> none  [the longest x1 78.4 us: per_device(): lax.all_to_all(joint_sent, 'seq', split_axis=2, concat_axis=1, tiled=True)]
    convert_element_type x28 -> x14, other arithmetic: 99.1 us -> 4.54 us  [the longest x1 2.61 us: per_device(): tokens_low = tokens.astype(BF)]
    all_gather x1 -> x0, blocking collectives: 81.9 us -> none  [per_device(): lax.all_gather(out_weight.astype(jnp.bfloat16), ('dp', 'seq'), axis=0, ti...]
    unnamed x2 -> x0, blocking collectives: 80.8 us -> none
    ppermute x0 -> x27, waiting for transfers between devices: none -> 75.1 us  [the longest x25 75.1 us: owner_sums(): arrived = [lax.ppermute(s, name, pairs) for s in sent]]
  transfers between devices with their start and end apart: 11 -> 27, of which waited for: 7 -> 18; matrix products, arithmetic and copies ran while one was open for 23% -> 9% of each run, Pallas kernels for 0% -> 38%
where the time goes in v1:
time: 547 us; the launch traced here: 539 us
  Pallas kernels  355 us (65%)
  waiting for transfers between devices  75.1 us (14%)
  starting transfers between devices  35.2 us (6%)
  local copies, waits for them, and re-layouts  34.6 us (6%)
  other arithmetic  23.2 us (4%)
  matrix products  14 us (3%)
    pallas_call x2, Pallas kernels, pull(): pl.pallas_call(functools.partial(pull_kernel, own), grid=grid, in_specs=i...  127 us
    pallas_call x1, Pallas kernels, attend(): pl.pallas_call(functools.partial(attend_kernel, parts, groups), grid=grid...  100 us
    pallas_call x1, Pallas kernels, gather_weights(): pl.pallas_call(functools.partial(gather_kernel, orders, bits_dp, bits_seq...  77.6 us
    ppermute x25, waiting for transfers between devices, owner_sums(): arrived = [lax.ppermute(s, name, pairs) for s in sent]  75.1 us
    pallas_call x1, Pallas kernels, middle(): pl.pallas_call(middle_kernel, grid=(count // block,), in_specs=[moving(),...  50.2 us
    ppermute x25, starting transfers between devices, owner_sums(): arrived = [lax.ppermute(s, name, pairs) for s in sent]  31.6 us
  transfers between devices with their start and end apart: 27, of which 18 were waited for; matrix products, arithmetic and copies ran while one was open for 9% of the time, Pallas kernels for 38%

profile of v1, /device:TPU:0, one launch (start us, length us, event | category | flops | bytes accessed | tf_op | source)
XLA Modules:
  0.0 538.9 jit_solution(10898679362019973957)
XLA Ops:
  0.8 2.6 convert_element_type.339.tokens_low
  3.4 3.0 collective-permute-start
  10.2 77.6 %gather_weights.1 = (bf16[2,2,2,2,2,16,1536]{6,5,4,3,2,1,0:T(8,128)(2,1)}, bf16[2,2,2,2,2,16,512]{6,5,4,3,2,1,0:T(8,128)(2,1)}, bf16[2,2,2,2,2,16,2048]{6,5,4,3,...) custom-call(bf16[16,1536]{1,0:T(8,128)(2,1)} %reshape.237.refs_0_, ...), custom_call_target="tpu_custom_call" | custom-call | tf_op jit(solution)/shard_map/gather_weights/pallas_call | solution.py:100
  89.7 7.4 %fusion = bf16[2048,1536]{0,1:T(8,128)(2,1)} fusion(bf16[512,1536]{1,0:T(8,128)(2,1)} %bitcast.174, bf16[2048,512]{1,0:T(8,128)(2,1)S(1)} %bitcast.171, f32[1536]{0:T(1024)S(1)} %pad_maximum_fusion.2), kind=kOutput, calls=%fused_computation.2 | convolution fusion | flops 3227516928 | bytes 9967616 | tf_op jit(solution)/shard_map/dot_general | solution.py:604
  97.1 8.6 %copy.62 = bf16[2048,1536]{1,0:T(8,128)(2,1)} copy(bf16[2048,1536]{0,1:T(8,128)(2,1)} %fusion) | data formatting | bytes 12582912 | tf_op jit(solution)/shard_map/convert_element_type | solution.py:606
  107.6 6.6 %fusion.1 = bf16[2048,1024]{0,1:T(8,128)(2,1)} fusion(f32[1024]{0:T(1024)S(1)} %concatenate.38, bf16[2048,512]{1,0:T(8,128)(2,1)} %bitcast.9, bf16[512,1536]{1,0:T(8,128)(2,1)} %bitcast.175), kind=kOutput, calls=%fused_computation.3 | convolution fusion | flops 2151677952 | bytes 7344128 | tf_op jit(solution)/shard_map/dot_general | solution.py:608
  114.3 6.4 %copy.63 = bf16[2048,1024]{1,0:T(8,128)(2,1)} copy(bf16[2048,1024]{0,1:T(8,128)(2,1)} %fusion.1) | data formatting | bytes 8388608 | tf_op jit(solution)/shard_map/convert_element_type | solution.py:613
  120.7 100.0 %attend.1 = (bf16[2,8,1024,1024]{3,2,1,0:T(8,128)(2,1)}, bf16[2,8,1024,1024]{3,2,1,0:T(8,128)(2,1)}, bf16[2,1024,512]{2,1,0:T(8,128)(2,1)}, bf16[2,512,1024]{2,1,0:T(8,128)(2,1)}, f32[2,4,2,1024]{3,2,1,0:T(2,128)}) custom-call(s32[4]{0:T(128)} %pad_add_fusion.info, bf16[2,1024,1536]{2,1,0:T(8,128)(2,1)} %bitcast.157, bf16[2,1024,1536]{2,1,0:T(8,128)(2,1)} %bitcast.158, ...), custom_call_target="tpu_custom_call" | custom-call | tf_op jit(solution)/shard_map/attend/pallas_call | solution.py:212
  220.6 50.2 %middle.1 = (f32[2048,512]{1,0:T(8,128)}, f32[2048,512]{1,0:T(8,128)}, bf16[2048,512]{1,0:T(8,128)(2,1)}, f32[512,512]{1,0:T(8,128)}, f32[512,2048]{1,0:T(8,128)...) custom-call(f32[2048,512]{1,0:T(8,128)} %bitcast.168, f32[2048,512]{1,0:T(8,128)} %bitcast.179, ...), custom_call_target="tpu_custom_call" | custom-call | tf_op jit(solution)/shard_map/middle/pallas_call | solution.py:340
  270.9 2.8 fusion.3
  278.1 60.9 %pull_rest.1 = (bf16[2,1024,512]{2,1,0:T(8,128)(2,1)}, f32[2,512,1024]{2,1,0:T(8,128)}, f32[512,1024]{1,0:T(8,128)}, f32[8,512]{1,0:T(8,128)}) custom-call(bf16[2,8,1024,1024]{3,2,1,0:T(8,128)(2,1)} %get-tuple-element.51.e_part, bf16[2,1024,1536]{2,1,0:T(8,128)(2,1)} %bitcast.160, bf16[2,1024,1024]{2,1,0:T(8,128)(2,1)} %bitcast.166, ...), custom_call_target="tpu_custom_call" | custom-call | tf_op jit(solution)/shard_map/pull_rest/pallas_call | solution.py:507
  339.0 66.4 %pull_own.1 = (f32[2,1024,512]{2,1,0:T(8,128)}, f32[512,1536]{1,0:T(8,128)}, f32[8,512]{1,0:T(8,128)}) custom-call(bf16[2,8,1024,1024]{3,2,1,0:T(8,128)(2,1)} %get-tuple-element.46.e_part, bf16[2,1024,1536]{2,1,0:T(8,128)(2,1)} %bitcast.161, bf16[2,1024,1536]{2,1,0:T(8,128)(2,1)} %bitcast.162, bf16[2,1024,1536]{2,1,0:T(8,128)(2,1)} %bitcast.163, ...), custom_call_target="tpu_custom_call" | custom-call | tf_op jit(solution)/shard_map/pull_own/pallas_call | solution.py:507
  416.1 2.8 collective-permute-done.8
  420.5 2.1 collective-permute-done.9
  426.9 2.6 collective-permute-start.11
  432.8 40.9 %collective-permute-done.13 = bf16[2,2,2,16,512]{4,3,0,1,2:T(8,128)(2,1)S(1)} collective-permute-done((bf16[2,2,2,16,512]{4,3,0,1,2:T(8,128)(2,1)S(1)}, bf16[2,2,2,16,512]{4,3,0,1,2:T(8,128)(2,1)S(1)}, u32[]{:S(2)}, u32[]{:S(2)}) %collective-permute-start.13) | collective-permute-done | bytes 131104 | tf_op jit(solution)/shard_map/ppermute | solution.py:140
  475.9 2.2 collective-permute-done.14
  482.1 2.7 collective-permute-start.16
  487.5 5.9 %collective-permute-done.3 = bf16[2,2,2,16,1536]{4,3,0,1,2:T(8,128)(2,1)S(1)} collective-permute-done((bf16[2,2,2,16,1536]{4,3,0,1,2:T(8,128)(2,1)S(1)}, bf16[2,2,2,16,1536]{4,3,0,1,2:T(8,128)(2,1)S(1)}, u32[]{:S(2)}, u32[]{:S(2)}) %collective-permute-start.3) | collective-permute-done | bytes 393248 | tf_op jit(solution)/shard_map/ppermute | solution.py:140
  493.5 2.5 collective-permute-start.4
  506.0 3.5 collective-permute-done.6
  512.0 2.1 collective-permute-start.24
  520.2 2.9 collective-permute-done.19
  534.2 4.4 convert_add_fusion
  (215 shorter events, 70.2 us)
Async XLA Ops:
  3.4 104.2 %collective-permute-start = (bf16[2,1024,512]{2,1,0:T(8,128)(2,1)S(1)}, bf16[2,1024,512]{2,1,0:T(8,128)(2,1)}, u32[]{:S(2)}, u32[]{:S(2)}) collective-permute-start(bf16[2,1024,512]{2,1,0:T(8,128)(2,1)S(1)} %convert_element_type.339.tokens_low), channel_id=1, source_target_pairs={{0,1},{1,0},{2,3},{3,2},{4,5},{5,4},{6,7},{7,6},{8,9},{9,8},{10,11... | collective-permute-start | bytes 6291464 | tf_op jit(solution)/shard_map/ppermute | solution.py:554
  273.6 222.4 %collective-permute-start.22 = (bf16[2,2,2,2,64,512]{5,4,0,1,2,3:T(8,128)(2,1)}, bf16[2,2,2,2,64,512]{5,4,0,1,2,3:T(8,128)(2,1)}, u32[]{:S(2)}, u32[]{:S(2)}) collective-permute-start(bf16[2,2,2,2,64,512]{5,4,0,1,2,3:T(8,128)(2,1)} %fusion.3), channel_id=1, source_target_pairs={{0,2},{2,0},{4,6},{6,4},{8,10},{10,8},{12,14},{14,12},{16,18},{18,... | collective-permute-start | bytes 3145736 | tf_op jit(solution)/shard_map/ppermute | solution.py:140
  275.7 225.7 %collective-permute-start.17 = (bf16[2,2,2,2,16,2048]{5,4,0,1,2,3:T(8,128)(2,1)S(1)}, bf16[2,2,2,2,16,2048]{5,4,0,1,2,3:T(8,128)(2,1)}, u32[]{:S(2)}, u32[]{:S(2)}) collective-permute-start(bf16[2,2,2,2,16,2048]{5,4,0,1,2,3:T(8,128)(2,1)S(1)} %fusion.2), channel_id=1, source_target_pairs={{0,2},{2,0},{4,6},{6,4},{8,10},{10,8},{12,14},{14,12},{16,18},{18,... | collective-permute-start | bytes 3145736 | tf_op jit(solution)/shard_map/ppermute | solution.py:140
  277.7 149.1 %collective-permute-start.12 = (bf16[2,2,2,2,16,512]{5,4,0,1,2,3:T(8,128)(2,1)}, bf16[2,2,2,2,16,512]{5,4,0,1,2,3:T(8,128)(2,1)S(1)}, u32[]{:S(2)}, u32[]{:S(2)}) collective-permute-start(bf16[2,2,2,2,16,512]{5,4,0,1,2,3:T(8,128)(2,1)} %fusion.11), channel_id=1, source_target_pairs={{0,2},{2,0},{4,6},{6,4},{8,10},{10,8},{12,14},{14,12},{16,18},{18,... | collective-permute-start | bytes 786440 | tf_op jit(solution)/shard_map/ppermute | solution.py:140
  411.4 3.8 collective-permute-start.7
  416.0 68.8 %collective-permute-start.2 = (bf16[2,2,2,2,16,1536]{5,4,0,1,2,3:T(8,128)(2,1)S(1)}, bf16[2,2,2,2,16,1536]{5,4,0,1,2,3:T(8,128)(2,1)S(1)}, u32[]{:S(2)}, u32[]{:S(2)}) collective-permute-start(bf16[2,2,2,2,16,1536]{5,4,0,1,2,3:T(8,128)(2,1)S(1)} %fusion.5), channel_id=1, source_target_pairs={{0,2},{2,0},{4,6},{6,4},{8,10},{10,8},{12,14},{14,12},{16,18},{18,... | collective-permute-start | bytes 2359304 | tf_op jit(solution)/shard_map/ppermute | solution.py:140
  426.2 108.0 %collective-permute-start.1 = (bf16[2,1024,512]{2,1,0:T(8,128)(2,1)}, bf16[2,1024,512]{2,1,0:T(8,128)(2,1)}, u32[]{:S(2)}, u32[]{:S(2)}) collective-permute-start(bf16[2,1024,512]{2,1,0:T(8,128)(2,1)} %get-tuple-element.54), channel_id=1, source_target_pairs={{0,1},{1,0},{2,3},{3,2},{4,5},{5,4},{6,7},{7,6},{8,9},{9,8},{10,11... | collective-permute-start | bytes 6291464 | tf_op jit(solution)/shard_map/ppermute | solution.py:636
  426.9 4.5 collective-permute-start.11
  431.4 42.3 %collective-permute-start.13 = (bf16[2,2,2,16,512]{4,3,0,1,2:T(8,128)(2,1)S(1)}, bf16[2,2,2,16,512]{4,3,0,1,2:T(8,128)(2,1)S(1)}, u32[]{:S(2)}, u32[]{:S(2)}) collective-permute-start(bf16[2,2,2,16,512]{4,3,0,1,2:T(8,128)(2,1)S(1)} %fusion.13), channel_id=1, source_target_pairs={{0,1},{1,0},{2,3},{3,2},{4,5},{5,4},{6,7},{7,6},{8,9},{9,8},{10,11... | collective-permute-start | bytes 393224 | tf_op jit(solution)/shard_map/ppermute | solution.py:140
  473.8 4.3 collective-permute-start.14
  478.1 4.0 collective-permute-start.15
  482.1 4.7 collective-permute-start.16
  485.1 8.3 %collective-permute-start.3 = (bf16[2,2,2,16,1536]{4,3,0,1,2:T(8,128)(2,1)S(1)}, bf16[2,2,2,16,1536]{4,3,0,1,2:T(8,128)(2,1)S(1)}, u32[]{:S(2)}, u32[]{:S(2)}) collective-permute-start(bf16[2,2,2,16,1536]{4,3,0,1,2:T(8,128)(2,1)S(1)} %fusion.8), channel_id=1, source_target_pairs={{0,1},{1,0},{2,3},{3,2},{4,5},{5,4},{6,7},{7,6},{8,9},{9,8},{10,11... | collective-permute-start | bytes 1179656 | tf_op jit(solution)/shard_map/ppermute | solution.py:140
  493.5 6.2 %collective-permute-start.4 = (bf16[2,2,16,1536]{3,2,0,1:T(8,128)(2,1)S(1)}, bf16[2,2,16,1536]{3,2,0,1:T(8,128)(2,1)S(1)}, u32[]{:S(2)}, u32[]{:S(2)}) collective-permute-start(bf16[2,2,16,1536]{3,2,0,1:T(8,128)(2,1)S(1)} %fusion.12), channel_id=1, source_target_pairs={{0,4},{2,6},{4,0},{6,2},{8,12},{10,14},{12,8},{14,10},{16,20},{18,... | collective-permute-start | bytes 589832 | tf_op jit(solution)/shard_map/ppermute | solution.py:140
  498.6 11.9 %collective-permute-start.23 = (bf16[2,2,2,64,512]{4,3,0,1,2:T(8,128)(2,1)}, bf16[2,2,2,64,512]{4,3,0,1,2:T(8,128)(2,1)}, u32[]{:S(2)}, u32[]{:S(2)}) collective-permute-start(bf16[2,2,2,64,512]{4,3,0,1,2:T(8,128)(2,1)} %fusion.7), channel_id=1, source_target_pairs={{0,1},{1,0},{2,3},{3,2},{4,5},{5,4},{6,7},{7,6},{8,9},{9,8},{10,11... | collective-permute-start | bytes 1572872 | tf_op jit(solution)/shard_map/ppermute | solution.py:140
  499.8 4.7 collective-permute-start.5
  504.5 5.1 collective-permute-start.6
  505.0 10.5 %collective-permute-start.18 = (bf16[2,2,2,16,2048]{4,3,0,1,2:T(8,128)(2,1)S(1)}, bf16[2,2,2,16,2048]{4,3,0,1,2:T(8,128)(2,1)}, u32[]{:S(2)}, u32[]{:S(2)}) collective-permute-start(bf16[2,2,2,16,2048]{4,3,0,1,2:T(8,128)(2,1)S(1)} %fusion.6), channel_id=1, source_target_pairs={{0,1},{1,0},{2,3},{3,2},{4,5},{5,4},{6,7},{7,6},{8,9},{9,8},{10,11... | collective-permute-start | bytes 1572872 | tf_op jit(solution)/shard_map/ppermute | solution.py:140
  512.0 6.4 %collective-permute-start.24 = (bf16[2,2,64,512]{3,2,0,1:T(8,128)(2,1)S(1)}, bf16[2,2,64,512]{3,2,0,1:T(8,128)(2,1)S(1)}, u32[]{:S(2)}, u32[]{:S(2)}) collective-permute-start(bf16[2,2,64,512]{3,2,0,1:T(8,128)(2,1)S(1)} %fusion.10), channel_id=1, source_target_pairs={{0,4},{2,6},{4,0},{6,2},{8,12},{10,14},{12,8},{14,10},{16,20},{18,... | collective-permute-start | bytes 786440 | tf_op jit(solution)/shard_map/ppermute | solution.py:140
  516.7 6.4 %collective-permute-start.19 = (bf16[2,2,16,2048]{3,2,0,1:T(8,128)(2,1)S(1)}, bf16[2,2,16,2048]{3,2,0,1:T(8,128)(2,1)S(1)}, u32[]{:S(2)}, u32[]{:S(2)}) collective-permute-start(bf16[2,2,16,2048]{3,2,0,1:T(8,128)(2,1)S(1)} %fusion.9), channel_id=1, source_target_pairs={{0,4},{2,6},{4,0},{6,2},{8,12},{10,14},{12,8},{14,10},{16,20},{18,... | collective-permute-start | bytes 786440 | tf_op jit(solution)/shard_map/ppermute | solution.py:140
  518.6 6.3 %collective-permute-start.25 = (bf16[2,64,512]{2,1,0:T(8,128)(2,1)S(1)}, bf16[2,64,512]{2,1,0:T(8,128)(2,1)S(1)}, u32[]{:S(2)}, u32[]{:S(2)}) collective-permute-start(bf16[2,64,512]{2,1,0:T(8,128)(2,1)S(1)} %fusion.15), channel_id=1, source_target_pairs={{0,8},{2,10},{4,12},{6,14},{8,0},{10,2},{12,4},{14,6},{16,24},{18,... | collective-permute-start | bytes 393224 | tf_op jit(solution)/shard_map/ppermute | solution.py:140
  523.2 5.0 collective-permute-start.20
  524.9 5.9 %collective-permute-start.26 = (bf16[64,512]{1,0:T(8,128)(2,1)S(1)}, bf16[64,512]{1,0:T(8,128)(2,1)S(1)}, u32[]{:S(2)}, u32[]{:S(2)}) collective-permute-start(bf16[64,512]{1,0:T(8,128)(2,1)S(1)} %fusion.19), channel_id=1, source_target_pairs={{0,16},{2,18},{4,20},{6,22},{8,24},{10,26},{12,28},{14,30},{16,0},... | collective-permute-start | bytes 196616 | tf_op jit(solution)/shard_map/ppermute | solution.py:140
  528.3 5.2 collective-permute-start.21
  (26 other events, 410.2 us)

commit v2 on v1

v2 whole, which is shorter than its diff:
```python
import functools
import math

import jax
import jax.numpy as jnp
from jax import lax
from jax.experimental import pallas as pl
from jax.experimental.pallas import tpu as pltpu
from jax.sharding import PartitionSpec as P

H = 8
HEAD = 64
PAIRS = H // 2
WIDE = 2 * HEAD
BF = jnp.bfloat16
F32 = jnp.float32
EPS = 1e-05
SCALE = 1.0 / math.sqrt(HEAD)
LOG2E = math.log2(math.e)
GELU_A = math.sqrt(2.0 / math.pi)
GELU_B = 0.044715
MESH = pl.DeviceIdType.MESH
MIB = 2**20
FORMS = {
    "nn": (((1,), (0,)), ((), ())),
    "nt": (((1,), (1,)), ((), ())),
    "tn": (((0,), (0,)), ((), ())),
}


def dot(left, right, form="nn"):
    return lax.dot_general(left, right, FORMS[form], preferred_element_type=F32)


def params(limit, steps):
    return pltpu.CompilerParams(
        vmem_limit_bytes=limit * MIB, dimension_semantics=("arbitrary",) * steps
    )


def log2(size):
    return size.bit_length() - 1


def place_bits(bits_dp, bits_seq):
    dp, seq = lax.axis_index("dp"), lax.axis_index("seq")
    mine = [lax.rem(dp // 2 ** (bits_dp - 1 - b), 2) for b in range(bits_dp)]
    mine += [lax.rem(seq // 2 ** (bits_seq - 1 - b), 2) for b in range(bits_seq)]

    def partner(bit):
        if bit < bits_dp:
            return (dp + (1 - 2 * mine[bit]) * 2 ** (bits_dp - 1 - bit), seq)
        return (dp, seq + (1 - 2 * mine[bit]) * 2 ** (bits_dp + bits_seq - 1 - bit))

    return mine, partner


def greet(partner, bits):
    barrier = pltpu.get_barrier_semaphore()
    for bit in range(bits):
        pl.semaphore_signal(barrier, inc=1, device_id=partner(bit), device_id_type=MESH)


def own_copies(shards, fulls, mine, sem):
    return [
        pltpu.make_async_copy(shard, full.at[tuple(mine)], sem.at[i])
        for i, (shard, full) in enumerate(zip(shards, fulls))
    ]


def stage_copies(stage, orders, fulls, mine, partner, send_sem, recv_sem):
    copies = []
    for i, full in enumerate(fulls):
        done = orders[i][:stage]
        place = tuple(slice(None) if b in done else mine[b] for b in range(len(mine)))
        copies.append(
            pltpu.make_async_remote_copy(
                src_ref=full.at[place],
                dst_ref=full.at[place],
                send_sem=send_sem.at[stage, i],
                recv_sem=recv_sem.at[stage, i],
                device_id=partner(orders[i][stage]),
                device_id_type=MESH,
            )
        )
    return copies


def gather_plan(first):
    bits_dp, bits_seq = log2(lax.axis_size("dp")), log2(lax.axis_size("seq"))
    bits = bits_dp + bits_seq
    upper = list(range(bits_dp - 1))
    beside = list(range(bits_dp, bits))
    plans = (upper + beside + [bits_dp - 1], upper[:-1] + beside + upper[-1:] + [bits_dp - 1])
    return bits_dp, bits_seq, tuple(tuple(plans[p]) for p in first)


def gather_kernel(orders, bits_dp, bits_seq, *refs):
    count = len(orders)
    shards, fulls = refs[:count], refs[count : 2 * count]
    own_sem, send_sem, recv_sem = refs[2 * count :]
    bits = bits_dp + bits_seq
    mine, partner = place_bits(bits_dp, bits_seq)
    greet(partner, bits)
    local = own_copies(shards, fulls, mine, own_sem)
    for copy in local:
        copy.start()
    for copy in local:
        copy.wait()
    pl.semaphore_wait(pltpu.get_barrier_semaphore(), bits)
    for stage in range(bits):
        copies = stage_copies(stage, orders, fulls, mine, partner, send_sem, recv_sem)
        for copy in copies:
            copy.start()
        for copy in copies:
            copy.wait()


def spread(full):
    return full.reshape((-1,) + full.shape[-1:])


def gather_weights(shards, first):
    bits_dp, bits_seq, orders = gather_plan(first)
    bits = bits_dp + bits_seq
    count = len(shards)
    fulls = pl.pallas_call(
        functools.partial(gather_kernel, orders, bits_dp, bits_seq),
        out_shape=[jax.ShapeDtypeStruct((2,) * bits + s.shape, s.dtype) for s in shards],
        in_specs=[pl.BlockSpec(memory_space=pl.ANY)] * count,
        out_specs=[pl.BlockSpec(memory_space=pl.ANY)] * count,
        scratch_shapes=[
            pltpu.SemaphoreType.DMA((count,)),
            pltpu.SemaphoreType.DMA((bits, count)),
            pltpu.SemaphoreType.DMA((bits, count)),
        ],
        compiler_params=pltpu.CompilerParams(collective_id=0, has_side_effects=True),
        name="gather_weights",
    )(*shards)
    return [spread(f) for f in fulls]


def owner_sums(arrays):
    size_dp, size_seq = lax.axis_size("dp"), lax.axis_size("seq")
    bits_dp, bits_seq = log2(size_dp), log2(size_seq)
    bits = bits_dp + bits_seq
    dp, seq = lax.axis_index("dp"), lax.axis_index("seq")
    rows = [a.shape[0] // (size_dp * size_seq) for a in arrays]
    arrays = [
        a.reshape((2,) * bits + (r,) + a.shape[1:]) for a, r in zip(arrays, rows)
    ]
    left = list(range(bits))
    order = [bits_dp - 1] + list(range(bits_dp, bits)) + list(range(bits_dp - 2, -1, -1))
    for bit in order:
        axis = left.index(bit)
        left.remove(bit)
        if bit < bits_dp:
            name, size, step, me = "dp", size_dp, 2 ** (bits_dp - 1 - bit), dp
        else:
            name, size, step, me = "seq", size_seq, 2 ** (bits - 1 - bit), seq
        mine = me // step % 2
        pairs = [(i, i ^ step) for i in range(size)]
        sent = [
            lax.dynamic_index_in_dim(a, 1 - mine, axis, keepdims=False).astype(BF) for a in arrays
        ]
        kept = [lax.dynamic_index_in_dim(a, mine, axis, keepdims=False) for a in arrays]
        arrived = [lax.ppermute(s, name, pairs) for s in sent]
        arrays = [k + a.astype(F32) for k, a in zip(kept, arrived)]
    return arrays


def project_kernel(own, tokens, weight, bias, *outs):
    x = tokens[...]
    if own:
        query, pair = outs
    else:
        (pair,) = outs
    for p in range(PAIRS):
        start = 3 * WIDE * p + (0 if own else WIDE)
        end = 3 * WIDE * (p + 1)
        joint = (dot(x, weight[:, start:end]) + bias[:, start:end]).astype(BF)
        if own:
            query[:, p * WIDE : (p + 1) * WIDE] = joint[:, :WIDE]
            joint = joint[:, WIDE:]
        pair[:, 2 * p * WIDE : 2 * (p + 1) * WIDE] = joint


def project(tokens, weight, bias, own):
    count, width = tokens.shape
    block = min(512, count)

    def moving(columns):
        return pl.BlockSpec((block, columns), lambda b: (b, 0))

    def still(*shape):
        return pl.BlockSpec(shape, lambda b: (0, 0), pipeline_mode=pl.Buffered(1))

    wide = [width, 2 * width] if own else [2 * width]
    return pl.pallas_call(
        functools.partial(project_kernel, own),
        grid=(count // block,),
        in_specs=[moving(width), still(width, 3 * width), still(1, 3 * width)],
        out_specs=[moving(w) for w in wide],
        out_shape=[jax.ShapeDtypeStruct((count, w), BF) for w in wide],
        compiler_params=params(40, 1),
        name="project_own" if own else "project_rest",
    )(tokens, weight, bias)


def attend_kernel(parts, groups, steps, blocks, orders, bits_dp, bits_seq, *refs):
    count = len(orders)
    info, query, keys_own, keys_rest, values_own, values_rest = refs[:6]
    shards = refs[6 : 6 + count]
    e_out, mixed, mixed_t, inverse = refs[6 + count : 10 + count]
    fulls = refs[10 + count : 10 + 2 * count]
    k_ext, v_ext, kept, tops, own_sem, send_sem, recv_sem = refs[10 + 2 * count :]
    local = keys_own.shape[1]
    block = query.shape[1]
    step = pl.program_id(0)
    chunk = min(256, local)

    bits = bits_dp + bits_seq
    mine, partner = place_bits(bits_dp, bits_seq)
    stages = [
        stage_copies(stage, orders, fulls, mine, partner, send_sem, recv_sem)
        for stage in range(bits)
    ]

    @pl.when(step == 0)
    def enter():
        greet(partner, bits)
        local_copies = own_copies(shards, fulls, mine, own_sem)
        for copy in local_copies:
            copy.start()
        for copy in local_copies:
            copy.wait()
        pl.semaphore_wait(pltpu.get_barrier_semaphore(), bits)
        for copy in stages[0]:
            copy.start()

    for stage in range(1, bits + 1):
        due = max(stage * steps // (bits + 1), 1) if bits <= steps else min(stage, steps)

        @pl.when(step == due)
        def advance():
            for copy in stages[stage - 1]:
                copy.wait()
            if stage < bits:
                for copy in stages[stage]:
                    copy.start()

    @pl.when(jnp.logical_and(step % blocks == 0, step < steps))
    def prepare_keys():
        for group in range(groups):
            @pl.when(step // (blocks * PAIRS) == group)
            def fill():
                length = info[group]
                for part in range(parts):
                    rows = slice(part * local, (part + 1) * local)
                    k_ext[rows, :WIDE] = keys_own[0] if part == 0 else keys_rest[part - 1, 0]
                    place = lax.broadcasted_iota(jnp.int32, (local, WIDE), 0) + info[groups + part]
                    k_ext[rows, WIDE:] = jnp.where(place < length, 0.0, -1e30).astype(BF)

    @pl.when(step % blocks == 1 % blocks)
    def prepare_values():
        for part in range(parts):
            rows = slice(part * local, (part + 1) * local)
            values = values_own[0] if part == 0 else values_rest[part - 1, 0]
            turned = values.T
            v_ext[0, :HEAD, rows] = turned[:HEAD]
            v_ext[1, :HEAD, rows] = turned[HEAD:]
            v_ext[:, HEAD:, rows] = jnp.ones((2, HEAD, local), BF)

    turned = query[0].T
    zero = jnp.zeros((HEAD, block), BF)
    one = (lax.broadcasted_iota(jnp.int32, (WIDE, block), 0) == 0).astype(F32).astype(BF)
    heads = []
    for head in range(2):
        if head == 0:
            picked = jnp.concatenate([turned[:HEAD], zero, one], axis=0)
        else:
            picked = jnp.concatenate([zero, turned[HEAD:], one], axis=0)
        top = tops[head : head + 1]
        out = None
        largest = None
        for at in range(0, parts * local, chunk):
            rows = slice(at, at + chunk)
            inside = slice(at % local, at % local + chunk)
            e = jnp.exp2((kept[head, rows] - top) * (SCALE * LOG2E)).astype(BF)
            e_out[at // local, 0, head, inside] = e
            add = dot(v_ext[head, :, rows], e)
            out = add if out is None else out + add
            scores = dot(k_ext[rows], picked)
            kept[head, rows] = scores
            most = jnp.max(scores.reshape(chunk // 8, 8, block), axis=0)
            largest = most if largest is None else jnp.maximum(largest, most)
        tops[head : head + 1] = jnp.max(largest, axis=0, keepdims=True)
        inv = 1.0 / out[HEAD : HEAD + 1]
        inverse[0, 0, head : head + 1] = inv
        heads.append(out[:HEAD] * inv)
    both = jnp.concatenate(heads, axis=0).astype(BF)
    mixed_t[0] = both
    mixed[0] = both.T


def attend(info, query, pair_own, pair_rest, shards, first):
    groups, local, width = query.shape
    others = pair_rest.shape[0]
    parts = others + 1
    block = min(512, local)
    blocks = local // block
    steps = groups * PAIRS * blocks
    bits_dp, bits_seq, orders = gather_plan(first)
    bits = bits_dp + bits_seq
    count = len(shards)

    def decode(t, place):
        return place(t // (PAIRS * blocks), t // blocks % PAIRS, t % blocks)

    def now(place):
        return lambda t: decode(jnp.minimum(t, steps - 1), place)

    def before(place):
        return lambda t: decode(jnp.maximum(t - 1, 0), place)

    outs = pl.pallas_call(
        functools.partial(
            attend_kernel, parts, groups, steps, blocks, orders, bits_dp, bits_seq
        ),
        grid=(steps + 1,),
        in_specs=[
            pl.BlockSpec(memory_space=pltpu.SMEM),
            pl.BlockSpec((1, block, WIDE), now(lambda g, p, b: (g, b, p))),
            pl.BlockSpec((1, local, WIDE), now(lambda g, p, b: (g, 0, 2 * p))),
            pl.BlockSpec((others, 1, local, WIDE), now(lambda g, p, b: (0, g, 0, 2 * p))),
            pl.BlockSpec((1, local, WIDE), before(lambda g, p, b: (g, 0, 2 * p + 1))),
            pl.BlockSpec((others, 1, local, WIDE), before(lambda g, p, b: (0, g, 0, 2 * p + 1))),
        ]
        + [pl.BlockSpec(memory_space=pl.ANY)] * count,
        out_specs=[
            pl.BlockSpec((parts, 1, 2, local, block), before(lambda g, p, b: (0, g, p, 0, b))),
            pl.BlockSpec((1, block, WIDE), before(lambda g, p, b: (g, b, p))),
            pl.BlockSpec((1, WIDE, block), before(lambda g, p, b: (g, p, b))),
            pl.BlockSpec((1, 1, 2, block), before(lambda g, p, b: (g, p, 0, b))),
        ]
        + [pl.BlockSpec(memory_space=pl.ANY)] * count,
        out_shape=[
            jax.ShapeDtypeStruct((parts, groups, H, local, local), BF),
            jax.ShapeDtypeStruct((groups, local, width), BF),
            jax.ShapeDtypeStruct((groups, width, local), BF),
            jax.ShapeDtypeStruct((groups, PAIRS, 2, local), F32),
        ]
        + [jax.ShapeDtypeStruct((2,) * bits + s.shape, s.dtype) for s in shards],
        scratch_shapes=[
            pltpu.VMEM((parts * local, 2 * WIDE), BF),
            pltpu.VMEM((2, WIDE, parts * local), BF),
            pltpu.VMEM((2, parts * local, block), F32),
            pltpu.VMEM((8, block), F32),
            pltpu.SemaphoreType.DMA((count,)),
            pltpu.SemaphoreType.DMA((bits, count)),
            pltpu.SemaphoreType.DMA((bits, count)),
        ],
        compiler_params=pltpu.CompilerParams(
            vmem_limit_bytes=56 * MIB,
            dimension_semantics=("arbitrary",),
            collective_id=1,
            has_side_effects=True,
        ),
        name="attend",
    )(info, query, pair_own, pair_rest, pair_own, pair_rest, *shards)
    return outs[:4], [spread(f) for f in outs[4:]]


def middle_kernel(
    tokens,
    cotangent,
    mixed,
    out_w,
    up_w,
    down_w,
    rows,
    up_bias,
    result,
    partial,
    mixed_grad,
    out_wg,
    up_wg,
    down_wg,
    row_sums,
    up_bias_sum,
):
    first = pl.program_id(0) == 0

    @pl.when(first)
    def clear():
        out_wg[...] = jnp.zeros_like(out_wg)
        up_wg[...] = jnp.zeros_like(up_wg)
        down_wg[...] = jnp.zeros_like(down_wg)
        row_sums[...] = jnp.zeros_like(row_sums)
        up_bias_sum[...] = jnp.zeros_like(up_bias_sum)

    out_bias, gain_one, shift_one = rows[0:1], rows[1:2], rows[2:3]
    down_bias, gain_two, shift_two = rows[3:4], rows[4:5], rows[5:6]

    def mean(v):
        return jnp.mean(v, axis=-1, keepdims=True)

    def total(v):
        return jnp.sum(v, axis=0, keepdims=True)

    x = tokens[...]
    heads = mixed[...]
    hidden = x + (dot(heads, out_w[...]) + out_bias)
    centred = hidden - mean(hidden)
    r_one = lax.rsqrt(mean(centred * centred) + EPS)
    n_one = centred * r_one
    normal = n_one * gain_one + shift_one
    normal_low = normal.astype(BF)
    inner = dot(normal_low, up_w[...]) + up_bias[...]
    square = inner * inner
    tanh = jnp.tanh(inner * (GELU_A + (GELU_A * GELU_B) * square))
    half = 0.5 + 0.5 * tanh
    active = (inner * half).astype(BF)
    slope = half + (0.5 * inner) * (1.0 - tanh * tanh) * (
        GELU_A + (3.0 * GELU_A * GELU_B) * square
    )
    branch = dot(active, down_w[...]) + down_bias
    last = normal + branch + x
    centred = last - mean(last)
    r_two = lax.rsqrt(mean(centred * centred) + EPS)
    n_two = centred * r_two
    result[...] = n_two * gain_two + shift_two
    grad = cotangent[...]
    e_two = grad * gain_two
    back = r_two * (e_two - mean(e_two) - n_two * mean(e_two * n_two))
    branch_grad = back.astype(BF)
    down_wg[...] += dot(active, branch_grad, "tn")
    inner_grad_wide = slope * dot(branch_grad, down_w[...], "nt")
    inner_grad = inner_grad_wide.astype(BF)
    up_wg[...] += dot(normal_low, inner_grad, "tn")
    up_bias_sum[...] += total(inner_grad.astype(F32))
    norm_grad = back + dot(inner_grad, up_w[...], "nt")
    e_one = norm_grad * gain_one
    hidden_grad = r_one * (e_one - mean(e_one) - n_one * mean(e_one * n_one))
    attn_grad = hidden_grad.astype(BF)
    partial[...] = back + hidden_grad
    out_wg[...] += dot(heads, attn_grad, "tn")
    mixed_grad[...] = dot(attn_grad, out_w[...], "nt").astype(BF)
    row_sums[0:1] += total(attn_grad.astype(F32))
    row_sums[1:2] += total(norm_grad * n_one)
    row_sums[2:3] += total(norm_grad)
    row_sums[3:4] += total(branch_grad.astype(F32))
    row_sums[4:5] += total(grad * n_two)
    row_sums[5:6] += total(grad)


def middle(tokens, cotangent, mixed, out_w, up_w, down_w, rows, up_bias):
    count, width = tokens.shape
    hidden = up_w.shape[1]
    block = min(256, count)

    def moving(columns=width):
        return pl.BlockSpec((block, columns), lambda b: (b, 0))

    def still(*shape):
        return pl.BlockSpec(shape, lambda b: (0, 0), pipeline_mode=pl.Buffered(1))

    return pl.pallas_call(
        middle_kernel,
        grid=(count // block,),
        in_specs=[
            moving(),
            moving(),
            moving(),
            still(width, width),
            still(width, hidden),
            still(hidden, width),
            still(8, width),
            still(1, hidden),
        ],
        out_specs=[
            moving(),
            moving(),
            moving(),
            still(width, width),
            still(width, hidden),
            still(hidden, width),
            still(8, width),
            still(1, hidden),
        ],
        out_shape=[
            jax.ShapeDtypeStruct((count, width), F32),
            jax.ShapeDtypeStruct((count, width), F32),
            jax.ShapeDtypeStruct((count, width), BF),
            jax.ShapeDtypeStruct((width, width), F32),
            jax.ShapeDtypeStruct((width, hidden), F32),
            jax.ShapeDtypeStruct((hidden, width), F32),
            jax.ShapeDtypeStruct((8, width), F32),
            jax.ShapeDtypeStruct((1, hidden), F32),
        ],
        compiler_params=params(58, 1),
        name="middle",
    )(tokens, cotangent, mixed, out_w, up_w, down_w, rows, up_bias)


def pull_kernel(
    parts,
    groups,
    e_part,
    query,
    pair_own,
    pair_rest,
    mixed_grad,
    mixed_t,
    inverse,
    tokens_own,
    tokens_rest,
    weight,
    partial,
    share_rest,
    share_own,
    weight_grad,
    bias_grad,
    d_scores,
    joint_grad,
    total,
    dq_sums,
    dq_turned,
):
    step = pl.program_id(0)
    part = lax.rem(step // (groups * PAIRS) + 1, parts)
    group, pair = lax.rem(step // PAIRS, groups), lax.rem(step, PAIRS)
    own = part == 0
    local = query.shape[1]
    chunk = min(256, local)
    turned = mixed_grad[0].astype(F32).T
    mixed = mixed_t[0].astype(F32)
    values = jnp.where(own, pair_own[0, :, WIDE:], pair_rest[0, 0, :, WIDE:])
    keys_t = jnp.where(own, pair_own[0, :, :WIDE], pair_rest[0, 0, :, :WIDE]).T
    query_now = query[0]
    lane = lax.broadcasted_iota(jnp.int32, (local, WIDE), 1)
    zero = jnp.zeros((HEAD, local), BF)
    grad_t, grad, centre, picked = [], [], [], []
    for head in range(2):
        side = slice(head * HEAD, (head + 1) * HEAD)
        inv = inverse[0, 0, head : head + 1]
        centre.append(inv * jnp.sum(turned[side] * mixed[side], axis=0, keepdims=True))
        scaled = (turned[side] * inv).astype(BF)
        grad_t.append(jnp.concatenate([scaled, zero] if head == 0 else [zero, scaled], axis=0))
        grad.append(grad_t[head].T)
        kept = lane < HEAD if head == 0 else lane >= HEAD
        picked.append(jnp.where(kept, query_now, jnp.zeros_like(query_now)))

    def key_grad(rows):
        sums = dot(d_scores[0, rows], picked[0]) + dot(d_scores[1, rows], picked[1])
        joint_grad[rows, WIDE : 2 * WIDE] = (sums * SCALE).astype(BF)

    last = None
    for at in range(0, local, chunk):
        rows = slice(at, at + chunk)
        for head in range(2):
            pulled = dot(values[rows], grad_t[head])
            e = e_part[0, 0, head, rows].astype(F32)
            d_scores[head, rows] = (e * (pulled - centre[head])).astype(BF)
        sums = dot(e_part[0, 0, 0, rows], grad[0]) + dot(e_part[0, 0, 1, rows], grad[1])
        joint_grad[rows, 2 * WIDE :] = sums.astype(BF)
        if last is not None:
            key_grad(last)
        last = rows
    key_grad(last)
    first_part = part == 1 % parts
    for head in range(2):
        side = slice(head * HEAD, (head + 1) * HEAD)
        dq = dot(keys_t, d_scores[head])[side]
        dq_turned[side] = dq

    @pl.when(step == 0)
    def clear():
        weight_grad[...] = jnp.zeros_like(weight_grad)
        bias_grad[...] = jnp.zeros_like(bias_grad)
        dq_sums[...] = jnp.zeros_like(dq_sums)

    @pl.when(pair == 0)
    def start():
        total[...] = jnp.zeros_like(total)

    side = pl.ds(pl.multiple_of(pair * WIDE, WIDE), WIDE)
    start_at = pair * (3 * WIDE)
    wide = pl.ds(pl.multiple_of(start_at, WIDE), 3 * WIDE)
    last_two = pl.ds(pl.multiple_of(start_at + WIDE, WIDE), 2 * WIDE)
    column = group * PAIRS + pair

    @pl.when(own)
    def near():
        dq = (dq_sums[column] + dq_turned[...]) * SCALE
        dq = dq.T.astype(BF)
        joint_grad[:, :WIDE] = dq
        bias_grad[0:1, side] += jnp.sum(dq.astype(F32), axis=0, keepdims=True)
        total[...] += dot(joint_grad[...], weight[:, wide], "nt")
        weight_grad[:, wide] += dot(tokens_own[0], joint_grad[...], "tn")

    @pl.when(jnp.logical_not(own))
    def far():
        dq_sums[column] += dq_turned[...]
        total[...] += dot(joint_grad[:, WIDE:], weight[:, last_two], "nt")
        weight_grad[:, last_two] += dot(tokens_rest[0, 0], joint_grad[:, WIDE:], "tn")

    bias_grad[1:2, side] += jnp.sum(joint_grad[:, 2 * WIDE :].astype(F32), axis=0, keepdims=True)

    @pl.when(jnp.logical_and(pair == PAIRS - 1, own))
    def finish_near():
        share_own[0] = total[...] + partial[0]

    @pl.when(jnp.logical_and(pair == PAIRS - 1, jnp.logical_not(own)))
    def finish_far():
        share_rest[0, 0] = total[...].astype(BF)


def pull(e_all, query, pair_own, pair_rest, mixed_grad, mixed_t, inverse, own, rest, weight, partial):
    parts, groups, _, local, _ = e_all.shape
    width = H * HEAD
    each = groups * PAIRS

    def at(place):
        return lambda t: place((t // each + 1) % parts, t // PAIRS % groups, t % PAIRS)

    def own_at(place):
        return lambda t: place(
            jnp.where(t // each == parts - 1, t // PAIRS % groups, 0),
            jnp.where(t // each == parts - 1, t % PAIRS, 0),
        )

    def rest_at(place):
        def index(t):
            t = jnp.minimum(t, (parts - 1) * each - 1)
            return place(t // each, t // PAIRS % groups, t % PAIRS)

        return index

    def still(*shape):
        return pl.BlockSpec(shape, lambda t: (0,) * len(shape), pipeline_mode=pl.Buffered(1))

    return pl.pallas_call(
        functools.partial(pull_kernel, parts, groups),
        grid=(parts * each,),
        in_specs=[
            pl.BlockSpec((1, 1, 2, local, local), at(lambda j, g, p: (j, g, p, 0, 0))),
            pl.BlockSpec((1, local, WIDE), at(lambda j, g, p: (g, 0, p))),
            pl.BlockSpec((1, local, 2 * WIDE), own_at(lambda g, p: (g, 0, p))),
            pl.BlockSpec((1, 1, local, 2 * WIDE), rest_at(lambda j, g, p: (j, g, 0, p))),
            pl.BlockSpec((1, local, WIDE), at(lambda j, g, p: (g, 0, p))),
            pl.BlockSpec((1, WIDE, local), at(lambda j, g, p: (g, p, 0))),
            pl.BlockSpec((1, 1, 2, local), at(lambda j, g, p: (g, p, 0, 0))),
            pl.BlockSpec((1, local, width), own_at(lambda g, p: (g, 0, 0))),
            pl.BlockSpec((1, 1, local, width), rest_at(lambda j, g, p: (j, g, 0, 0))),
            still(width, 3 * width),
            pl.BlockSpec((1, local, width), own_at(lambda g, p: (g, 0, 0))),
        ],
        out_specs=[
            pl.BlockSpec((1, 1, local, width), rest_at(lambda j, g, p: (j, g, 0, 0))),
            pl.BlockSpec((1, local, width), own_at(lambda g, p: (g, 0, 0))),
            still(width, 3 * width),
            still(8, width),
        ],
        out_shape=[
            jax.ShapeDtypeStruct((parts - 1, groups, local, width), BF),
            jax.ShapeDtypeStruct((groups, local, width), F32),
            jax.ShapeDtypeStruct((width, 3 * width), F32),
            jax.ShapeDtypeStruct((8, width), F32),
        ],
        scratch_shapes=[
            pltpu.VMEM((2, local, local), BF),
            pltpu.VMEM((local, 3 * WIDE), BF),
            pltpu.VMEM((local, width), F32),
            pltpu.VMEM((each, WIDE, local), F32),
            pltpu.VMEM((WIDE, local), F32),
        ],
        compiler_params=params(60, 1),
        name="pull",
    )(e_all, query, pair_own, pair_rest, mixed_grad, mixed_t, inverse, own, rest, weight, partial)


def per_device(
    tokens,
    lengths,
    joint_weight,
    joint_bias,
    out_weight,
    out_bias,
    gain_first,
    shift_first,
    up_weight,
    up_bias,
    down_weight,
    down_bias,
    gain_second,
    shift_second,
    cotangent,
):
    groups, local, width = tokens.shape
    parts = lax.axis_size("seq")
    devices = lax.axis_size("dp") * parts
    me = lax.axis_index("seq")
    rows = groups * local
    tokens_low = tokens.astype(BF)
    tokens_rest = jnp.stack(
        [
            lax.ppermute(tokens_low, "seq", [(i, (i - shift) % parts) for i in range(parts)])
            for shift in range(1, parts)
        ]
    )

    own_rows = joint_weight.shape[0]
    joint_shard = (
        joint_weight.astype(BF)
        .reshape(own_rows, PAIRS, 2, 3, HEAD)
        .transpose(0, 1, 3, 2, 4)
        .reshape(own_rows, 3 * width)
    )
    vectors = [
        joint_bias,
        out_bias,
        gain_first,
        shift_first,
        up_bias,
        down_bias,
        gain_second,
        shift_second,
    ]
    lens = [v.shape[0] for v in vectors]
    packed = jnp.concatenate([v.astype(BF) for v in vectors])
    room = -packed.shape[0] % 128
    packed = jnp.pad(packed, (0, room)).reshape(1, -1)
    packed = jnp.broadcast_to(packed, (16, packed.shape[1]))
    joint_w, packed = gather_weights([joint_shard, packed], (0, 1))
    packed = packed.reshape(devices, 16, -1)[:, 0].astype(F32)
    full, at = [], 0
    for size in lens:
        full.append(packed[:, at : at + size].reshape(devices * size))
        at += size
    pair_full, out_b, gain_1, shift_1, up_b, down_b, gain_2, shift_2 = full
    pair_full = pair_full.reshape(PAIRS, 2, 2, HEAD)
    bias_all = jnp.stack(
        [pair_full[:, :, 0], jnp.zeros((PAIRS, 2, HEAD), F32), pair_full[:, :, 1]], axis=1
    ).reshape(1, 3 * width)
    blank = jnp.zeros(width, F32)
    row_stack = jnp.stack([out_b, gain_1, shift_1, down_b, gain_2, shift_2, blank, blank])

    query, pair_own = project(tokens_low.reshape(rows, width), joint_w, bias_all, True)
    (pair_rest,) = project(tokens_rest.reshape(-1, width), joint_w, bias_all, False)
    query = query.reshape(groups, local, width)
    pair_own = pair_own.reshape(groups, local, 2 * width)
    pair_rest = pair_rest.reshape(parts - 1, groups, local, 2 * width)

    places = (me + jnp.arange(parts, dtype=jnp.int32)) % parts * local
    info = jnp.concatenate([lengths, places.astype(jnp.int32)])
    (e_all, mixed, mixed_t, inverse), (out_w, up_w, down_w) = attend(
        info,
        query,
        pair_own,
        pair_rest,
        [out_weight.astype(BF), up_weight.astype(BF), down_weight.astype(BF)],
        (0, 0, 1),
    )

    result, partial, mixed_grad, out_wg, up_wg, down_wg, row_sums, up_bias_sum = middle(
        tokens.reshape(rows, width),
        cotangent.reshape(rows, width),
        mixed.reshape(rows, width),
        out_w,
        up_w,
        down_w,
        row_stack,
        up_b.reshape(1, -1),
    )
    mixed_grad = mixed_grad.reshape(groups, local, width)
    out_sum, up_sum, down_sum = owner_sums([out_wg, up_wg, down_wg])

    share_rest, input_grad, joint_wg, bias_grad = pull(
        e_all,
        query,
        pair_own,
        pair_rest,
        mixed_grad,
        mixed_t,
        inverse,
        tokens_low,
        tokens_rest,
        joint_w,
        partial.reshape(groups, local, width),
    )
    for shift in range(1, parts):
        piece = lax.ppermute(
            share_rest[shift - 1], "seq", [(i, (i + shift) % parts) for i in range(parts)]
        )
        input_grad = input_grad + piece.astype(F32)

    pair_grad = jnp.stack(
        [bias_grad[0].reshape(H, HEAD), bias_grad[1].reshape(H, HEAD)], axis=1
    ).reshape(2 * width)
    sums = [
        pair_grad,
        row_sums[0],
        row_sums[1],
        row_sums[2],
        up_bias_sum[0],
        row_sums[3],
        row_sums[4],
        row_sums[5],
    ]
    vec = jnp.concatenate([s.reshape(devices, -1) for s in sums], axis=1)
    joint_sum, vec = owner_sums([joint_wg, vec])
    joint_sum = joint_sum.reshape(own_rows, PAIRS, 3, 2, HEAD).transpose(0, 1, 3, 2, 4)
    joint_sum = joint_sum.reshape(own_rows, 3 * width)
    vec = vec.reshape(-1)
    small, at = [], 0
    for size in lens:
        small.append(vec[at : at + size])
        at += size
    return (
        result.reshape(groups, local, width),
        input_grad,
        joint_sum,
        small[0],
        out_sum,
        small[1],
        small[2],
        small[3],
        up_sum,
        small[4],
        down_sum,
        small[5],
        small[6],
        small[7],
    )


def solution(mesh):
    both = ("dp", "seq")
    matrix, vector, whole = P(both, None), P(both), P("dp", "seq", None)
    return jax.shard_map(
        per_device,
        mesh=mesh,
        in_specs=(
            whole,
            P("dp"),
            matrix,
            vector,
            matrix,
            vector,
            vector,
            vector,
            matrix,
            vector,
            matrix,
            vector,
            vector,
            vector,
            whole,
        ),
        out_specs=(
            whole,
            whole,
            matrix,
            vector,
            matrix,
            vector,
            vector,
            vector,
            matrix,
            vector,
            matrix,
            vector,
            vector,
            vector,
        ),
        check_vma=False,
    )
```

time: 547 us -> 442 us (0.81); the launches traced: 539 us -> 441 us
  Pallas kernels: 355 us -> 285 us
  matrix products: 14 us -> 0 us
  starting transfers between devices: 35.2 us -> 24 us
  waiting for transfers between devices: 75.1 us -> 85.5 us
  local copies, waits for them, and re-layouts: 34.6 us -> 26.1 us
    pallas_call x3 -> x4, Pallas kernels: 227 us -> 178 us  [the longest x1 98.6 us: pull(): pl.pallas_call(functools.partial(pull_kernel, parts, groups), grid=(parts...]
    pallas_call x1, Pallas kernels: 77.6 us -> 57.5 us  [gather_weights(): pl.pallas_call(functools.partial(gather_kernel, orders, bits_dp, bits_seq...]
    convert_element_type x2 -> x0, local copies, waits for them, and re-layouts: 15 us -> none  [the longest x1 8.64 us: per_device(): joint_own = joint_own.astype(BF).reshape(groups, local, 3 * width)]
    dot_general x2 -> x0, matrix products: 14 us -> none  [the longest x1 7.39 us: per_device(): jnp.dot(tokens_low.reshape(rows, width), joint_w, preferred_element_type=...]
    ppermute x25, starting transfers between devices: 31.6 us -> 19.5 us  [owner_sums(): arrived = [lax.ppermute(s, name, pairs) for s in sent]]
    ppermute x25, waiting for transfers between devices: 75.1 us -> 85.5 us  [owner_sums(): arrived = [lax.ppermute(s, name, pairs) for s in sent]]
    unnamed x48 -> x58, local copies, waits for them, and re-layouts: 0.11 us -> 8.34 us
  transfers between devices with their start and end apart: 27 -> 27, of which waited for: 18 -> 18; matrix products, arithmetic and copies ran while one was open for 9% -> 6% of each run, Pallas kernels for 38% -> 37%
where the time goes in v2:
time: 442 us; the launch traced here: 441 us
  Pallas kernels  285 us (64%)
  waiting for transfers between devices  85.5 us (19%)
  local copies, waits for them, and re-layouts  26.1 us (6%)
  starting transfers between devices  24 us (5%)
  other arithmetic  18.7 us (4%)
    pallas_call x1, Pallas kernels, pull(): pl.pallas_call(functools.partial(pull_kernel, parts, groups), grid=(parts...  98.6 us
    ppermute x25, waiting for transfers between devices, owner_sums(): arrived = [lax.ppermute(s, name, pairs) for s in sent]  85.5 us
    pallas_call x1, Pallas kernels, attend(): pl.pallas_call(functools.partial(attend_kernel, parts, groups, steps, blo...  70.2 us
    pallas_call x1, Pallas kernels, gather_weights(): pl.pallas_call(functools.partial(gather_kernel, orders, bits_dp, bits_seq...  57.5 us
    pallas_call x1, Pallas kernels, middle(): pl.pallas_call(middle_kernel, grid=(count // block,), in_specs=[moving(),...  49.7 us
    ppermute x25, starting transfers between devices, owner_sums(): arrived = [lax.ppermute(s, name, pairs) for s in sent]  19.5 us
    pallas_call x2, Pallas kernels, project(): pl.pallas_call(functools.partial(project_kernel, own), grid=(count // blo...  9.34 us
  transfers between devices with their start and end apart: 27, of which 18 were waited for; matrix products, arithmetic and copies ran while one was open for 6% of the time, Pallas kernels for 37%

profile of v2, /device:TPU:0, one launch (start us, length us, event | category | flops | bytes accessed | tf_op | source)
XLA Modules:
  0.0 441.1 jit_solution(16920375491640248006)
XLA Ops:
  0.8 2.6 convert_element_type.315.tokens_own
  3.4 3.0 collective-permute-start
  8.3 57.5 %gather_weights.1 = (bf16[2,2,2,2,2,16,1536]{6,5,4,3,2,1,0:T(8,128)(2,1)}, bf16[2,2,2,2,2,16,256]{6,5,4,3,2,1,0:T(8,128)(2,1)}) custom-call(bf16[16,1536]{1,0:T(8,128)(2,1)} %reshape.220.refs_0_, bf16[16,256]{1,0:T(8,128)(2,1)} %broadcast_in_dim.2.refs_1_), custom_call_target="tpu_custom_call" | custom-call | tf_op jit(solution)/shard_map/gather_weights/pallas_call | solution.py:127
  71.8 5.1 %project_own.1 = (bf16[2048,512]{1,0:T(8,128)(2,1)S(1)}, bf16[2048,1024]{1,0:T(8,128)(2,1)S(1)}) custom-call(bf16[2048,512]{1,0:T(8,128)(2,1)S(1)} %bitcast.164, bf16[512,1536]{1,0:T(8,128)(2,1)S(1)} %bitcast.166, f32[1,1536]{1,0:T(1,128)S(1)} %reshape.222.bias), custom_call_target="tpu_custom_call" | custom-call | tf_op jit(solution)/shard_map/project_own/pallas_call | solution.py:199
  82.9 4.3 project_rest.1
  89.2 70.2 %attend.1 = (bf16[2,2,8,1024,1024]{4,3,2,1,0:T(8,128)(2,1)}, bf16[2,1024,512]{2,1,0:T(8,128)(2,1)}, bf16[2,512,1024]{2,1,0:T(8,128)(2,1)}, f32[2,4,2,1024]{3,2,1...) custom-call(s32[4]{0:T(128)} %pad_add_fusion.refs_0_, ...), custom_call_target="tpu_custom_call" | custom-call | tf_op jit(solution)/shard_map/attend/pallas_call | solution.py:326
  159.4 49.7 %middle.1 = (f32[2048,512]{1,0:T(8,128)}, f32[2048,512]{1,0:T(8,128)}, bf16[2048,512]{1,0:T(8,128)(2,1)}, f32[512,512]{1,0:T(8,128)}, f32[512,2048]{1,0:T(8,128)...) custom-call(f32[2048,512]{1,0:T(8,128)} %bitcast.170, f32[2048,512]{1,0:T(8,128)} %bitcast.172, ...), custom_call_target="tpu_custom_call" | custom-call | tf_op jit(solution)/shard_map/middle/pallas_call | solution.py:468
  213.3 98.6 %pull.1 = (bf16[1,2,1024,512]{3,2,1,0:T(8,128)(2,1)}, f32[2,1024,512]{2,1,0:T(8,128)}, f32[512,1536]{1,0:T(8,128)}, f32[8,512]{1,0:T(8,128)}) custom-call(bf16[2,2,8,1024,1024]{4,3,2,1,0:T(8,128)(2,1)} %get-tuple-element.46.e_part, bf16[2,1024,512]{2,1,0:T(8,128)(2,1)} %bitcast.169, bf16[2,1024,1024]{2,1,0:T(8,128)(2,1)} %bitcast.163, ...), custom_call_target="tpu_custom_call" | custom-call | tf_op jit(solution)/shard_map/pull/pallas_call | solution.py:643
  321.3 3.0 collective-permute-done.9
  324.5 3.4 collective-permute-done.10
  330.7 3.3 collective-permute-done.11
  334.5 41.8 %collective-permute-done.13 = bf16[2,2,2,16,512]{4,3,0,1,2:T(8,128)(2,1)S(1)} collective-permute-done((bf16[2,2,2,16,512]{4,3,0,1,2:T(8,128)(2,1)S(1)}, bf16[2,2,2,16,512]{4,3,0,1,2:T(8,128)(2,1)S(1)}, u32[]{:S(2)}, u32[]{:S(2)}) %collective-permute-start.13) | collective-permute-done | bytes 131104 | tf_op jit(solution)/shard_map/ppermute | solution.py:167
  377.6 3.0 collective-permute-done.14
  381.7 3.0 collective-permute-done.15
  387.2 2.2 collective-permute-done.16
  390.1 4.5 %collective-permute-done.3 = bf16[2,2,2,16,1536]{4,3,0,1,2:T(8,128)(2,1)S(1)} collective-permute-done((bf16[2,2,2,16,1536]{4,3,0,1,2:T(8,128)(2,1)S(1)}, bf16[2,2,2,16,1536]{4,3,0,1,2:T(8,128)(2,1)S(1)}, u32[]{:S(2)}, u32[]{:S(2)}) %collective-permute-start.3) | collective-permute-done | bytes 393248 | tf_op jit(solution)/shard_map/ppermute | solution.py:167
  398.2 2.2 collective-permute-done.4
  405.2 2.1 collective-permute-start.6
  408.2 2.0 collective-permute-done.6
  413.6 3.6 collective-permute-done.18
  421.1 3.8 collective-permute-done.19
  427.7 2.3 collective-permute-done.20
  432.0 4.0 collective-permute-done.21
  436.7 4.4 convert_add_fusion
  (217 shorter events, 59.9 us)
Async XLA Ops:
  3.4 78.2 %collective-permute-start = (bf16[2,1024,512]{2,1,0:T(8,128)(2,1)S(1)}, bf16[2,1024,512]{2,1,0:T(8,128)(2,1)}, u32[]{:S(2)}, u32[]{:S(2)}) collective-permute-start(bf16[2,1024,512]{2,1,0:T(8,128)(2,1)S(1)} %convert_element_type.315.tokens_own), channel_id=1, source_target_pairs={{0,1},{1,0},{2,3},{3,2},{4,5},{5,4},{6,7},{7,6},{8,9},{9,8},{10,11... | collective-permute-start | bytes 6291464 | tf_op jit(solution)/shard_map/ppermute | solution.py:708
  210.9 184.0 %collective-permute-start.22 = (bf16[2,2,2,2,64,512]{5,4,0,1,2,3:T(8,128)(2,1)S(1)}, bf16[2,2,2,2,64,512]{5,4,0,1,2,3:T(8,128)(2,1)}, u32[]{:S(2)}, u32[]{:S(2)}) collective-permute-start(bf16[2,2,2,2,64,512]{5,4,0,1,2,3:T(8,128)(2,1)S(1)} %fusion.1), channel_id=1, source_target_pairs={{0,2},{2,0},{4,6},{6,4},{8,10},{10,8},{12,14},{14,12},{16,18},{18,... | collective-permute-start | bytes 3145736 | tf_op jit(solution)/shard_map/ppermute | solution.py:167
  212.7 189.5 %collective-permute-start.17 = (bf16[2,2,2,2,16,2048]{5,4,0,1,2,3:T(8,128)(2,1)S(1)}, bf16[2,2,2,2,16,2048]{5,4,0,1,2,3:T(8,128)(2,1)}, u32[]{:S(2)}, u32[]{:S(2)}) collective-permute-start(bf16[2,2,2,2,16,2048]{5,4,0,1,2,3:T(8,128)(2,1)S(1)} %fusion), channel_id=1, source_target_pairs={{0,2},{2,0},{4,6},{6,4},{8,10},{10,8},{12,14},{14,12},{16,18},{18,... | collective-permute-start | bytes 3145736 | tf_op jit(solution)/shard_map/ppermute | solution.py:167
  316.3 13.1 %collective-permute-start.12 = (bf16[2,2,2,2,16,512]{5,4,0,1,2,3:T(8,128)(2,1)S(1)}, bf16[2,2,2,2,16,512]{5,4,0,1,2,3:T(8,128)(2,1)S(1)}, u32[]{:S(2)}, u32[]{:S(2)}) collective-permute-start(bf16[2,2,2,2,16,512]{5,4,0,1,2,3:T(8,128)(2,1)S(1)} %fusion.8), channel_id=1, source_target_pairs={{0,2},{2,0},{4,6},{6,4},{8,10},{10,8},{12,14},{14,12},{16,18},{18,... | collective-permute-start | bytes 786440 | tf_op jit(solution)/shard_map/ppermute | solution.py:167
  316.9 3.7 collective-permute-start.8
  320.1 65.8 %collective-permute-start.2 = (bf16[2,2,2,2,16,1536]{5,4,0,1,2,3:T(8,128)(2,1)S(1)}, bf16[2,2,2,2,16,1536]{5,4,0,1,2,3:T(8,128)(2,1)S(1)}, u32[]{:S(2)}, u32[]{:S(2)}) collective-permute-start(bf16[2,2,2,2,16,1536]{5,4,0,1,2,3:T(8,128)(2,1)S(1)} %fusion.2), channel_id=1, source_target_pairs={{0,2},{2,0},{4,6},{6,4},{8,10},{10,8},{12,14},{14,12},{16,18},{18,... | collective-permute-start | bytes 2359304 | tf_op jit(solution)/shard_map/ppermute | solution.py:167
  327.9 108.7 %collective-permute-start.1 = (bf16[2,1024,512]{2,1,0:T(8,128)(2,1)}, bf16[2,1024,512]{2,1,0:T(8,128)(2,1)}, u32[]{:S(2)}, u32[]{:S(2)}) collective-permute-start(bf16[2,1024,512]{2,1,0:T(8,128)(2,1)} %bitcast.194), channel_id=1, source_target_pairs={{0,1},{1,0},{2,3},{3,2},{4,5},{5,4},{6,7},{7,6},{8,9},{9,8},{10,11... | collective-permute-start | bytes 6291464 | tf_op jit(solution)/shard_map/ppermute | solution.py:793
  329.4 4.5 %collective-permute-start.11 = (bf16[1,192]{1,0:T(2,128)(2,1)S(1)}, bf16[1,192]{1,0:T(2,128)(2,1)S(1)}, u32[]{:S(2)}, u32[]{:S(2)}) collective-permute-start(bf16[1,192]{1,0:T(2,128)(2,1)S(1)} %fusion.31), channel_id=1, source_target_pairs={{0,16},{2,18},{4,20},{6,22},{8,24},{10,26},{12,28},{14,30},{16,0},... | collective-permute-start | bytes 1160 | tf_op jit(solution)/shard_map/ppermute | solution.py:167
  334.0 42.3 %collective-permute-start.13 = (bf16[2,2,2,16,512]{4,3,0,1,2:T(8,128)(2,1)S(1)}, bf16[2,2,2,16,512]{4,3,0,1,2:T(8,128)(2,1)S(1)}, u32[]{:S(2)}, u32[]{:S(2)}) collective-permute-start(bf16[2,2,2,16,512]{4,3,0,1,2:T(8,128)(2,1)S(1)} %fusion.10), channel_id=1, source_target_pairs={{0,1},{1,0},{2,3},{3,2},{4,5},{5,4},{6,7},{7,6},{8,9},{9,8},{10,11... | collective-permute-start | bytes 393224 | tf_op jit(solution)/shard_map/ppermute | solution.py:167
  376.4 4.3 collective-permute-start.14
  380.7 4.0 collective-permute-start.15
  384.7 4.7 %collective-permute-start.16 = (bf16[16,512]{1,0:T(8,128)(2,1)S(1)}, bf16[16,512]{1,0:T(8,128)(2,1)S(1)}, u32[]{:S(2)}, u32[]{:S(2)}) collective-permute-start(bf16[16,512]{1,0:T(8,128)(2,1)S(1)} %fusion.19), channel_id=1, source_target_pairs={{0,16},{2,18},{4,20},{6,22},{8,24},{10,26},{12,28},{14,30},{16,0},... | collective-permute-start | bytes 49160 | tf_op jit(solution)/shard_map/ppermute | solution.py:167
  386.1 8.4 %collective-permute-start.3 = (bf16[2,2,2,16,1536]{4,3,0,1,2:T(8,128)(2,1)S(1)}, bf16[2,2,2,16,1536]{4,3,0,1,2:T(8,128)(2,1)S(1)}, u32[]{:S(2)}, u32[]{:S(2)}) collective-permute-start(bf16[2,2,2,16,1536]{4,3,0,1,2:T(8,128)(2,1)S(1)} %fusion.5), channel_id=1, source_target_pairs={{0,1},{1,0},{2,3},{3,2},{4,5},{5,4},{6,7},{7,6},{8,9},{9,8},{10,11... | collective-permute-start | bytes 1179656 | tf_op jit(solution)/shard_map/ppermute | solution.py:167
  394.6 5.7 %collective-permute-start.4 = (bf16[2,2,16,1536]{3,2,0,1:T(8,128)(2,1)S(1)}, bf16[2,2,16,1536]{3,2,0,1:T(8,128)(2,1)S(1)}, u32[]{:S(2)}, u32[]{:S(2)}) collective-permute-start(bf16[2,2,16,1536]{3,2,0,1:T(8,128)(2,1)S(1)} %fusion.9), channel_id=1, source_target_pairs={{0,4},{2,6},{4,0},{6,2},{8,12},{10,14},{12,8},{14,10},{16,20},{18,... | collective-permute-start | bytes 589832 | tf_op jit(solution)/shard_map/ppermute | solution.py:167
  397.5 14.1 %collective-permute-start.23 = (bf16[2,2,2,64,512]{4,3,0,1,2:T(8,128)(2,1)}, bf16[2,2,2,64,512]{4,3,0,1,2:T(8,128)(2,1)}, u32[]{:S(2)}, u32[]{:S(2)}) collective-permute-start(bf16[2,2,2,64,512]{4,3,0,1,2:T(8,128)(2,1)} %fusion.4), channel_id=1, source_target_pairs={{0,1},{1,0},{2,3},{3,2},{4,5},{5,4},{6,7},{7,6},{8,9},{9,8},{10,11... | collective-permute-start | bytes 1572872 | tf_op jit(solution)/shard_map/ppermute | solution.py:167
  400.4 4.7 %collective-permute-start.5 = (bf16[2,16,1536]{2,1,0:T(8,128)(2,1)S(1)}, bf16[2,16,1536]{2,1,0:T(8,128)(2,1)S(1)}, u32[]{:S(2)}, u32[]{:S(2)}) collective-permute-start(bf16[2,16,1536]{2,1,0:T(8,128)(2,1)S(1)} %fusion.13), channel_id=1, source_target_pairs={{0,8},{2,10},{4,12},{6,14},{8,0},{10,2},{12,4},{14,6},{16,24},{18,... | collective-permute-start | bytes 294920 | tf_op jit(solution)/shard_map/ppermute | solution.py:167
  405.2 5.1 %collective-permute-start.6 = (bf16[16,1536]{1,0:T(8,128)(2,1)S(1)}, bf16[16,1536]{1,0:T(8,128)(2,1)S(1)}, u32[]{:S(2)}, u32[]{:S(2)}) collective-permute-start(bf16[16,1536]{1,0:T(8,128)(2,1)S(1)} %fusion.17), channel_id=1, source_target_pairs={{0,16},{2,18},{4,20},{6,22},{8,24},{10,26},{12,28},{14,30},{16,0},... | collective-permute-start | bytes 147464 | tf_op jit(solution)/shard_map/ppermute | solution.py:167
  407.3 9.9 %collective-permute-start.18 = (bf16[2,2,2,16,2048]{4,3,0,1,2:T(8,128)(2,1)S(1)}, bf16[2,2,2,16,2048]{4,3,0,1,2:T(8,128)(2,1)}, u32[]{:S(2)}, u32[]{:S(2)}) collective-permute-start(bf16[2,2,2,16,2048]{4,3,0,1,2:T(8,128)(2,1)S(1)} %fusion.3), channel_id=1, source_target_pairs={{0,1},{1,0},{2,3},{3,2},{4,5},{5,4},{6,7},{7,6},{8,9},{9,8},{10,11... | collective-permute-start | bytes 1572872 | tf_op jit(solution)/shard_map/ppermute | solution.py:167
  413.1 7.2 %collective-permute-start.24 = (bf16[2,2,64,512]{3,2,0,1:T(8,128)(2,1)S(1)}, bf16[2,2,64,512]{3,2,0,1:T(8,128)(2,1)S(1)}, u32[]{:S(2)}, u32[]{:S(2)}) collective-permute-start(bf16[2,2,64,512]{3,2,0,1:T(8,128)(2,1)S(1)} %fusion.7), channel_id=1, source_target_pairs={{0,4},{2,6},{4,0},{6,2},{8,12},{10,14},{12,8},{14,10},{16,20},{18,... | collective-permute-start | bytes 786440 | tf_op jit(solution)/shard_map/ppermute | solution.py:167
  418.5 6.4 %collective-permute-start.19 = (bf16[2,2,16,2048]{3,2,0,1:T(8,128)(2,1)S(1)}, bf16[2,2,16,2048]{3,2,0,1:T(8,128)(2,1)S(1)}, u32[]{:S(2)}, u32[]{:S(2)}) collective-permute-start(bf16[2,2,16,2048]{3,2,0,1:T(8,128)(2,1)S(1)} %fusion.6), channel_id=1, source_target_pairs={{0,4},{2,6},{4,0},{6,2},{8,12},{10,14},{12,8},{14,10},{16,20},{18,... | collective-permute-start | bytes 786440 | tf_op jit(solution)/shard_map/ppermute | solution.py:167
  420.3 5.4 %collective-permute-start.25 = (bf16[2,64,512]{2,1,0:T(8,128)(2,1)S(1)}, bf16[2,64,512]{2,1,0:T(8,128)(2,1)S(1)}, u32[]{:S(2)}, u32[]{:S(2)}) collective-permute-start(bf16[2,64,512]{2,1,0:T(8,128)(2,1)S(1)} %fusion.12), channel_id=1, source_target_pairs={{0,8},{2,10},{4,12},{6,14},{8,0},{10,2},{12,4},{14,6},{16,24},{18,... | collective-permute-start | bytes 393224 | tf_op jit(solution)/shard_map/ppermute | solution.py:167
  425.0 5.0 %collective-permute-start.20 = (bf16[2,16,2048]{2,1,0:T(8,128)(2,1)S(1)}, bf16[2,16,2048]{2,1,0:T(8,128)(2,1)S(1)}, u32[]{:S(2)}, u32[]{:S(2)}) collective-permute-start(bf16[2,16,2048]{2,1,0:T(8,128)(2,1)S(1)} %fusion.11), channel_id=1, source_target_pairs={{0,8},{2,10},{4,12},{6,14},{8,0},{10,2},{12,4},{14,6},{16,24},{18,... | collective-permute-start | bytes 393224 | tf_op jit(solution)/shard_map/ppermute | solution.py:167
  425.8 5.5 %collective-permute-start.26 = (bf16[64,512]{1,0:T(8,128)(2,1)S(1)}, bf16[64,512]{1,0:T(8,128)(2,1)S(1)}, u32[]{:S(2)}, u32[]{:S(2)}) collective-permute-start(bf16[64,512]{1,0:T(8,128)(2,1)S(1)} %fusion.16), channel_id=1, source_target_pairs={{0,16},{2,18},{4,20},{6,22},{8,24},{10,26},{12,28},{14,30},{16,0},... | collective-permute-start | bytes 196616 | tf_op jit(solution)/shard_map/ppermute | solution.py:167
  430.1 5.9 %collective-permute-start.21 = (bf16[16,2048]{1,0:T(8,128)(2,1)S(1)}, bf16[16,2048]{1,0:T(8,128)(2,1)S(1)}, u32[]{:S(2)}, u32[]{:S(2)}) collective-permute-start(bf16[16,2048]{1,0:T(8,128)(2,1)S(1)} %fusion.15), channel_id=1, source_target_pairs={{0,16},{2,18},{4,20},{6,22},{8,24},{10,26},{12,28},{14,30},{16,0},... | collective-permute-start | bytes 196616 | tf_op jit(solution)/shard_map/ppermute | solution.py:167
  (31 other events, 693.4 us)

commit v3 on v2

--- a/solution.py
+++ b/solution.py
@@ -30,6 +30,10 @@
 
 def dot(left, right, form="nn"):
     return lax.dot_general(left, right, FORMS[form], preferred_element_type=F32)
+
+
+def whole_tiles(width, devices):
+    return width // devices % 16 == 0
 
 
 def params(limit, steps):
@@ -145,13 +149,9 @@
     bits_dp, bits_seq = log2(size_dp), log2(size_seq)
     bits = bits_dp + bits_seq
     dp, seq = lax.axis_index("dp"), lax.axis_index("seq")
-    rows = [a.shape[0] // (size_dp * size_seq) for a in arrays]
-    arrays = [
-        a.reshape((2,) * bits + (r,) + a.shape[1:]) for a, r in zip(arrays, rows)
-    ]
+    arrays = [a.reshape((2,) * bits + (-1,) + a.shape[1:]) for a in arrays]
     left = list(range(bits))
-    order = [bits_dp - 1] + list(range(bits_dp, bits)) + list(range(bits_dp - 2, -1, -1))
-    for bit in order:
+    for bit in [bits_dp - 1] + list(range(bits_dp, bits)) + list(range(bits_dp - 2, -1, -1)):
         axis = left.index(bit)
         left.remove(bit)
         if bit < bits_dp:
@@ -164,9 +164,71 @@
             lax.dynamic_index_in_dim(a, 1 - mine, axis, keepdims=False).astype(BF) for a in arrays
         ]
         kept = [lax.dynamic_index_in_dim(a, mine, axis, keepdims=False) for a in arrays]
-        arrived = [lax.ppermute(s, name, pairs) for s in sent]
+        arrived = [lax.ppermute(v, name, pairs) for v in sent]
         arrays = [k + a.astype(F32) for k, a in zip(kept, arrived)]
     return arrays
+
+
+class Halving:
+    def __init__(self, order, held, landing, send_sem, recv_sem, mine, partner, source=None):
+        self.order, self.held, self.landing = order, held, landing
+        self.send_sem, self.recv_sem = send_sem, recv_sem
+        self.mine, self.partner, self.source = mine, partner, source
+
+    def place(self, stage, value):
+        at = []
+        for bit in range(len(self.mine)):
+            if bit in self.order[:stage]:
+                at.append(self.mine[bit])
+            elif bit == self.order[stage]:
+                at.append(value)
+            else:
+                at.append(slice(None))
+        return at
+
+    def copy(self, stage):
+        bit = self.order[stage]
+        at = self.place(stage, 1 - self.mine[bit])
+        source = self.source if stage == 0 and self.source is not None else self.held
+        if source is self.held and self.source is not None:
+            at = at[: self.order[0]] + at[self.order[0] + 1 :]
+        return pltpu.make_async_remote_copy(
+            src_ref=source.at[tuple(at)],
+            dst_ref=self.landing[stage],
+            send_sem=self.send_sem.at[stage],
+            recv_sem=self.recv_sem.at[stage],
+            device_id=self.partner(bit),
+            device_id_type=MESH,
+        )
+
+    def add(self, stage, out=None):
+        at = self.place(stage, self.mine[self.order[stage]])
+        if self.source is not None:
+            at = at[: self.order[0]] + at[self.order[0] + 1 :]
+        free = [i for i, a in enumerate(at) if isinstance(a, slice)]
+        landing = self.landing[stage]
+
+        def one(flat, carry):
+            inner = [lax.rem(flat // 2 ** (len(free) - 1 - i), 2) for i in range(len(free))]
+            there = list(at)
+            for axis, value in zip(free, inner):
+                there[axis] = value
+            there = tuple(there)
+            value = self.held[there].astype(F32) + landing[tuple(inner)].astype(F32)
+            if out is None:
+                self.held[there] = value.astype(BF)
+            else:
+                out[...] = value
+            return carry
+
+        if free:
+            lax.fori_loop(0, 2 ** len(free), one, 0)
+        else:
+            one(0, 0)
+
+
+def landing_shapes(bits, rows, width):
+    return [pltpu.VMEM((2,) * (bits - 1 - s) + (rows, width), BF) for s in range(bits)]
 
 
 def project_kernel(own, tokens, weight, bias, *outs):
@@ -372,6 +434,7 @@
 
 
 def middle_kernel(
+    packed,
     tokens,
     cotangent,
     mixed,
@@ -383,6 +446,9 @@
     result,
     partial,
     mixed_grad,
+    upper_sums,
+    lower_sums,
+    vec_sums,
     out_wg,
     up_wg,
     down_wg,
@@ -453,20 +519,58 @@
     row_sums[4:5] += total(grad * n_two)
     row_sums[5:6] += total(grad)
 
-
-def middle(tokens, cotangent, mixed, out_w, up_w, down_w, rows, up_bias):
+    @pl.when(pl.program_id(0) == pl.num_programs(0) - 1)
+    def pack():
+        width = tokens.shape[1]
+        pieces = up_wg.shape[1] // width
+        vec_sums[...] = jnp.zeros_like(vec_sums)
+        vec_sums[0:8] = row_sums[...]
+        for piece in range(pieces):
+            columns = slice(piece * width, (piece + 1) * width)
+            vec_sums[8 + piece : 9 + piece] = up_bias_sum[:, columns]
+        if not packed:
+            upper_sums[:, :width] = out_wg[...]
+            upper_sums[:, width:] = up_wg[...]
+            lower_sums[...] = down_wg[...]
+            return
+        owners = upper_sums.shape[0]
+        rows_out = out_wg.shape[0] // owners
+        rows_down = down_wg.shape[0] // owners
+
+        def one(owner, carry):
+            near = pl.ds(pl.multiple_of(owner * rows_out, rows_out), rows_out)
+            upper_sums[owner, :rows_out] = out_wg[near].astype(BF)
+            for piece in range(pieces):
+                columns = slice(piece * width, (piece + 1) * width)
+                to = slice((piece + 1) * rows_out, (piece + 2) * rows_out)
+                upper_sums[owner, to] = up_wg[near, columns].astype(BF)
+            far = pl.ds(pl.multiple_of(owner * rows_down, rows_down), rows_down)
+            lower_sums[owner] = down_wg[far].astype(BF)
+            return carry
+
+        lax.fori_loop(0, owners, one, 0)
+
+
+def middle(tokens, cotangent, mixed, out_w, up_w, down_w, rows, up_bias, owners):
     count, width = tokens.shape
     hidden = up_w.shape[1]
     block = min(256, count)
+    packed = whole_tiles(width, owners)
 
     def moving(columns=width):
         return pl.BlockSpec((block, columns), lambda b: (b, 0))
 
     def still(*shape):
-        return pl.BlockSpec(shape, lambda b: (0, 0), pipeline_mode=pl.Buffered(1))
-
+        return pl.BlockSpec(shape, lambda b: (0,) * len(shape), pipeline_mode=pl.Buffered(1))
+
+    rows_upper = width // owners * (1 + hidden // width)
+    rows_lower = hidden // owners
+    if packed:
+        sums = [((owners, rows_upper, width), BF), ((owners, rows_lower, width), BF)]
+    else:
+        sums = [((width, width + hidden), F32), ((hidden, width), F32)]
     return pl.pallas_call(
-        middle_kernel,
+        functools.partial(middle_kernel, packed),
         grid=(count // block,),
         in_specs=[
             moving(),
@@ -482,55 +586,135 @@
             moving(),
             moving(),
             moving(),
-            still(width, width),
-            still(width, hidden),
-            still(hidden, width),
-            still(8, width),
-            still(1, hidden),
-        ],
+        ]
+        + [still(*shape) for shape, _ in sums]
+        + [still(16, width)],
         out_shape=[
             jax.ShapeDtypeStruct((count, width), F32),
             jax.ShapeDtypeStruct((count, width), F32),
             jax.ShapeDtypeStruct((count, width), BF),
-            jax.ShapeDtypeStruct((width, width), F32),
-            jax.ShapeDtypeStruct((width, hidden), F32),
-            jax.ShapeDtypeStruct((hidden, width), F32),
-            jax.ShapeDtypeStruct((8, width), F32),
-            jax.ShapeDtypeStruct((1, hidden), F32),
+        ]
+        + [jax.ShapeDtypeStruct(shape, kind) for shape, kind in sums]
+        + [jax.ShapeDtypeStruct((16, width), F32)],
+        scratch_shapes=[
+            pltpu.VMEM((width, width), F32),
+            pltpu.VMEM((width, hidden), F32),
+            pltpu.VMEM((hidden, width), F32),
+            pltpu.VMEM((8, width), F32),
+            pltpu.VMEM((1, hidden), F32),
         ],
-        compiler_params=params(58, 1),
+        compiler_params=params(60, 1),
         name="middle",
     )(tokens, cotangent, mixed, out_w, up_w, down_w, rows, up_bias)
 
 
-def pull_kernel(
-    parts,
-    groups,
-    e_part,
-    query,
-    pair_own,
-    pair_rest,
-    mixed_grad,
-    mixed_t,
-    inverse,
-    tokens_own,
-    tokens_rest,
-    weight,
-    partial,
-    share_rest,
-    share_own,
-    weight_grad,
-    bias_grad,
-    d_scores,
-    joint_grad,
-    total,
-    dq_sums,
-    dq_turned,
-):
+def pull_kernel(parts, groups, orders, bits_dp, bits_seq, packed, *refs):
+    bits = bits_dp + bits_seq
+    lands = 3 * bits if packed else 0
+    (
+        e_part,
+        query,
+        pair_own,
+        pair_rest,
+        mixed_grad,
+        mixed_t,
+        inverse,
+        tokens_own,
+        tokens_rest,
+        weight,
+        partial,
+        *sources,
+    ) = refs[: 13 if packed else 11]
+    vec_in = refs[13 if packed else 11]
+    share_own, joint_out, vec_out = refs[14:17] if packed else refs[12:15]
+    (
+        d_scores,
+        joint_grad,
+        total,
+        dq_sums,
+        dq_turned,
+        weight_grad,
+        bias_grad,
+        shares,
+        arrived,
+        share_send,
+        share_recv,
+    ) = refs[19:30] if packed else refs[15:26]
+    if packed:
+        outs = refs[17:19] + (joint_out,)
+        helds = refs[30:33]
+        vec_landing, own_sem, send_sem, recv_sem, vec_send, vec_recv = refs[33:39]
+        landings = [refs[39 + i * bits : 39 + (i + 1) * bits] for i in range(3)]
     step = pl.program_id(0)
+    steps = pl.num_programs(0)
     part = lax.rem(step // (groups * PAIRS) + 1, parts)
     group, pair = lax.rem(step // PAIRS, groups), lax.rem(step, PAIRS)
     own = part == 0
+
+    mine, partner = place_bits(bits_dp, bits_seq)
+    dp, seq = lax.axis_index("dp"), lax.axis_index("seq")
+    streams, halves = [], []
+    if packed:
+        streams = [
+            Halving(
+                orders[i],
+                helds[i],
+                landings[i],
+                send_sem.at[i],
+                recv_sem.at[i],
+                mine,
+                partner,
+                sources[i] if i < 2 else None,
+            )
+            for i in range(3)
+        ]
+        joint = streams.pop()
+        for i, stream in enumerate(streams):
+            at = tuple(stream.place(0, mine[orders[i][0]]))
+            halves.append(
+                pltpu.make_async_copy(stream.source.at[at], stream.held, own_sem.at[i])
+            )
+
+    def share_copy(other, g):
+        return pltpu.make_async_remote_copy(
+            src_ref=shares.at[other - 1, g],
+            dst_ref=arrived.at[other - 1, g],
+            send_sem=share_send.at[other - 1, g],
+            recv_sem=share_recv.at[other - 1, g],
+            device_id=(dp, lax.rem(seq + other, parts)),
+            device_id_type=MESH,
+        )
+
+    @pl.when(step == 0)
+    def enter():
+        barrier = pltpu.get_barrier_semaphore()
+        if packed:
+            greet(partner, bits)
+        for other in range(1, parts):
+            pl.semaphore_signal(
+                barrier,
+                inc=1,
+                device_id=(dp, lax.rem(seq + other, parts)),
+                device_id_type=MESH,
+            )
+        for copy in halves:
+            copy.start()
+        pl.semaphore_wait(barrier, (bits if packed else 0) + parts - 1)
+        for stream in streams:
+            stream.copy(0).start()
+
+    for stage in range(bits if packed else 0):
+        @pl.when(step == (1, 5, 9, 11, 13, 13, 13, 13)[stage])
+        def advance():
+            if stage == 0:
+                for copy in halves:
+                    copy.wait()
+            for stream, out in zip(streams, outs):
+                stream.copy(stage).wait()
+                stream.add(stage, out if stage == bits - 1 else None)
+                if stage < bits - 1:
+                    stream.copy(stage + 1).start()
+
     local = query.shape[1]
     chunk = min(256, local)
     turned = mixed_grad[0].astype(F32).T
@@ -607,19 +791,106 @@
 
     bias_grad[1:2, side] += jnp.sum(joint_grad[:, 2 * WIDE :].astype(F32), axis=0, keepdims=True)
 
-    @pl.when(jnp.logical_and(pair == PAIRS - 1, own))
-    def finish_near():
-        share_own[0] = total[...] + partial[0]
-
-    @pl.when(jnp.logical_and(pair == PAIRS - 1, jnp.logical_not(own)))
-    def finish_far():
-        share_rest[0, 0] = total[...].astype(BF)
-
-
-def pull(e_all, query, pair_own, pair_rest, mixed_grad, mixed_t, inverse, own, rest, weight, partial):
+    for other in range(1, parts):
+        for g in range(groups):
+            @pl.when(step == ((other - 1) * groups + g + 1) * PAIRS - 1)
+            def finish_far():
+                shares[other - 1, g] = total[...].astype(BF)
+                share_copy(other, g).start()
+
+    for g in range(groups):
+        @pl.when(step == ((parts - 1) * groups + g + 1) * PAIRS - 1)
+        def finish_near():
+            value = total[...] + partial[0]
+            for other in range(1, parts):
+                share_copy(other, g).wait()
+                value += arrived[other - 1, g].astype(F32)
+            share_own[0] = value
+
+    @pl.when(step == steps - 1)
+    def finish():
+        vec_out[...] = vec_in[...]
+        vec_out[12:14] = bias_grad[0:2]
+        if not packed:
+            joint_out[...] = weight_grad[...]
+            return
+        rows_each = weight_grad.shape[0] // 2**bits
+        width = total.shape[1]
+
+        def pack(flat, carry):
+            place = tuple(lax.rem(flat // 2 ** (bits - 1 - i), 2) for i in range(bits))
+            near = pl.ds(pl.multiple_of(flat * rows_each, rows_each), rows_each)
+            for piece in range(3):
+                columns = slice(piece * width, (piece + 1) * width)
+                to = slice(piece * rows_each, (piece + 1) * rows_each)
+                joint.held[place + (to,)] = weight_grad[near, columns].astype(BF)
+            return carry
+
+        lax.fori_loop(0, 2**bits, pack, 0)
+        for stage in range(bits):
+            copy = joint.copy(stage)
+            vec_landing[stage, 0] = vec_out[...]
+            vec_copy = pltpu.make_async_remote_copy(
+                src_ref=vec_landing.at[stage, 0],
+                dst_ref=vec_landing.at[stage, 1],
+                send_sem=vec_send.at[stage],
+                recv_sem=vec_recv.at[stage],
+                device_id=partner(orders[2][stage]),
+                device_id_type=MESH,
+            )
+            copy.start()
+            vec_copy.start()
+            vec_copy.wait()
+            vec_out[...] += vec_landing[stage, 1]
+            copy.wait()
+            joint.add(stage, joint_out if stage == bits - 1 else None)
+
+
+def pull(
+    e_all,
+    query,
+    pair_own,
+    pair_rest,
+    mixed_grad,
+    mixed_t,
+    inverse,
+    own,
+    rest,
+    weight,
+    partial,
+    upper_sums,
+    lower_sums,
+    vec_sums,
+):
     parts, groups, _, local, _ = e_all.shape
     width = H * HEAD
     each = groups * PAIRS
+    bits_dp, bits_seq, orders = gather_plan((0, 1, 1))
+    orders = tuple(tuple(reversed(order)) for order in orders)
+    bits = bits_dp + bits_seq
+    packed = whole_tiles(width, 2**bits)
+    split = (2,) * bits
+    sums, out_blocks, extra = [], [], []
+    if packed:
+        rows_upper, rows_lower = upper_sums.shape[1], lower_sums.shape[1]
+        rows_joint = 3 * width // 2**bits
+        sums = [v.reshape(split + v.shape[1:]) for v in (upper_sums, lower_sums)]
+        out_blocks = [(rows_joint, width), (16, width), (rows_upper, width), (rows_lower, width)]
+        extra = [
+            pltpu.VMEM((2,) * (bits - 1) + (rows_upper, width), BF),
+            pltpu.VMEM((2,) * (bits - 1) + (rows_lower, width), BF),
+            pltpu.VMEM(split + (rows_joint, width), BF),
+            pltpu.VMEM((bits, 2, 16, width), F32),
+            pltpu.SemaphoreType.DMA((2,)),
+            pltpu.SemaphoreType.DMA((3, bits)),
+            pltpu.SemaphoreType.DMA((3, bits)),
+            pltpu.SemaphoreType.DMA((bits,)),
+            pltpu.SemaphoreType.DMA((bits,)),
+        ]
+        for count in (rows_upper, rows_lower, rows_joint):
+            extra += landing_shapes(bits, count, width)
+    else:
+        out_blocks = [(width, 3 * width), (16, width)]
 
     def at(place):
         return lambda t: place((t // each + 1) % parts, t // PAIRS % groups, t % PAIRS)
@@ -640,8 +911,9 @@
     def still(*shape):
         return pl.BlockSpec(shape, lambda t: (0,) * len(shape), pipeline_mode=pl.Buffered(1))
 
+    once = pl.Buffered(1)
     return pl.pallas_call(
-        functools.partial(pull_kernel, parts, groups),
+        functools.partial(pull_kernel, parts, groups, orders, bits_dp, bits_seq, packed),
         grid=(parts * each,),
         in_specs=[
             pl.BlockSpec((1, 1, 2, local, local), at(lambda j, g, p: (j, g, p, 0, 0))),
@@ -651,33 +923,57 @@
             pl.BlockSpec((1, local, WIDE), at(lambda j, g, p: (g, 0, p))),
             pl.BlockSpec((1, WIDE, local), at(lambda j, g, p: (g, p, 0))),
             pl.BlockSpec((1, 1, 2, local), at(lambda j, g, p: (g, p, 0, 0))),
-            pl.BlockSpec((1, local, width), own_at(lambda g, p: (g, 0, 0))),
-            pl.BlockSpec((1, 1, local, width), rest_at(lambda j, g, p: (j, g, 0, 0))),
+            pl.BlockSpec((1, local, width), own_at(lambda g, p: (g, 0, 0)), pipeline_mode=once),
+            pl.BlockSpec(
+                (1, 1, local, width), rest_at(lambda j, g, p: (j, g, 0, 0)), pipeline_mode=once
+            ),
             still(width, 3 * width),
-            pl.BlockSpec((1, local, width), own_at(lambda g, p: (g, 0, 0))),
-        ],
+            pl.BlockSpec((1, local, width), own_at(lambda g, p: (g, 0, 0)), pipeline_mode=once),
+        ]
+        + [pl.BlockSpec(memory_space=pl.ANY)] * len(sums)
+        + [still(16, width)],
         out_specs=[
-            pl.BlockSpec((1, 1, local, width), rest_at(lambda j, g, p: (j, g, 0, 0))),
-            pl.BlockSpec((1, local, width), own_at(lambda g, p: (g, 0, 0))),
-            still(width, 3 * width),
-            still(8, width),
-        ],
-        out_shape=[
-            jax.ShapeDtypeStruct((parts - 1, groups, local, width), BF),
-            jax.ShapeDtypeStruct((groups, local, width), F32),
-            jax.ShapeDtypeStruct((width, 3 * width), F32),
-            jax.ShapeDtypeStruct((8, width), F32),
-        ],
+            pl.BlockSpec((1, local, width), own_at(lambda g, p: (g, 0, 0)), pipeline_mode=once),
+        ]
+        + [still(*shape) for shape in out_blocks],
+        out_shape=[jax.ShapeDtypeStruct((groups, local, width), F32)]
+        + [jax.ShapeDtypeStruct(shape, F32) for shape in out_blocks],
         scratch_shapes=[
             pltpu.VMEM((2, local, local), BF),
             pltpu.VMEM((local, 3 * WIDE), BF),
             pltpu.VMEM((local, width), F32),
             pltpu.VMEM((each, WIDE, local), F32),
             pltpu.VMEM((WIDE, local), F32),
-        ],
-        compiler_params=params(60, 1),
+            pltpu.VMEM((width, 3 * width), F32),
+            pltpu.VMEM((8, width), F32),
+            pltpu.VMEM((parts - 1, groups, local, width), BF),
+            pltpu.VMEM((parts - 1, groups, local, width), BF),
+            pltpu.SemaphoreType.DMA((parts - 1, groups)),
+            pltpu.SemaphoreType.DMA((parts - 1, groups)),
+        ]
+        + extra,
+        compiler_params=pltpu.CompilerParams(
+            vmem_limit_bytes=63 * MIB,
+            dimension_semantics=("arbitrary",),
+            collective_id=2,
+            has_side_effects=True,
+        ),
         name="pull",
-    )(e_all, query, pair_own, pair_rest, mixed_grad, mixed_t, inverse, own, rest, weight, partial)
+    )(
+        e_all,
+        query,
+        pair_own,
+        pair_rest,
+        mixed_grad,
+        mixed_t,
+        inverse,
+        own,
+        rest,
+        weight,
+        partial,
+        *sums,
+        vec_sums,
+    )
 
 
 def per_device(
@@ -763,7 +1059,7 @@
         (0, 0, 1),
     )
 
-    result, partial, mixed_grad, out_wg, up_wg, down_wg, row_sums, up_bias_sum = middle(
+    result, partial, mixed_grad, upper_sums, lower_sums, vec_sums = middle(
         tokens.reshape(rows, width),
         cotangent.reshape(rows, width),
         mixed.reshape(rows, width),
@@ -772,11 +1068,10 @@
         down_w,
         row_stack,
         up_b.reshape(1, -1),
+        devices,
     )
     mixed_grad = mixed_grad.reshape(groups, local, width)
-    out_sum, up_sum, down_sum = owner_sums([out_wg, up_wg, down_wg])
-
-    share_rest, input_grad, joint_wg, bias_grad = pull(
+    input_grad, joint, vec, *owned = pull(
         e_all,
         query,
         pair_own,
@@ -788,35 +1083,40 @@
         tokens_rest,
         joint_w,
         partial.reshape(groups, local, width),
+        upper_sums,
+        lower_sums,
+        vec_sums,
     )
-    for shift in range(1, parts):
-        piece = lax.ppermute(
-            share_rest[shift - 1], "seq", [(i, (i + shift) % parts) for i in range(parts)]
-        )
-        input_grad = input_grad + piece.astype(F32)
-
+    pieces = up_weight.shape[1] // width
+    if owned:
+        upper, lower = owned
+        out_sum = upper[:own_rows]
+        up_sum = upper[own_rows:].reshape(pieces, own_rows, width).transpose(1, 0, 2)
+        up_sum = up_sum.reshape(own_rows, pieces * width)
+        joint_sum = joint.reshape(3, own_rows, width).transpose(1, 0, 2)
+    else:
+        joint_sum, upper, lower = owner_sums([joint, upper_sums, lower_sums])
+        out_sum, up_sum = upper[:, :width], upper[:, width:]
+        vec = lax.psum(vec, ("dp", "seq"))
+    joint_sum = joint_sum.reshape(own_rows, PAIRS, 3, 2, HEAD).transpose(0, 1, 3, 2, 4)
+    joint_sum = joint_sum.reshape(own_rows, 3 * width)
     pair_grad = jnp.stack(
-        [bias_grad[0].reshape(H, HEAD), bias_grad[1].reshape(H, HEAD)], axis=1
+        [vec[12].reshape(H, HEAD), vec[13].reshape(H, HEAD)], axis=1
     ).reshape(2 * width)
+    device = lax.axis_index("dp") * parts + me
     sums = [
         pair_grad,
-        row_sums[0],
-        row_sums[1],
-        row_sums[2],
-        up_bias_sum[0],
-        row_sums[3],
-        row_sums[4],
-        row_sums[5],
+        vec[0],
+        vec[1],
+        vec[2],
+        vec[8 : 8 + pieces].reshape(-1),
+        vec[3],
+        vec[4],
+        vec[5],
     ]
-    vec = jnp.concatenate([s.reshape(devices, -1) for s in sums], axis=1)
-    joint_sum, vec = owner_sums([joint_wg, vec])
-    joint_sum = joint_sum.reshape(own_rows, PAIRS, 3, 2, HEAD).transpose(0, 1, 3, 2, 4)
-    joint_sum = joint_sum.reshape(own_rows, 3 * width)
-    vec = vec.reshape(-1)
-    small, at = [], 0
-    for size in lens:
-        small.append(vec[at : at + size])
-        at += size
+    small = [
+        lax.dynamic_slice_in_dim(v, device * size, size, 0) for v, size in zip(sums, lens)
+    ]
     return (
         result.reshape(groups, local, width),
         input_grad,
@@ -828,7 +1128,7 @@
         small[3],
         up_sum,
         small[4],
-        down_sum,
+        lower,
         small[5],
         small[6],
         small[7],

time: 442 us -> 364 us (0.82)
  waiting for transfers between devices: 85.5 us -> 0.01 us
  Pallas kernels: 285 us -> 325 us
  starting transfers between devices: 24 us -> 3.03 us
  other arithmetic: 18.7 us -> 5.2 us
    ppermute x26 -> x0, waiting for transfers between devices: 85.5 us -> none  [the longest x25 85.5 us: owner_sums(): arrived = [lax.ppermute(s, name, pairs) for s in sent]]
    pallas_call x2, Pallas kernels: 148 us -> 189 us  [the longest x1 138 us: pull(): pl.pallas_call(functools.partial(pull_kernel, parts, groups, orders, bits...]
    ppermute x26 -> x0, starting transfers between devices: 20.9 us -> none  [the longest x25 19.5 us: owner_sums(): arrived = [lax.ppermute(s, name, pairs) for s in sent]]
    add x26 -> x0, other arithmetic: 12.9 us -> none  [the longest x25 8.48 us: owner_sums(): arrays = [k + a.astype(F32) for k, a in zip(kept, arrived)]]
    convert_element_type x25 -> x0, local copies, waits for them, and re-layouts: 7.58 us -> none  [owner_sums(): lax.dynamic_index_in_dim(a, 1 - mine, axis, keepdims=False).astype(BF)]
    unnamed x58 -> x44, local copies, waits for them, and re-layouts: 8.34 us -> 14.3 us
  transfers between devices with their start and end apart: 27 -> 1, of which waited for: 18 -> 0; matrix products, arithmetic and copies ran while one was open for 6% -> 2% of each run, Pallas kernels for 37% -> 17%
where the time goes in v3:
time: 364 us; the launch traced here: 363 us
  Pallas kernels  325 us (89%)
  local copies, waits for them, and re-layouts  28.3 us (8%)
  other arithmetic  5.2 us (1%)
    pallas_call x1, Pallas kernels, pull(): pl.pallas_call(functools.partial(pull_kernel, parts, groups, orders, bits...  138 us
    pallas_call x1, Pallas kernels, attend(): pl.pallas_call(functools.partial(attend_kernel, parts, groups, steps, blo...  70.1 us
    pallas_call x1, Pallas kernels, gather_weights(): pl.pallas_call(functools.partial(gather_kernel, orders, bits_dp, bits_seq...  57.5 us
    pallas_call x1, Pallas kernels, middle(): pl.pallas_call(functools.partial(middle_kernel, packed), grid=(count // b...  50.7 us
    unnamed x44, local copies, waits for them, and re-layouts  14.3 us
    pallas_call x2, Pallas kernels, project(): pl.pallas_call(functools.partial(project_kernel, own), grid=(count // blo...  9.34 us
  transfers between devices with their start and end apart: 1, of which 0 were waited for; matrix products, arithmetic and copies ran while one was open for 2% of the time, Pallas kernels for 17%

profile of v3, /device:TPU:0, one launch (start us, length us, event | category | flops | bytes accessed | tf_op | source)
XLA Modules:
  0.0 363.0 jit_solution(8896274890237786021)
XLA Ops:
  0.8 2.6 convert_element_type.47.refs_7_
  3.4 3.0 collective-permute-start
  6.7 0.8 reshape.120.refs_0_
  8.3 57.5 %gather_weights.1 = (bf16[2,2,2,2,2,16,1536]{6,5,4,3,2,1,0:T(8,128)(2,1)}, bf16[2,2,2,2,2,16,256]{6,5,4,3,2,1,0:T(8,128)(2,1)}) custom-call(bf16[16,1536]{1,0:T(8,128)(2,1)} %reshape.120.refs_0_, bf16[16,256]{1,0:T(8,128)(2,1)} %broadcast_in_dim.2.refs_1_), custom_call_target="tpu_custom_call" | custom-call | tf_op jit(solution)/shard_map/gather_weights/pallas_call | solution.py:131
  65.8 0.9 slice.88
  69.6 0.7 reshape_reshape.11.up_bias
  70.3 1.4 copy-done.3
  71.7 5.1 %project_own.1 = (bf16[2048,512]{1,0:T(8,128)(2,1)S(1)}, bf16[2048,1024]{1,0:T(8,128)(2,1)S(1)}) custom-call(bf16[2048,512]{1,0:T(8,128)(2,1)S(1)} %bitcast.65, bf16[512,1536]{1,0:T(8,128)(2,1)S(1)} %bitcast.67, f32[1,1536]{1,0:T(1,128)S(1)} %reshape.122.bias), custom_call_target="tpu_custom_call" | custom-call | tf_op jit(solution)/shard_map/project_own/pallas_call | solution.py:261
  76.8 2.0 copy-done.1
  78.8 1.4 copy-done.5
  81.4 1.4 copy-done.4
  82.8 4.3 %project_rest.1 = bf16[2048,1024]{1,0:T(8,128)(2,1)S(1)} custom-call(bf16[2048,512]{1,0:T(8,128)(2,1)} %bitcast.11.tokens, bf16[512,1536]{1,0:T(8,128)(2,1)S(1)} %bitcast.68, f32[1,1536]{1,0:T(1,128)S(1)} %reshape.122.bias), custom_call_target="tpu_custom_call" | custom-call | tf_op jit(solution)/shard_map/project_rest/pallas_call | solution.py:261
  87.1 2.0 copy-done
  89.1 70.1 %attend.1 = (bf16[2,2,8,1024,1024]{4,3,2,1,0:T(8,128)(2,1)}, bf16[2,1024,512]{2,1,0:T(8,128)(2,1)}, bf16[2,512,1024]{2,1,0:T(8,128)(2,1)}, f32[2,4,2,1024]{3,2,1...) custom-call(s32[4]{0:T(128)} %pad_add_fusion.refs_0_, ...), custom_call_target="tpu_custom_call" | custom-call | tf_op jit(solution)/shard_map/attend/pallas_call | solution.py:388
  159.2 50.7 %middle.1 = (f32[2048,512]{1,0:T(8,128)}, f32[2048,512]{1,0:T(8,128)}, bf16[2048,512]{1,0:T(8,128)(2,1)}, bf16[32,80,512]{2,1,0:T(8,128)(2,1)}, bf16[32,64,512]{2,1,0:T(8,128)(2,1)}, /*index=5*/f32[16,512]{1,0:T(8,128)}) custom-call(f32[2048,512]{1,0:T(8,128)} %bitcast.71, f32[2048,512]{1,0:T(8,128)} %bitcast.73, bf16[2048,512]{1,0:T(8,128)(2,1)} %bitcast.77, ...), custom_call_target="tpu_custom_call" | custom-call | tf_op jit(solution)/shard_map/middle/pallas_call | solution.py:572
  210.0 137.8 %pull.1 = (f32[2,1024,512]{2,1,0:T(8,128)}, f32[48,512]{1,0:T(8,128)}, f32[16,512]{1,0:T(8,128)}, f32[80,512]{1,0:T(8,128)}, f32[64,512]{1,0:T(8,128)}) custom-call(bf16[2,2,8,1024,1024]{4,3,2,1,0:T(8,128)(2,1)} %get-tuple-element.45.refs_0_, bf16[2,1024,512]{2,1,0:T(8,128)(2,1)} %bitcast.70, bf16[2,1024,1024]{2,1,0:T(8,128)(2,1)} %bitcast.64, ...), custom_call_target="tpu_custom_call" | custom-call | tf_op jit(solution)/shard_map/pull/pallas_call | solution.py:915
  347.8 1.0 fusion.9
  348.8 0.7 slice_bitcast_fusion
  349.5 0.9 slice.83
  350.4 1.4 slice.79
  352.0 1.0 copy.52
  353.2 0.8 reshape.137
  354.1 0.7 copy.46
  357.7 4.7 %copy.55 = f32[2,1024,512]{2,1,0:T(8,128)} copy(f32[2,1024,512]{2,1,0:T(8,128)} %get-tuple-element.97) | data formatting | bytes 8388608
  (85 shorter events, 9.2 us)
Async XLA Ops:
  0.6 5.8 %copy-start.9 = (f32[16,1536]{1,0:T(8,128)S(1)}, f32[16,1536]{1,0:T(8,128)}, u32[]{:S(2)}) copy-start(f32[16,1536]{1,0:T(8,128)} %param.17) | copy-start | bytes 294916
  0.7 6.8 %copy-start.11 = (f32[32]{0:T(128)S(1)}, f32[32]{0:T(128)}, u32[]{:S(2)}) copy-start(f32[32]{0:T(128)} %param.18) | copy-start | bytes 388
  0.7 6.8 %copy-start.12 = (f32[16]{0:T(128)S(1)}, f32[16]{0:T(128)}, u32[]{:S(2)}) copy-start(f32[16]{0:T(128)} %param.20) | copy-start | bytes 196
  0.7 6.8 %copy-start.13 = (f32[16]{0:T(128)S(1)}, f32[16]{0:T(128)}, u32[]{:S(2)}) copy-start(f32[16]{0:T(128)} %param.21) | copy-start | bytes 196
  0.7 6.8 %copy-start.14 = (f32[16]{0:T(128)S(1)}, f32[16]{0:T(128)}, u32[]{:S(2)}) copy-start(f32[16]{0:T(128)} %param.22) | copy-start | bytes 196
  0.7 6.8 %copy-start.15 = (f32[64]{0:T(128)S(1)}, f32[64]{0:T(128)}, u32[]{:S(2)}) copy-start(f32[64]{0:T(128)} %param.24) | copy-start | bytes 772
  0.7 6.8 %copy-start.16 = (f32[16]{0:T(128)S(1)}, f32[16]{0:T(128)}, u32[]{:S(2)}) copy-start(f32[16]{0:T(128)} %param.26) | copy-start | bytes 196
  0.7 6.8 %copy-start.17 = (f32[16]{0:T(128)S(1)}, f32[16]{0:T(128)}, u32[]{:S(2)}) copy-start(f32[16]{0:T(128)} %param.27) | copy-start | bytes 196
  0.7 6.8 %copy-start.18 = (f32[16]{0:T(128)S(1)}, f32[16]{0:T(128)}, u32[]{:S(2)}) copy-start(f32[16]{0:T(128)} %param.28) | copy-start | bytes 196
  0.7 66.4 %copy-start.6 = (f32[16,2048]{1,0:T(8,128)S(1)}, f32[16,2048]{1,0:T(8,128)}, u32[]{:S(2)}) copy-start(f32[16,2048]{1,0:T(8,128)} %param.23) | copy-start | bytes 393220
  0.7 67.0 %copy-start.7 = (f32[64,512]{1,0:T(8,128)S(1)}, f32[64,512]{1,0:T(8,128)}, u32[]{:S(2)}) copy-start(f32[64,512]{1,0:T(8,128)} %param.25) | copy-start | bytes 393220
  0.8 67.7 %copy-start.10 = (f32[16,512]{1,0:T(8,128)S(1)}, f32[16,512]{1,0:T(8,128)}, u32[]{:S(2)}) copy-start(f32[16,512]{1,0:T(8,128)} %param.19) | copy-start | bytes 98308
  3.4 73.4 %copy-start.2 = (bf16[2,1024,512]{2,1,0:T(8,128)(2,1)}, bf16[2,1024,512]{2,1,0:T(8,128)(2,1)S(1)}, u32[]{:S(2)}) copy-start(bf16[2,1024,512]{2,1,0:T(8,128)(2,1)S(1)} %convert_element_type.47.refs_7_) | copy-start | bytes 6291460
  3.4 78.0 %collective-permute-start = (bf16[2,1024,512]{2,1,0:T(8,128)(2,1)S(1)}, bf16[2,1024,512]{2,1,0:T(8,128)(2,1)}, u32[]{:S(2)}, u32[]{:S(2)}) collective-permute-start(bf16[2,1024,512]{2,1,0:T(8,128)(2,1)S(1)} %convert_element_type.47.refs_7_), channel_id=1, source_target_pairs={{0,1},{1,0},{2,3},{3,2},{4,5},{5,4},{6,7},{7,6},{8,9},{9,8},{10,11... | collective-permute-start | bytes 6291464 | tf_op jit(solution)/shard_map/ppermute | solution.py:1004
  6.6 74.2 %copy-start.19 = (s32[2]{0:T(128)S(1)}, s32[2]{0:T(128)}, u32[]{:S(2)}) copy-start(s32[2]{0:T(128)} %param.16) | copy-start | bytes 28
  70.3 1.4 copy-start.3
  76.8 2.0 copy-start.1
  78.8 1.4 copy-start.5
  81.4 1.4 copy-start.4
  87.1 2.0 copy-start
  357.7 4.7 %copy-start.8 = (f32[64,512]{1,0:T(8,128)S(1)}, f32[64,512]{1,0:T(8,128)}, u32[]{:S(2)}) copy-start(f32[64,512]{1,0:T(8,128)} %get-tuple-element.106) | copy-start | bytes 393220

commit v4 on v3

v4 whole, which is shorter than its diff:
```python
import functools
import math

import jax
import jax.numpy as jnp
from jax import lax
from jax.experimental import pallas as pl
from jax.experimental.pallas import tpu as pltpu
from jax.sharding import PartitionSpec as P

H = 8
HEAD = 64
PAIRS = H // 2
WIDE = 2 * HEAD
BF = jnp.bfloat16
F32 = jnp.float32
EPS = 1e-05
SCALE = 1.0 / math.sqrt(HEAD)
LOG2E = math.log2(math.e)
GELU_A = math.sqrt(2.0 / math.pi)
GELU_B = 0.044715
MESH = pl.DeviceIdType.MESH
MIB = 2**20
FORMS = {
    "nn": (((1,), (0,)), ((), ())),
    "nt": (((1,), (1,)), ((), ())),
    "tn": (((0,), (0,)), ((), ())),
}


def dot(left, right, form="nn"):
    return lax.dot_general(left, right, FORMS[form], preferred_element_type=F32)


def whole_tiles(width, devices):
    return width // devices % 16 == 0


def params(limit, steps):
    return pltpu.CompilerParams(
        vmem_limit_bytes=limit * MIB, dimension_semantics=("arbitrary",) * steps
    )


def log2(size):
    return size.bit_length() - 1


class Net:
    def __init__(self, bits_dp, bits_seq):
        self.bits_dp, self.bits_seq = bits_dp, bits_seq
        self.bits = bits_dp + bits_seq
        self.dp, self.seq = lax.axis_index("dp"), lax.axis_index("seq")
        self.mine = [lax.rem(self.dp // 2 ** (bits_dp - 1 - b), 2) for b in range(bits_dp)]
        self.mine += [lax.rem(self.seq // 2 ** (bits_seq - 1 - b), 2) for b in range(bits_seq)]

    def partner(self, flips):
        dp, seq = self.dp, self.seq
        for bit in flips:
            turn = 1 - 2 * self.mine[bit]
            if bit < self.bits_dp:
                dp = dp + turn * 2 ** (self.bits_dp - 1 - bit)
            else:
                seq = seq + turn * 2 ** (self.bits - 1 - bit)
        return (dp, seq)

    def place(self, done, turned=()):
        at = []
        for bit in range(self.bits):
            if bit in done:
                at.append(slice(None))
            else:
                at.append(1 - self.mine[bit] if bit in turned else self.mine[bit])
        return tuple(at)

    def signal(self, device):
        pl.semaphore_signal(
            pltpu.get_barrier_semaphore(), inc=1, device_id=device, device_id_type=MESH
        )

    def greet(self, groups):
        count = 0
        for group in groups:
            for flips in subsets(group):
                self.signal(self.partner(flips))
                count += 1
        return count


def subsets(group):
    return [
        tuple(b for i, b in enumerate(group) if pick >> i & 1)
        for pick in range(1, 2 ** len(group))
    ]


def stages_of(bits_dp, bits_seq):
    bits = bits_dp + bits_seq

    def twos(numbers):
        return [tuple(numbers[i : i + 2]) for i in range(0, len(numbers), 2)]

    beside = twos(list(range(bits_dp, bits)))
    upper = twos(list(range(bits_dp - 2)))
    return beside, upper, [(bits_dp - 2,)], [(bits_dp - 1,)]


def mesh_bits():
    return log2(lax.axis_size("dp")), log2(lax.axis_size("seq"))


class Links:
    def __init__(self, net, send_sem, recv_sem):
        self.net, self.send_sem, self.recv_sem, self.used = net, send_sem, recv_sem, 0

    def copy(self, source, target, device):
        at = self.used
        self.used += 1
        return pltpu.make_async_remote_copy(
            src_ref=source,
            dst_ref=target,
            send_sem=self.send_sem.at[at],
            recv_sem=self.recv_sem.at[at],
            device_id=device,
            device_id_type=MESH,
        )

    def spread(self, full, done, group):
        place = self.net.place(done)
        return [
            self.copy(full.at[place], full.at[place], self.net.partner(flips))
            for flips in subsets(group)
        ]


def start(copies):
    for copy in copies:
        copy.start()


def wait(copies):
    for copy in copies:
        copy.wait()


def flat(groups):
    return tuple(b for group in groups for b in group)


def ring(net, parts, other):
    return (net.dp, lax.rem(net.seq + parts - other, parts))


def owned_row(vector, row, device):
    size, width = vector.shape[1], H * HEAD
    shift = log2(size)
    entry = lax.broadcasted_iota(jnp.int32, (size, width), 0)
    column = lax.broadcasted_iota(jnp.int32, (size, width), 1) + row * width
    here = (column >> shift == device) & (column & (size - 1) == entry)
    return dot(vector.astype(BF), here.astype(F32).astype(BF))


def owned_pair(vector, row, device):
    size, width = vector.shape[1], H * HEAD
    shift = log2(size)
    entry = lax.broadcasted_iota(jnp.int32, (size, width), 0)
    column = lax.broadcasted_iota(jnp.int32, (1, width), 1) + row * width
    pair = column * 0
    for p in range(1, PAIRS):
        pair += (column >= 3 * WIDE * p).astype(jnp.int32)
    inside = column - 3 * WIDE * pair
    kind = inside >> log2(WIDE)
    head = 2 * pair + (inside >> log2(HEAD) & 1)
    index = (2 * head + (kind >> 1)) * HEAD + (inside & (HEAD - 1))
    index = jnp.where(kind == 1, -1, index)
    here = (index >> shift == device) & (index & (size - 1) == entry)
    return dot(vector.astype(BF), here.astype(F32).astype(BF))


def begin_kernel(bits_dp, bits_seq, parts, packed, *refs):
    (
        tokens,
        joint_wide,
        up_wide,
        down_wide,
        out_wide,
        pair_bias,
        out_bias,
        gain_one,
        shift_one,
        up_bias,
        down_bias,
        gain_two,
        shift_two,
        tokens_low,
        tokens_rest,
        joint_out,
        vec,
        up_w,
        down_w,
        out_w,
        query,
        pair_own,
        wide,
        narrow,
        joint_here,
        joint_shard,
        up_shard,
        down_shard,
        out_shard,
        vec_sent,
        vec_landing,
        query_here,
        pair_here,
        own_sem,
        send_sem,
        recv_sem,
    ) = refs
    joint_w = joint_here if packed else joint_out
    net = Net(bits_dp, bits_seq)
    links = Links(net, send_sem, recv_sem)
    beside, upper, next_to, cores = stages_of(bits_dp, bits_seq)
    order = beside + upper + next_to + cores
    groups, local, width = tokens.shape
    due = net.greet(order)
    for other in range(1, parts):
        net.signal(ring(net, parts, other))
        due += 1
    loads = [
        pltpu.make_async_copy(tokens.at[g], wide.at[g], own_sem.at[g]) for g in range(groups)
    ]
    stores = [
        pltpu.make_async_copy(narrow.at[g], tokens_low.at[g], own_sem.at[groups + g])
        for g in range(groups)
    ]
    mine = net.place(())
    placed = [
        pltpu.make_async_copy(shard, full.at[mine], own_sem.at[2 * groups + i])
        for i, (shard, full) in enumerate(
            ((joint_shard, joint_w), (up_shard, up_w), (down_shard, down_w), (out_shard, out_w))
        )
    ]
    start(loads)
    joint = joint_wide[...]
    turned = []
    for head in range(0, H, 2):
        for kind in range(3):
            for at in (head, head + 1):
                turned.append(joint[:, (3 * at + kind) * HEAD : (3 * at + kind + 1) * HEAD])
    joint_shard[...] = jnp.concatenate(turned, axis=1).astype(BF)
    start(placed[:1])
    up_shard[...] = up_wide[...].astype(BF)
    down_shard[...] = down_wide[...].astype(BF)
    out_shard[...] = out_wide[...].astype(BF)
    start(placed[1:])
    device = net.dp * parts + net.seq
    vec[...] = jnp.zeros_like(vec)
    lines = (out_bias, gain_one, shift_one, down_bias, gain_two, shift_two)
    for row, vector in enumerate(lines):
        vec[row : row + 1] = owned_row(vector[...], 0, device)
    for row in range(4):
        vec[6 + row : 7 + row] = owned_row(up_bias[...], row, device)
    for row in range(3):
        vec[10 + row : 11 + row] = owned_pair(pair_bias[...], row, device)
    wait(placed)
    pl.semaphore_wait(pltpu.get_barrier_semaphore(), due)

    def narrowed(g):
        wait(loads[g : g + 1])
        narrow[g] = wide[g].astype(BF)
        start(stores[g : g + 1])

    late = []
    exchange = []
    for stage, group in enumerate(order):
        done = flat(order[:stage])
        joint = links.spread(joint_w, done, group)
        vec_sent[stage] = vec[...]
        small = [
            links.copy(vec_sent.at[stage], vec_landing.at[stage, i], net.partner(flips))
            for i, flips in enumerate(subsets(group))
        ]
        start(joint)
        start(small)
        if stage < len(beside):
            rest = [links.spread(full, done, group) for full in (up_w, down_w, out_w)]
            for copies in rest:
                start(copies)
        if stage == len(beside) - 1:
            narrowed(0)
            exchange = [
                links.copy(narrow.at[0], tokens_rest.at[other - 1, 0], ring(net, parts, other))
                for other in range(1, parts)
            ]
            start(exchange)
        elif stage == len(beside):
            for g in range(1, groups):
                narrowed(g)
        wait(joint)
        wait(small)
        for i in range(len(small)):
            vec[...] += vec_landing[stage, i]
        if stage < len(beside):
            for copies in rest:
                wait(copies)
        elif stage < len(beside) + len(upper):
            wait(late)
            late = links.spread(up_w, done, group)
            start(late)
    wait(late)
    if packed:
        whole = pltpu.make_async_copy(joint_here, joint_out, own_sem.at[4 * groups + 4])
        whole.start()
        weight = joint_w.shape[-1]
        bias = jnp.concatenate([vec[10 + i : 11 + i] for i in range(3)], axis=1)
        block = min(256, local)
        results = []
        for g in range(groups):

            def rows_of(b, carry):
                rows = pl.ds(pl.multiple_of(b * block, block), block)
                full = joint_w[...].reshape(width, weight)
                joint = (dot(narrow[g, rows], full) + bias).astype(BF)
                for p in range(PAIRS):
                    at = 3 * WIDE * p
                    query_here[g, rows, p * WIDE : (p + 1) * WIDE] = joint[:, at : at + WIDE]
                    pair_here[g, rows, 2 * p * WIDE : 2 * (p + 1) * WIDE] = joint[
                        :, at + WIDE : at + 3 * WIDE
                    ]
                return carry

            lax.fori_loop(0, local // block, rows_of, 0)
            results.append(
                pltpu.make_async_copy(query_here.at[g], query.at[g], own_sem.at[2 * groups + 4 + g])
            )
            results.append(
                pltpu.make_async_copy(
                    pair_here.at[g], pair_own.at[g], own_sem.at[3 * groups + 4 + g]
                )
            )
            start(results[-2:])
        wait(results)
        whole.wait()
    wait(exchange)
    wait(stores)


def begin(tokens, joint, up, down, out, vectors, parts):
    bits_dp, bits_seq = mesh_bits()
    bits = bits_dp + bits_seq
    groups, local, width = tokens.shape
    packed = joint.shape[0] % 16 == 0
    beside, upper, next_to, cores = stages_of(bits_dp, bits_seq)
    order = beside + upper + next_to + cores
    sends = sum(2 ** len(group) - 1 for group in order)
    copies = 2 * sends + 4 * sends + parts
    split = (2,) * bits
    hbm = pl.BlockSpec(memory_space=pl.ANY)
    vmem = pl.BlockSpec(memory_space=pltpu.VMEM)
    return pl.pallas_call(
        functools.partial(begin_kernel, bits_dp, bits_seq, parts, packed),
        in_specs=[hbm] + [vmem] * (4 + len(vectors)),
        out_specs=[hbm, hbm, hbm, vmem] + [hbm] * 5,
        out_shape=[
            jax.ShapeDtypeStruct((groups, local, width), BF),
            jax.ShapeDtypeStruct((parts - 1, groups, local, width), BF),
            jax.ShapeDtypeStruct(split + joint.shape, BF),
            jax.ShapeDtypeStruct((16, width), F32),
            jax.ShapeDtypeStruct(split + up.shape, BF),
            jax.ShapeDtypeStruct(split + down.shape, BF),
            jax.ShapeDtypeStruct(split + out.shape, BF),
            jax.ShapeDtypeStruct((groups, local, width), BF),
            jax.ShapeDtypeStruct((groups, local, 2 * width), BF),
        ],
        scratch_shapes=[
            pltpu.VMEM((groups, local, width), F32),
            pltpu.VMEM((groups, local, width), BF),
            pltpu.VMEM(split + joint.shape if packed else (16, 128), BF),
            pltpu.VMEM(joint.shape, BF),
            pltpu.VMEM(up.shape, BF),
            pltpu.VMEM(down.shape, BF),
            pltpu.VMEM(out.shape, BF),
            pltpu.VMEM((len(order), 16, width), F32),
            pltpu.VMEM((len(order), 3, 16, width), F32),
            pltpu.VMEM((groups, local, width), BF),
            pltpu.VMEM((groups, local, 2 * width), BF),
            pltpu.SemaphoreType.DMA((4 * groups + 5,)),
            pltpu.SemaphoreType.DMA((copies,)),
            pltpu.SemaphoreType.DMA((copies,)),
        ],
        compiler_params=pltpu.CompilerParams(
            vmem_limit_bytes=62 * MIB, collective_id=0, has_side_effects=True
        ),
        name="begin",
    )(tokens, joint, up, down, out, *vectors)


def matrix_of(full):
    return full.reshape((-1,) + full.shape[-1:])


def owner_sums(arrays):
    size_dp, size_seq = lax.axis_size("dp"), lax.axis_size("seq")
    bits_dp, bits_seq = log2(size_dp), log2(size_seq)
    bits = bits_dp + bits_seq
    dp, seq = lax.axis_index("dp"), lax.axis_index("seq")
    arrays = [a.reshape((2,) * bits + (-1,) + a.shape[1:]) for a in arrays]
    left = list(range(bits))
    for bit in [bits_dp - 1] + list(range(bits_dp, bits)) + list(range(bits_dp - 2, -1, -1)):
        axis = left.index(bit)
        left.remove(bit)
        if bit < bits_dp:
            name, size, step, me = "dp", size_dp, 2 ** (bits_dp - 1 - bit), dp
        else:
            name, size, step, me = "seq", size_seq, 2 ** (bits - 1 - bit), seq
        mine = me // step % 2
        pairs = [(i, i ^ step) for i in range(size)]
        sent = [
            lax.dynamic_index_in_dim(a, 1 - mine, axis, keepdims=False).astype(BF) for a in arrays
        ]
        kept = [lax.dynamic_index_in_dim(a, mine, axis, keepdims=False) for a in arrays]
        arrived = [lax.ppermute(v, name, pairs) for v in sent]
        arrays = [k + a.astype(F32) for k, a in zip(kept, arrived)]
    return arrays


class Halving:
    def __init__(self, net, links, groups, held, landing, source=None):
        self.net, self.groups, self.held, self.landing = net, groups, held, landing
        self.gone = groups[0] if source is not None else ()
        self.rounds = []
        for stage, group in enumerate(groups):
            copies = []
            for i, flips in enumerate(subsets(group)):
                at = self.place(stage, flips)
                part = source.at[at] if stage == 0 and source is not None else held.at[self.cut(at)]
                copies.append(links.copy(part, landing[stage].at[i], net.partner(flips)))
            self.rounds.append(copies)

    def place(self, stage, turned):
        done, group = flat(self.groups[:stage]), self.groups[stage]
        at = []
        for bit, mine in enumerate(self.net.mine):
            if bit in done or bit in group:
                at.append(1 - mine if bit in turned else mine)
            else:
                at.append(slice(None))
        return tuple(at)

    def cut(self, at):
        return tuple(a for bit, a in enumerate(at) if bit not in self.gone)

    def start(self, stage):
        start(self.rounds[stage])

    def add(self, stage, out=None):
        wait(self.rounds[stage])
        at = self.cut(self.place(stage, ()))
        free = [i for i, a in enumerate(at) if isinstance(a, slice)]
        landing = self.landing[stage]

        def one(flat_index, carry):
            inner = [lax.rem(flat_index // 2 ** (len(free) - 1 - i), 2) for i in range(len(free))]
            there = list(at)
            for axis, value in zip(free, inner):
                there[axis] = value
            there = tuple(there)
            value = self.held[there].astype(F32)
            for i in range(landing.shape[0]):
                value += landing[(i,) + tuple(inner)].astype(F32)
            if out is None:
                self.held[there] = value.astype(BF)
            else:
                out[...] = value
            return carry

        if free:
            lax.fori_loop(0, 2 ** len(free), one, 0)
        else:
            one(0, 0)


class Everywhere:
    def __init__(self, net, links, groups, value, sent, landing):
        self.value, self.sent, self.landing = value, sent, landing
        self.rounds = [
            [
                links.copy(sent.at[stage], landing.at[stage, i], net.partner(flips))
                for i, flips in enumerate(subsets(group))
            ]
            for stage, group in enumerate(groups)
        ]

    def start(self, stage):
        self.sent[stage] = self.value[...]
        start(self.rounds[stage])

    def add(self, stage, out=None):
        wait(self.rounds[stage])
        for i in range(len(self.rounds[stage])):
            self.value[...] += self.landing[stage, i]


def landing_shapes(groups, bits, rows, width):
    shapes, left = [], bits
    for group in groups:
        left -= len(group)
        shapes.append(pltpu.VMEM((2 ** len(group) - 1,) + (2,) * left + (rows, width), BF))
    return shapes


def sum_orders(bits_dp, bits_seq):
    beside, upper, next_to, cores = stages_of(bits_dp, bits_seq)
    far = upper[::-1]
    if len(beside) == 1 and len(beside[0]) == 1:
        near = [beside[0] + next_to[0]]
    else:
        near = beside + next_to
    return cores + beside + next_to + far, cores + next_to + beside + far, cores + near + far


def project_kernel(tokens, weight, bias, query, pair):
    x = tokens[...]
    for p in range(PAIRS):
        columns = slice(3 * WIDE * p, 3 * WIDE * (p + 1))
        joint = (dot(x, weight[:, columns]) + bias[:, columns]).astype(BF)
        query[:, p * WIDE : (p + 1) * WIDE] = joint[:, :WIDE]
        pair[:, 2 * p * WIDE : 2 * (p + 1) * WIDE] = joint[:, WIDE:]


def project(tokens, weight, bias):
    count, width = tokens.shape
    block = min(512, count)

    def moving(columns):
        return pl.BlockSpec((block, columns), lambda b: (b, 0))

    def still(*shape):
        return pl.BlockSpec(shape, lambda b: (0, 0), pipeline_mode=pl.Buffered(1))

    return pl.pallas_call(
        project_kernel,
        grid=(count // block,),
        in_specs=[moving(width), still(width, 3 * width), still(1, 3 * width)],
        out_specs=[moving(width), moving(2 * width)],
        out_shape=[
            jax.ShapeDtypeStruct((count, width), BF),
            jax.ShapeDtypeStruct((count, 2 * width), BF),
        ],
        compiler_params=params(40, 1),
        name="project",
    )(tokens, weight, bias)


def attend_kernel(parts, groups, steps, blocks, bits_dp, bits_seq, *refs):
    (
        lengths,
        query,
        keys_own,
        values_own,
        weight,
        vec,
        tokens_low,
        _,
        _,
        _,
        _,
        e_out,
        mixed,
        mixed_t,
        inverse,
        pair_rest,
        tokens_rest,
        up_w,
        down_w,
        out_w,
        k_ext,
        v_ext,
        kept,
        tops,
        rest_here,
        pair_here,
        own_sem,
        send_sem,
        recv_sem,
    ) = refs
    local = keys_own.shape[1]
    block = query.shape[1]
    step = pl.program_id(0)
    chunk = min(256, local)

    net = Net(bits_dp, bits_seq)
    links = Links(net, send_sem, recv_sem)
    beside, upper, next_to, cores = stages_of(bits_dp, bits_seq)
    order = beside + upper + next_to + cores
    first, last = len(beside), len(order)
    lead = len(upper)
    rounds = []
    for stage in range(first, last):
        copies = []
        for full in (down_w, out_w):
            copies += links.spread(full, flat(order[:stage]), order[stage])
        ahead = stage + lead
        if ahead < last:
            copies += links.spread(up_w, flat(order[:ahead]), order[ahead])
        rounds.append(copies)
    times = [0, 7, 12, 14, 15, 16]
    if len(rounds) > 3:
        times = [i * steps // (len(rounds) + 1) for i in range(len(rounds) + 1)]
    else:
        times = [0, steps * 7 // 16, steps * 12 // 16, steps * 14 // 16]
    exchange = [
        [
            links.copy(
                tokens_low.at[g], tokens_rest.at[other - 1, g], ring(net, parts, other)
            )
            for other in range(1, parts)
        ]
        for g in range(1, groups)
    ]

    @pl.when(step == 0)
    def enter():
        due = net.greet(order[first:])
        for other in range(1, parts):
            net.signal(ring(net, parts, other))
            due += 1
        pl.semaphore_wait(pltpu.get_barrier_semaphore(), due)
        for copies in exchange:
            start(copies)
        start(rounds[0])

    for i in range(len(rounds)):
        @pl.when(step == times[i + 1])
        def advance():
            wait(rounds[i])
            if i + 1 < len(rounds):
                start(rounds[i + 1])

    @pl.when(step % blocks == 1 % blocks)
    def prepare_values():
        for part in range(parts):
            rows = slice(part * local, (part + 1) * local)
            values = values_own[0] if part == 0 else pair_here[part - 1, :, WIDE:]
            turned = values.T
            v_ext[0, :HEAD, rows] = turned[:HEAD]
            v_ext[1, :HEAD, rows] = turned[HEAD:]
            v_ext[:, HEAD:, rows] = jnp.ones((2, HEAD, local), BF)

    for group in range(groups):
        @pl.when(step == group * blocks * PAIRS)
        def fetch():
            if group > 0:
                wait(exchange[group - 1])
            copy = pltpu.make_async_copy(tokens_rest.at[:, group], rest_here, own_sem.at[group])
            copy.start()
            copy.wait()

    @pl.when(jnp.logical_and(step % blocks == 0, step < steps))
    def prepare_keys():
        pair = lax.rem(step // blocks, PAIRS)
        columns = pl.ds(pl.multiple_of(pair * (3 * WIDE) + WIDE, WIDE), 2 * WIDE)
        bias = jnp.zeros((1, 2 * WIDE), F32)
        flat_bias = jnp.concatenate([vec[10 + i : 11 + i] for i in range(3)], axis=1)
        for p in range(PAIRS):
            at = 3 * WIDE * p + WIDE
            bias = jnp.where(pair == p, flat_bias[:, at : at + 2 * WIDE], bias)
        for part in range(1, parts):
            both = (dot(rest_here[part - 1], weight[:, columns]) + bias).astype(BF)
            pair_here[part - 1] = both
            pair_rest[part - 1, 0] = both
        for group in range(groups):
            @pl.when(step // (blocks * PAIRS) == group)
            def fill():
                length = lengths[group]
                for part in range(parts):
                    rows = slice(part * local, (part + 1) * local)
                    k_ext[rows, :WIDE] = keys_own[0] if part == 0 else pair_here[part - 1, :, :WIDE]
                    first_key = lax.rem(net.seq + part, parts) * local
                    place = lax.broadcasted_iota(jnp.int32, (local, WIDE), 0) + first_key
                    k_ext[rows, WIDE:] = jnp.where(place < length, 0.0, -1e30).astype(BF)

    turned = query[0].T
    zero = jnp.zeros((HEAD, block), BF)
    one = (lax.broadcasted_iota(jnp.int32, (WIDE, block), 0) == 0).astype(F32).astype(BF)
    heads = []
    for head in range(2):
        if head == 0:
            picked = jnp.concatenate([turned[:HEAD], zero, one], axis=0)
        else:
            picked = jnp.concatenate([zero, turned[HEAD:], one], axis=0)
        top = tops[head : head + 1]
        out = None
        largest = None
        for at in range(0, parts * local, chunk):
            rows = slice(at, at + chunk)
            inside = slice(at % local, at % local + chunk)
            e = jnp.exp2((kept[head, rows] - top) * (SCALE * LOG2E)).astype(BF)
            e_out[at // local, 0, head, inside] = e
            add = dot(v_ext[head, :, rows], e)
            out = add if out is None else out + add
            scores = dot(k_ext[rows], picked)
            kept[head, rows] = scores
            most = jnp.max(scores.reshape(chunk // 8, 8, block), axis=0)
            largest = most if largest is None else jnp.maximum(largest, most)
        tops[head : head + 1] = jnp.max(largest, axis=0, keepdims=True)
        inv = 1.0 / out[HEAD : HEAD + 1]
        inverse[0, 0, head : head + 1] = inv
        heads.append(out[:HEAD] * inv)
    both = jnp.concatenate(heads, axis=0).astype(BF)
    mixed_t[0] = both
    mixed[0] = both.T


def attend(lengths, query, pair_own, weight, vec, tokens_low, tokens_rest, up_w, down_w, out_w):
    groups, local, width = query.shape
    others = tokens_rest.shape[0]
    parts = others + 1
    block = min(512, local)
    blocks = local // block
    steps = groups * PAIRS * blocks
    bits_dp, bits_seq = mesh_bits()
    beside, upper, next_to, cores = stages_of(bits_dp, bits_seq)
    sends = sum(2 ** len(group) - 1 for group in upper + next_to + cores)
    copies = 3 * sends + groups * others

    def decode(t, place):
        return place(t // (PAIRS * blocks), t // blocks % PAIRS, t % blocks)

    def now(place):
        return lambda t: decode(jnp.minimum(t, steps - 1), place)

    def before(place):
        return lambda t: decode(jnp.maximum(t - 1, 0), place)

    def still(*shape):
        return pl.BlockSpec(shape, lambda t: (0,) * len(shape), pipeline_mode=pl.Buffered(1))

    hbm = pl.BlockSpec(memory_space=pl.ANY)
    passed = (tokens_rest, up_w, down_w, out_w)
    return pl.pallas_call(
        functools.partial(attend_kernel, parts, groups, steps, blocks, bits_dp, bits_seq),
        grid=(steps + 1,),
        in_specs=[
            pl.BlockSpec(memory_space=pltpu.SMEM),
            pl.BlockSpec((1, block, WIDE), now(lambda g, p, b: (g, b, p))),
            pl.BlockSpec((1, local, WIDE), now(lambda g, p, b: (g, 0, 2 * p))),
            pl.BlockSpec((1, local, WIDE), before(lambda g, p, b: (g, 0, 2 * p + 1))),
            still(width, 3 * width),
            still(*vec.shape),
        ]
        + [hbm] * 5,
        out_specs=[
            pl.BlockSpec((parts, 1, 2, local, block), before(lambda g, p, b: (0, g, p, 0, b))),
            pl.BlockSpec((1, block, WIDE), before(lambda g, p, b: (g, b, p))),
            pl.BlockSpec((1, WIDE, block), before(lambda g, p, b: (g, p, b))),
            pl.BlockSpec((1, 1, 2, block), before(lambda g, p, b: (g, p, 0, b))),
            pl.BlockSpec((others, 1, local, 2 * WIDE), now(lambda g, p, b: (0, g, 0, p))),
        ]
        + [hbm] * 4,
        out_shape=[
            jax.ShapeDtypeStruct((parts, groups, H, local, local), BF),
            jax.ShapeDtypeStruct((groups, local, width), BF),
            jax.ShapeDtypeStruct((groups, width, local), BF),
            jax.ShapeDtypeStruct((groups, PAIRS, 2, local), F32),
            jax.ShapeDtypeStruct((others, groups, local, 2 * width), BF),
        ]
        + [jax.ShapeDtypeStruct(v.shape, v.dtype) for v in passed],
        input_output_aliases={7: 5, 8: 6, 9: 7, 10: 8},
        scratch_shapes=[
            pltpu.VMEM((parts * local, 2 * WIDE), BF),
            pltpu.VMEM((2, WIDE, parts * local), BF),
            pltpu.VMEM((2, parts * local, block), F32),
            pltpu.VMEM((8, block), F32),
            pltpu.VMEM((others, local, width), BF),
            pltpu.VMEM((others, local, 2 * WIDE), BF),
            pltpu.SemaphoreType.DMA((groups,)),
            pltpu.SemaphoreType.DMA((copies,)),
            pltpu.SemaphoreType.DMA((copies,)),
        ],
        compiler_params=pltpu.CompilerParams(
            vmem_limit_bytes=62 * MIB,
            dimension_semantics=("arbitrary",),
            collective_id=1,
            has_side_effects=True,
        ),
        name="attend",
    )(lengths, query, pair_own, pair_own, weight, vec, tokens_low, *passed)


def middle_kernel(
    packed,
    tokens,
    cotangent,
    mixed,
    out_w,
    up_w,
    down_w,
    rows,
    result,
    partial,
    mixed_grad,
    upper_sums,
    lower_sums,
    vec_sums,
    out_wg,
    up_wg,
    down_wg,
    row_sums,
    up_bias_sum,
):
    first = pl.program_id(0) == 0

    @pl.when(first)
    def clear():
        out_wg[...] = jnp.zeros_like(out_wg)
        up_wg[...] = jnp.zeros_like(up_wg)
        down_wg[...] = jnp.zeros_like(down_wg)
        row_sums[...] = jnp.zeros_like(row_sums)
        up_bias_sum[...] = jnp.zeros_like(up_bias_sum)

    pieces = up_w.shape[1] // tokens.shape[1]
    up_bias = jnp.concatenate([rows[6 + i : 7 + i] for i in range(pieces)], axis=1)
    out_bias, gain_one, shift_one = rows[0:1], rows[1:2], rows[2:3]
    down_bias, gain_two, shift_two = rows[3:4], rows[4:5], rows[5:6]

    def mean(v):
        return jnp.mean(v, axis=-1, keepdims=True)

    def total(v):
        return jnp.sum(v, axis=0, keepdims=True)

    x = tokens[...]
    heads = mixed[...]
    hidden = x + (dot(heads, out_w[...]) + out_bias)
    centred = hidden - mean(hidden)
    r_one = lax.rsqrt(mean(centred * centred) + EPS)
    n_one = centred * r_one
    normal = n_one * gain_one + shift_one
    normal_low = normal.astype(BF)
    inner = dot(normal_low, up_w[...]) + up_bias
    square = inner * inner
    tanh = jnp.tanh(inner * (GELU_A + (GELU_A * GELU_B) * square))
    half = 0.5 + 0.5 * tanh
    active = (inner * half).astype(BF)
    slope = half + (0.5 * inner) * (1.0 - tanh * tanh) * (
        GELU_A + (3.0 * GELU_A * GELU_B) * square
    )
    branch = dot(active, down_w[...]) + down_bias
    last = normal + branch + x
    centred = last - mean(last)
    r_two = lax.rsqrt(mean(centred * centred) + EPS)
    n_two = centred * r_two
    result[...] = n_two * gain_two + shift_two
    grad = cotangent[...]
    e_two = grad * gain_two
    back = r_two * (e_two - mean(e_two) - n_two * mean(e_two * n_two))
    branch_grad = back.astype(BF)
    down_wg[...] += dot(active, branch_grad, "tn")
    inner_grad_wide = slope * dot(branch_grad, down_w[...], "nt")
    inner_grad = inner_grad_wide.astype(BF)
    up_wg[...] += dot(normal_low, inner_grad, "tn")
    up_bias_sum[...] += total(inner_grad.astype(F32))
    norm_grad = back + dot(inner_grad, up_w[...], "nt")
    e_one = norm_grad * gain_one
    hidden_grad = r_one * (e_one - mean(e_one) - n_one * mean(e_one * n_one))
    attn_grad = hidden_grad.astype(BF)
    partial[...] = back + hidden_grad
    out_wg[...] += dot(heads, attn_grad, "tn")
    mixed_grad[...] = dot(attn_grad, out_w[...], "nt").astype(BF)
    row_sums[0:1] += total(attn_grad.astype(F32))
    row_sums[1:2] += total(norm_grad * n_one)
    row_sums[2:3] += total(norm_grad)
    row_sums[3:4] += total(branch_grad.astype(F32))
    row_sums[4:5] += total(grad * n_two)
    row_sums[5:6] += total(grad)

    @pl.when(pl.program_id(0) == pl.num_programs(0) - 1)
    def pack():
        width = tokens.shape[1]
        pieces = up_wg.shape[1] // width
        vec_sums[...] = jnp.zeros_like(vec_sums)
        vec_sums[0:8] = row_sums[...]
        for piece in range(pieces):
            columns = slice(piece * width, (piece + 1) * width)
            vec_sums[8 + piece : 9 + piece] = up_bias_sum[:, columns]
        if not packed:
            upper_sums[:, :width] = out_wg[...]
            upper_sums[:, width:] = up_wg[...]
            lower_sums[...] = down_wg[...]
            return
        owners = upper_sums.shape[0]
        rows_out = out_wg.shape[0] // owners
        rows_down = down_wg.shape[0] // owners

        def one(owner, carry):
            near = pl.ds(pl.multiple_of(owner * rows_out, rows_out), rows_out)
            upper_sums[owner, :rows_out] = out_wg[near].astype(BF)
            for piece in range(pieces):
                columns = slice(piece * width, (piece + 1) * width)
                to = slice((piece + 1) * rows_out, (piece + 2) * rows_out)
                upper_sums[owner, to] = up_wg[near, columns].astype(BF)
            far = pl.ds(pl.multiple_of(owner * rows_down, rows_down), rows_down)
            lower_sums[owner] = down_wg[far].astype(BF)
            return carry

        lax.fori_loop(0, owners, one, 0)


def middle(tokens, cotangent, mixed, out_w, up_w, down_w, rows, owners):
    count, width = tokens.shape
    hidden = up_w.shape[1]
    block = min(256, count)
    packed = whole_tiles(width, owners)

    def moving(columns=width):
        return pl.BlockSpec((block, columns), lambda b: (b, 0))

    def still(*shape):
        return pl.BlockSpec(shape, lambda b: (0,) * len(shape), pipeline_mode=pl.Buffered(1))

    rows_upper = width // owners * (1 + hidden // width)
    rows_lower = hidden // owners
    if packed:
        sums = [((owners, rows_upper, width), BF), ((owners, rows_lower, width), BF)]
    else:
        sums = [((width, width + hidden), F32), ((hidden, width), F32)]
    return pl.pallas_call(
        functools.partial(middle_kernel, packed),
        grid=(count // block,),
        in_specs=[
            moving(),
            moving(),
            moving(),
            still(width, width),
            still(width, hidden),
            still(hidden, width),
            still(16, width),
        ],
        out_specs=[
            moving(),
            moving(),
            moving(),
        ]
        + [still(*shape) for shape, _ in sums]
        + [still(16, width)],
        out_shape=[
            jax.ShapeDtypeStruct((count, width), F32),
            jax.ShapeDtypeStruct((count, width), F32),
            jax.ShapeDtypeStruct((count, width), BF),
        ]
        + [jax.ShapeDtypeStruct(shape, kind) for shape, kind in sums]
        + [jax.ShapeDtypeStruct((16, width), F32)],
        scratch_shapes=[
            pltpu.VMEM((width, width), F32),
            pltpu.VMEM((width, hidden), F32),
            pltpu.VMEM((hidden, width), F32),
            pltpu.VMEM((8, width), F32),
            pltpu.VMEM((1, hidden), F32),
        ],
        compiler_params=params(62, 1),
        name="middle",
    )(tokens, cotangent, mixed, out_w, up_w, down_w, rows)


def pull_kernel(parts, groups, bits_dp, bits_seq, packed, *refs):
    taken = 0

    def take(count):
        nonlocal taken
        taken += count
        return refs[taken - count : taken]

    e_part, query, pair_own, pair_rest, mixed_grad, mixed_t, inverse = take(7)
    tokens_own, tokens_rest, weight, partial = take(4)
    sources = take(2) if packed else ()
    (vec_in,) = take(1)
    share_own, arrived, joint_out, vec_out = take(4)
    owned = take(2) if packed else ()
    d_scores, joint_grad, total, dq_sums, dq_turned, weight_grad, bias_grad, shares = take(8)
    share_send, share_recv, own_sem = take(3)
    step = pl.program_id(0)
    steps = pl.num_programs(0)
    each = groups * PAIRS
    part = lax.rem(step // each + 1, parts)
    own = part == 0
    inside = lax.rem(step, each)
    group = jnp.where(own, lax.rem(inside, groups), inside // PAIRS)
    pair = jnp.where(own, inside // groups, lax.rem(inside, PAIRS))

    net = Net(bits_dp, bits_seq)
    bits = net.bits
    orders = sum_orders(bits_dp, bits_seq)
    streams, loads = [], []
    if packed:
        upper_held, lower_held, early_held, late_held = take(4)
        vec_sent, vec_landing, bias_sent, bias_landing = take(4)
        send_sem, recv_sem = take(2)
        links = Links(net, send_sem, recv_sem)
        upper, lower = streams = [
            Halving(net, links, orders[i], held, take(len(orders[i])), sources[i])
            for i, held in enumerate((upper_held, lower_held))
        ]
        early, late = [
            Halving(net, links, orders[2], held, take(len(orders[2])))
            for held in (early_held, late_held)
        ]
        early_vec = Everywhere(net, links, orders[2], vec_out.at[0:16], vec_sent, vec_landing)
        late_vec = Everywhere(net, links, orders[2], bias_grad, bias_sent, bias_landing)
        for i, stream in enumerate(streams):
            at = stream.place(0, ())
            loads.append(pltpu.make_async_copy(sources[i].at[at], stream.held, own_sem.at[i]))
    stores = [
        pltpu.make_async_copy(total.at[g], share_own.at[g], own_sem.at[2 + g])
        for g in range(groups)
    ]

    def share_copy(other, g):
        return pltpu.make_async_remote_copy(
            src_ref=shares.at[other - 1, g],
            dst_ref=arrived.at[other - 1, g],
            send_sem=share_send.at[other - 1, g],
            recv_sem=share_recv.at[other - 1, g],
            device_id=(net.dp, lax.rem(net.seq + other, parts)),
            device_id_type=MESH,
        )

    @pl.when(step == 0)
    def enter():
        due = parts - 1
        for other in range(1, parts):
            net.signal((net.dp, lax.rem(net.seq + other, parts)))
        if packed:
            due += net.greet(orders[0]) + net.greet(orders[2])
        start(loads)
        pl.semaphore_wait(pltpu.get_barrier_semaphore(), due)
        for stream in streams:
            stream.start(0)

    def advance(streams, stage, outs, count):
        for stream, out in zip(streams, outs):
            stream.add(stage, out if stage == count - 1 else None)
            if stage < count - 1:
                stream.start(stage + 1)

    def pack(held, first, columns):
        rows_each = weight_grad.shape[0] // 2**bits

        def one(flat_index, carry):
            place = tuple(lax.rem(flat_index // 2 ** (bits - 1 - i), 2) for i in range(bits))
            near = pl.ds(pl.multiple_of(flat_index * rows_each, rows_each), rows_each)
            held[place] = weight_grad[near, first : first + columns].astype(BF)
            return carry

        lax.fori_loop(0, 2**bits, one, 0)

    split_at = 3 * WIDE * (PAIRS - 1)
    if packed:
        for stage, when in enumerate((1, 5, 9, 12)):
            @pl.when(step == when)
            def ffn():
                if stage == 0:
                    wait(loads)
                advance(streams, stage, owned, len(orders[0]))

        joint_early = joint_out.at[:, :split_at]

        @pl.when(step == steps - groups)
        def joint_first():
            pack(early.held, 0, split_at)
            vec_out[...] = vec_in[...]
            for stream in (early, early_vec):
                stream.start(0)

        @pl.when(step == steps - 1)
        def joint_second():
            advance((early, early_vec), 0, (joint_early, None), len(orders[2]))

    local = query.shape[1]
    chunk = min(256, local)
    turned = mixed_grad[0].astype(F32).T
    mixed = mixed_t[0].astype(F32)
    values = jnp.where(own, pair_own[0, :, WIDE:], pair_rest[0, 0, :, WIDE:])
    keys_t = jnp.where(own, pair_own[0, :, :WIDE], pair_rest[0, 0, :, :WIDE]).T
    query_now = query[0]
    lane = lax.broadcasted_iota(jnp.int32, (local, WIDE), 1)
    zero = jnp.zeros((HEAD, local), BF)
    grad_t, grad, centre, picked = [], [], [], []
    for head in range(2):
        side = slice(head * HEAD, (head + 1) * HEAD)
        inv = inverse[0, 0, head : head + 1]
        centre.append(inv * jnp.sum(turned[side] * mixed[side], axis=0, keepdims=True))
        scaled = (turned[side] * inv).astype(BF)
        grad_t.append(jnp.concatenate([scaled, zero] if head == 0 else [zero, scaled], axis=0))
        grad.append(grad_t[head].T)
        kept = lane < HEAD if head == 0 else lane >= HEAD
        picked.append(jnp.where(kept, query_now, jnp.zeros_like(query_now)))

    def key_grad(rows):
        sums = dot(d_scores[0, rows], picked[0]) + dot(d_scores[1, rows], picked[1])
        joint_grad[rows, WIDE : 2 * WIDE] = (sums * SCALE).astype(BF)

    last = None
    for at in range(0, local, chunk):
        rows = slice(at, at + chunk)
        for head in range(2):
            pulled = dot(values[rows], grad_t[head])
            e = e_part[0, 0, head, rows].astype(F32)
            d_scores[head, rows] = (e * (pulled - centre[head])).astype(BF)
        sums = dot(e_part[0, 0, 0, rows], grad[0]) + dot(e_part[0, 0, 1, rows], grad[1])
        joint_grad[rows, 2 * WIDE :] = sums.astype(BF)
        if last is not None:
            key_grad(last)
        last = rows
    key_grad(last)
    first_part = part == 1 % parts
    for head in range(2):
        side = slice(head * HEAD, (head + 1) * HEAD)
        dq = dot(keys_t, d_scores[head])[side]
        dq_turned[side] = dq

    @pl.when(step == 0)
    def clear():
        weight_grad[...] = jnp.zeros_like(weight_grad)
        bias_grad[...] = jnp.zeros_like(bias_grad)
        dq_sums[...] = jnp.zeros_like(dq_sums)

    @pl.when(jnp.logical_and(pair == 0, own))
    def start_near():
        total[group] = partial[0]

    @pl.when(jnp.logical_and(pair == 0, jnp.logical_not(own)))
    def start_far():
        total[group] = jnp.zeros(total.shape[1:], F32)

    side = pl.ds(pl.multiple_of(pair * WIDE, WIDE), WIDE)
    start_at = pair * (3 * WIDE)
    wide = pl.ds(pl.multiple_of(start_at, WIDE), 3 * WIDE)
    last_two = pl.ds(pl.multiple_of(start_at + WIDE, WIDE), 2 * WIDE)
    column = group * PAIRS + pair

    @pl.when(own)
    def near():
        dq = (dq_sums[column] + dq_turned[...]) * SCALE
        dq = dq.T.astype(BF)
        joint_grad[:, :WIDE] = dq
        bias_grad[0:1, side] += jnp.sum(dq.astype(F32), axis=0, keepdims=True)
        total[group] += dot(joint_grad[...], weight[:, wide], "nt")
        weight_grad[:, wide] += dot(tokens_own[group], joint_grad[...], "tn")

    @pl.when(jnp.logical_not(own))
    def far():
        dq_sums[column] += dq_turned[...]
        total[group] += dot(joint_grad[:, WIDE:], weight[:, last_two], "nt")
        weight_grad[:, last_two] += dot(tokens_rest[0, 0], joint_grad[:, WIDE:], "tn")

    bias_grad[1:2, side] += jnp.sum(joint_grad[:, 2 * WIDE :].astype(F32), axis=0, keepdims=True)

    for other in range(1, parts):
        for g in range(groups):
            @pl.when(step == ((other - 1) * groups + g + 1) * PAIRS - 1)
            def finish_far():
                shares[other - 1, g] = total[g].astype(BF)
                share_copy(other, g).start()

    for g in range(groups):
        @pl.when(step == steps - groups + g)
        def finish_near():
            start(stores[g : g + 1])

    @pl.when(step == steps - 1)
    def finish():
        if packed:
            last = len(orders[2])
            pack(late.held, split_at, 3 * WIDE)
            pairs = ((early, early_vec), (late, late_vec))
            outs = (joint_early, None), (joint_out.at[:, split_at:], None)
            for stream in pairs[1]:
                stream.start(0)
            for stage in range(last):
                if stage + 1 < last:
                    advance(pairs[0], stage + 1, outs[0], last)
                advance(pairs[1], stage, outs[1], last)
        else:
            vec_out[...] = vec_in[...]
            joint_out[...] = weight_grad[...]
        vec_out[12:14] = bias_grad[0:2]
        for g in range(groups):
            for other in range(1, parts):
                share_copy(other, g).wait()
        wait(stores)


def pull(
    e_all,
    query,
    pair_own,
    pair_rest,
    mixed_grad,
    mixed_t,
    inverse,
    own,
    rest,
    weight,
    partial,
    upper_sums,
    lower_sums,
    vec_sums,
):
    parts, groups, _, local, _ = e_all.shape
    width = H * HEAD
    each = groups * PAIRS
    bits_dp, bits_seq = mesh_bits()
    bits = bits_dp + bits_seq
    orders = sum_orders(bits_dp, bits_seq)
    packed = whole_tiles(width, 2**bits)
    split = (2,) * bits
    sums, out_blocks, extra = [], [], []
    if packed:
        rows_upper, rows_lower = upper_sums.shape[1], lower_sums.shape[1]
        rows_joint = width // 2**bits
        sums = [v.reshape(split + v.shape[1:]) for v in (upper_sums, lower_sums)]
        out_blocks = [(rows_joint, 3 * width), (16, width), (rows_upper, width), (rows_lower, width)]
        early = 3 * WIDE * (PAIRS - 1)
        late = 3 * WIDE
        last = len(orders[2])
        sends = sum(2 ** len(g) - 1 for order in orders for g in order)
        sends += 3 * sum(2 ** len(g) - 1 for g in orders[2])
        extra = [
            pltpu.VMEM((2,) * (bits - 1) + (rows_upper, width), BF),
            pltpu.VMEM((2,) * (bits - 1) + (rows_lower, width), BF),
            pltpu.VMEM(split + (rows_joint, early), BF),
            pltpu.VMEM(split + (rows_joint, late), BF),
            pltpu.VMEM((last, 16, width), F32),
            pltpu.VMEM((last, 3, 16, width), F32),
            pltpu.VMEM((last, 8, width), F32),
            pltpu.VMEM((last, 3, 8, width), F32),
            pltpu.SemaphoreType.DMA((sends,)),
            pltpu.SemaphoreType.DMA((sends,)),
        ]
        extra += landing_shapes(orders[0], bits, rows_upper, width)
        extra += landing_shapes(orders[1], bits, rows_lower, width)
        extra += landing_shapes(orders[2], bits, rows_joint, early)
        extra += landing_shapes(orders[2], bits, rows_joint, late)
    else:
        out_blocks = [(width, 3 * width), (16, width)]

    def decode(t):
        part, inside = (t // each + 1) % parts, t % each
        own = part == 0
        group = jnp.where(own, inside % groups, inside // PAIRS)
        pair = jnp.where(own, inside // groups, inside % PAIRS)
        return part, group, pair

    def at(place):
        return lambda t: place(*decode(t))

    def own_at(place):
        def index(t):
            part, group, pair = decode(t)
            return place(jnp.where(part == 0, group, 0), jnp.where(part == 0, pair, 0))

        return index

    def once_at(t):
        return jnp.clip(t - (parts - 1) * each, 0, groups - 1), 0, 0

    def rest_at(place):
        def index(t):
            t = jnp.minimum(t, (parts - 1) * each - 1)
            return place(t // each, t // PAIRS % groups, t % PAIRS)

        return index

    def still(*shape):
        return pl.BlockSpec(shape, lambda t: (0,) * len(shape), pipeline_mode=pl.Buffered(1))

    once = pl.Buffered(1)
    return pl.pallas_call(
        functools.partial(pull_kernel, parts, groups, bits_dp, bits_seq, packed),
        grid=(parts * each,),
        in_specs=[
            pl.BlockSpec((1, 1, 2, local, local), at(lambda j, g, p: (j, g, p, 0, 0))),
            pl.BlockSpec((1, local, WIDE), at(lambda j, g, p: (g, 0, p))),
            pl.BlockSpec((1, local, 2 * WIDE), own_at(lambda g, p: (g, 0, p))),
            pl.BlockSpec((1, 1, local, 2 * WIDE), rest_at(lambda j, g, p: (j, g, 0, p))),
            pl.BlockSpec((1, local, WIDE), at(lambda j, g, p: (g, 0, p))),
            pl.BlockSpec((1, WIDE, local), at(lambda j, g, p: (g, p, 0))),
            pl.BlockSpec((1, 1, 2, local), at(lambda j, g, p: (g, p, 0, 0))),
            still(groups, local, width),
            pl.BlockSpec(
                (1, 1, local, width), rest_at(lambda j, g, p: (j, g, 0, 0)), pipeline_mode=once
            ),
            still(width, 3 * width),
            pl.BlockSpec((1, local, width), once_at, pipeline_mode=once),
        ]
        + [pl.BlockSpec(memory_space=pl.ANY)] * len(sums)
        + [still(16, width)],
        out_specs=[
            pl.BlockSpec(memory_space=pl.ANY),
            pl.BlockSpec(memory_space=pl.ANY),
        ]
        + [still(*shape) for shape in out_blocks],
        out_shape=[
            jax.ShapeDtypeStruct((groups, local, width), F32),
            jax.ShapeDtypeStruct((parts - 1, groups, local, width), BF),
        ]
        + [jax.ShapeDtypeStruct(shape, F32) for shape in out_blocks],
        scratch_shapes=[
            pltpu.VMEM((2, local, local), BF),
            pltpu.VMEM((local, 3 * WIDE), BF),
            pltpu.VMEM((groups, local, width), F32),
            pltpu.VMEM((each, WIDE, local), F32),
            pltpu.VMEM((WIDE, local), F32),
            pltpu.VMEM((width, 3 * width), F32),
            pltpu.VMEM((8, width), F32),
            pltpu.VMEM((parts - 1, groups, local, width), BF),
            pltpu.SemaphoreType.DMA((parts - 1, groups)),
            pltpu.SemaphoreType.DMA((parts - 1, groups)),
            pltpu.SemaphoreType.DMA((2 + groups,)),
        ]
        + extra,
        compiler_params=pltpu.CompilerParams(
            vmem_limit_bytes=63 * MIB,
            dimension_semantics=("arbitrary",),
            collective_id=2,
            has_side_effects=True,
        ),
        name="pull",
    )(
        e_all,
        query,
        pair_own,
        pair_rest,
        mixed_grad,
        mixed_t,
        inverse,
        own,
        rest,
        weight,
        partial,
        *sums,
        vec_sums,
    )


def finish_kernel(bits_dp, bits_seq, share, arrived, joint, vec, upper, lower, *outs):
    (
        input_grad,
        joint_sum,
        pair_sum,
        out_sum,
        out_bias,
        gain_one,
        shift_one,
        up_sum,
        up_bias,
        down_sum,
        down_bias,
        gain_two,
        shift_two,
    ) = outs
    value = share[...]
    for other in range(arrived.shape[0]):
        value += arrived[other].astype(F32)
    input_grad[...] = value

    @pl.when(pl.program_id(0) == 0)
    def small():
        net = Net(bits_dp, bits_seq)
        device = net.dp * 2**bits_seq + net.seq
        rows, width = out_sum.shape
        summed = joint[...]
        turned = []
        for head in range(H):
            for kind in range(3):
                at = ((head // 2 * 3 + kind) * 2 + head % 2) * HEAD
                turned.append(summed[:, at : at + HEAD])
        joint_sum[...] = jnp.concatenate(turned, axis=1)
        out_sum[...] = upper[:rows]
        for piece in range(up_sum.shape[1] // width):
            up_sum[:, piece * width : (piece + 1) * width] = upper[
                (piece + 1) * rows : (piece + 2) * rows
            ]
        down_sum[...] = lower[...]
        lines = vec[...]
        which = lax.broadcasted_iota(jnp.int32, lines.shape, 0)

        def entries(out, row, column):
            line = jnp.sum(jnp.where(which == row, lines, 0.0), axis=0, keepdims=True)
            line = jnp.broadcast_to(line, (8, width))
            out[...] = pltpu.roll(line, lax.rem(width - column, width), 1)[:1, : out.shape[1]]

        plain = (out_bias, gain_one, shift_one, down_bias, gain_two, shift_two)
        for row, out in enumerate(plain):
            entries(out, row, device * out.shape[1])
        first = device * up_bias.shape[1]
        entries(up_bias, 8 + first // width, lax.rem(first, width))
        first = device * pair_sum.shape[1]
        kind = lax.rem(first // HEAD, 2)
        entries(pair_sum, 12 + kind, first // WIDE * HEAD + lax.rem(first, HEAD))


def finish(share, arrived, joint, vec, upper, lower, shards):
    groups, local, width = share.shape
    block = min(512, local)
    each = local // block

    def moving(*lead):
        return pl.BlockSpec(
            (1,) * len(lead) + (block, width), lambda b: (b // each, b % each, 0)
        )

    def still(shape):
        return pl.BlockSpec(shape, lambda b: (0,) * len(shape), pipeline_mode=pl.Buffered(1))

    bits_dp, bits_seq = mesh_bits()
    others = arrived.shape[0]
    small = (joint, vec, upper, lower)
    outs = pl.pallas_call(
        functools.partial(finish_kernel, bits_dp, bits_seq),
        grid=(groups * each,),
        in_specs=[
            moving(1),
            pl.BlockSpec((others, 1, block, width), lambda b: (0, b // each, b % each, 0)),
        ]
        + [still(v.shape) for v in small],
        out_specs=[moving(1)] + [still(shape) for shape in shards],
        out_shape=[jax.ShapeDtypeStruct(share.shape, F32)]
        + [jax.ShapeDtypeStruct(shape, F32) for shape in shards],
        compiler_params=params(62, 1),
        name="finish",
    )(share, arrived, *small)
    return [outs[0]] + [
        v.reshape(v.shape[1:]) if v.shape[0] == 1 else v for v in outs[1:]
    ]


def per_device(
    tokens,
    lengths,
    joint_weight,
    joint_bias,
    out_weight,
    out_bias,
    gain_first,
    shift_first,
    up_weight,
    up_bias,
    down_weight,
    down_bias,
    gain_second,
    shift_second,
    cotangent,
):
    groups, local, width = tokens.shape
    parts = lax.axis_size("seq")
    devices = lax.axis_size("dp") * parts
    me = lax.axis_index("seq")
    rows = groups * local
    own_rows = joint_weight.shape[0]
    vectors = [
        joint_bias,
        out_bias,
        gain_first,
        shift_first,
        up_bias,
        down_bias,
        gain_second,
        shift_second,
    ]
    lens = [v.shape[0] for v in vectors]
    tokens_low, tokens_rest, joint_w, vec, up_w, down_w, out_w, query, pair_own = begin(
        tokens,
        joint_weight,
        up_weight,
        down_weight,
        out_weight,
        [v.reshape(1, -1) for v in vectors],
        parts,
    )
    joint_w = matrix_of(joint_w)
    pieces = up_weight.shape[1] // width
    if not whole_tiles(width, devices):
        query, pair_own = project(
            tokens_low.reshape(rows, width), joint_w, vec[10:13].reshape(1, -1)
        )
        query = query.reshape(groups, local, width)
        pair_own = pair_own.reshape(groups, local, 2 * width)

    e_all, mixed, mixed_t, inverse, pair_rest, tokens_rest, up_w, down_w, out_w = attend(
        lengths, query, pair_own, joint_w, vec, tokens_low, tokens_rest, up_w, down_w, out_w
    )
    out_w, up_w, down_w = matrix_of(out_w), matrix_of(up_w), matrix_of(down_w)

    result, partial, mixed_grad, upper_sums, lower_sums, vec_sums = middle(
        tokens.reshape(rows, width),
        cotangent.reshape(rows, width),
        mixed.reshape(rows, width),
        out_w,
        up_w,
        down_w,
        vec,
        devices,
    )
    mixed_grad = mixed_grad.reshape(groups, local, width)
    share, arrived, joint, vec, *owned = pull(
        e_all,
        query,
        pair_own,
        pair_rest,
        mixed_grad,
        mixed_t,
        inverse,
        tokens_low,
        tokens_rest,
        joint_w,
        partial.reshape(groups, local, width),
        upper_sums,
        lower_sums,
        vec_sums,
    )
    if owned:
        upper, lower = owned
        shards = [
            (1, v.shape[0]) if v.ndim == 1 else v.shape
            for v in (
                joint_weight,
                joint_bias,
                out_weight,
                out_bias,
                gain_first,
                shift_first,
                up_weight,
                up_bias,
                down_weight,
                down_bias,
                gain_second,
                shift_second,
            )
        ]
        outs = finish(share, arrived, joint, vec, upper, lower, shards)
        return (result.reshape(groups, local, width), *outs)
    input_grad = share + jnp.sum(arrived.astype(F32), axis=0)
    joint_sum, upper, lower = owner_sums([joint, upper_sums, lower_sums])
    out_sum, up_sum = upper[:, :width], upper[:, width:]
    vec = lax.psum(vec, ("dp", "seq"))
    device = lax.axis_index("dp") * parts + me
    joint_sum = joint_sum.reshape(own_rows, PAIRS, 3, 2, HEAD).transpose(0, 1, 3, 2, 4)
    joint_sum = joint_sum.reshape(own_rows, 3 * width)
    pair_grad = jnp.stack(
        [vec[12].reshape(H, HEAD), vec[13].reshape(H, HEAD)], axis=1
    ).reshape(2 * width)
    sums = [
        pair_grad,
        vec[0],
        vec[1],
        vec[2],
        vec[8 : 8 + pieces].reshape(-1),
        vec[3],
        vec[4],
        vec[5],
    ]
    small = [
        lax.dynamic_slice_in_dim(v, device * size, size, 0) for v, size in zip(sums, lens)
    ]
    return (
        result.reshape(groups, local, width),
        input_grad,
        joint_sum,
        small[0],
        out_sum,
        small[1],
        small[2],
        small[3],
        up_sum,
        small[4],
        lower,
        small[5],
        small[6],
        small[7],
    )


def solution(mesh):
    both = ("dp", "seq")
    matrix, vector, whole = P(both, None), P(both), P("dp", "seq", None)
    return jax.shard_map(
        per_device,
        mesh=mesh,
        in_specs=(
            whole,
            P("dp"),
            matrix,
            vector,
            matrix,
            vector,
            vector,
            vector,
            matrix,
            vector,
            matrix,
            vector,
            vector,
            vector,
            whole,
        ),
        out_specs=(
            whole,
            whole,
            matrix,
            vector,
            matrix,
            vector,
            vector,
            vector,
            matrix,
            vector,
            matrix,
            vector,
            vector,
            vector,
        ),
        check_vma=False,
    )
```

time: 364 us -> 281 us (0.77)
  Pallas kernels: 325 us -> 280 us
  local copies, waits for them, and re-layouts: 28.3 us -> 0 us
  other arithmetic: 5.2 us -> 0 us
    pallas_call x4 -> x3, Pallas kernels: 205 us -> 171 us  [the longest x1 120 us: pull(): pl.pallas_call(functools.partial(pull_kernel, parts, groups, bits_dp, bit...]
    unnamed x44 -> x0, local copies, waits for them, and re-layouts: 14.3 us -> none
    pallas_call x1, Pallas kernels: 70.1 us -> 58.8 us  [attend(): pl.pallas_call(functools.partial(attend_kernel, parts, groups, steps, blo...]
    convert_element_type x14 -> x0, other arithmetic: 4.52 us -> none  [the longest x1 2.59 us: per_device(): tokens_low = tokens.astype(BF)]
    slice x8 -> x0, local copies, waits for them, and re-layouts: 4.35 us -> none  [the longest x1 1.38 us: per_device(): out_sum = upper[:own_rows]]
    reshape x8 -> x0, local copies, waits for them, and re-layouts: 3.72 us -> none  [the longest x1 0.96 us: per_device(): joint_sum = joint.reshape(3, own_rows, width).transpose(1, 0, 2)]
  transfers between devices with their start and end apart: 1 -> 0, of which waited for: 0 -> 0; matrix products, arithmetic and copies ran while one was open for 2% -> 0% of each run, Pallas kernels for 17% -> 0%
where the time goes in v4:
time: 281 us
  Pallas kernels  280 us (100%)
    pallas_call x1, Pallas kernels, pull(): pl.pallas_call(functools.partial(pull_kernel, parts, groups, bits_dp, bit...  120 us
    pallas_call x1, Pallas kernels, attend(): pl.pallas_call(functools.partial(attend_kernel, parts, groups, steps, blo...  58.8 us
    pallas_call x1, Pallas kernels, middle(): pl.pallas_call(functools.partial(middle_kernel, packed), grid=(count // b...  50.8 us
    pallas_call x1, Pallas kernels, begin(): pl.pallas_call(functools.partial(begin_kernel, bits_dp, bits_seq, parts,...  44.8 us

profile of v4, /device:TPU:0, one launch (start us, length us, event | category | flops | bytes accessed | tf_op | source)
XLA Modules:
  0.0 280.9 jit_solution(2238722031415236747)
XLA Ops:
  0.6 44.8 %begin.1 = (bf16[2,1024,512]{2,1,0:T(8,128)(2,1)}, bf16[1,2,1024,512]{3,2,1,0:T(8,128)(2,1)}, bf16[2,2,2,2,2,16,1536]{6,5,4,3,2,1,0:T(8,128)(2,1)}, f32[16,512]{...) custom-call(f32[2,1024,512]{2,1,0:T(8,128)} %refs_0_.2, ...), custom_call_target="tpu_custom_call" | custom-call | tf_op jit(solution)/shard_map/begin/pallas_call | solution.py:360
  45.5 58.8 %attend.1 = (bf16[2,2,8,1024,1024]{4,3,2,1,0:T(8,128)(2,1)}, bf16[2,1024,512]{2,1,0:T(8,128)(2,1)}, bf16[2,512,1024]{2,1,0:T(8,128)(2,1)}, f32[2,4,2,1024]{3,2,1...) custom-call(s32[2]{0:T(128)} %refs_0_.3, ...), custom_call_target="tpu_custom_call", output_to_operand_aliasing={{5}: (7, {}), {6}: (8, {}), {7}: (9, {}), {8}: (10, {})} | custom-call | tf_op jit(solution)/shard_map/attend/pallas_call | solution.py:741
  104.3 50.8 %middle.1 = (f32[2048,512]{1,0:T(8,128)}, f32[2048,512]{1,0:T(8,128)}, bf16[2048,512]{1,0:T(8,128)(2,1)}, bf16[32,80,512]{2,1,0:T(8,128)(2,1)}, bf16[32,64,512]{2,1,0:T(8,128)(2,1)}, /*index=5*/f32[16,512]{1,0:T(8,128)}) custom-call(f32[2048,512]{1,0:T(8,128)} %bitcast.28, f32[2048,512]{1,0:T(8,128)} %bitcast.34, bf16[2048,512]{1,0:T(8,128)(2,1)} %bitcast.38, ...), custom_call_target="tpu_custom_call" | custom-call | tf_op jit(solution)/shard_map/middle/pallas_call | solution.py:928
  155.1 120.1 %pull.1 = (f32[2,1024,512]{2,1,0:T(8,128)}, bf16[1,2,1024,512]{3,2,1,0:T(8,128)(2,1)}, f32[16,1536]{1,0:T(8,128)}, f32[16,512]{1,0:T(8,128)}, f32[80,512]{1,0:T(8,128)}, /*index=5*/f32[64,512]{1,0:T(8,128)}) custom-call(bf16[2,2,8,1024,1024]{4,3,2,1,0:T(8,128)(2,1)} %get-tuple-element.71.refs_0_, bf16[2,1024,512]{2,1,0:T(8,128)(2,1)} %get-tuple-element.57.refs_1_, ...), custom_call_target="tpu_custom_call" | custom-call | tf_op jit(solution)/shard_map/pull/pallas_call | solution.py:1279
  275.2 5.6 %finish.1 = (f32[2,1024,512]{2,1,0:T(8,128)}, f32[16,1536]{1,0:T(8,128)}, f32[1,32]{1,0:T(1,128)}, f32[16,512]{1,0:T(8,128)}, f32[1,16]{1,0:T(1,128)}, /*index=5...) custom-call(f32[2,1024,512]{2,1,0:T(8,128)} %get-tuple-element.81.sh, ...), custom_call_target="tpu_custom_call" | custom-call | tf_op jit(solution)/shard_map/finish/pallas_call | solution.py:1420

commit v5 on v4

--- a/solution.py
+++ b/solution.py
@@ -12,6 +12,8 @@
 HEAD = 64
 PAIRS = H // 2
 WIDE = 2 * HEAD
+JOINT_PARTS = ((0, 2), (2, 1), (3, 1))
+AHEAD = 16
 BF = jnp.bfloat16
 F32 = jnp.float32
 EPS = 1e-05
@@ -125,10 +127,11 @@
             device_id_type=MESH,
         )
 
-    def spread(self, full, done, group):
-        place = self.net.place(done)
+    def spread(self, full, done, group, columns=slice(None), shard=None):
+        place = self.net.place(done) + (slice(None), columns)
+        source = full.at[place] if shard is None else shard.at[:, columns]
         return [
-            self.copy(full.at[place], full.at[place], self.net.partner(flips))
+            self.copy(source, full.at[place], self.net.partner(flips))
             for flips in subsets(group)
         ]
 
@@ -164,17 +167,23 @@
     size, width = vector.shape[1], H * HEAD
     shift = log2(size)
     entry = lax.broadcasted_iota(jnp.int32, (size, width), 0)
-    column = lax.broadcasted_iota(jnp.int32, (1, width), 1) + row * width
-    pair = column * 0
-    for p in range(1, PAIRS):
-        pair += (column >= 3 * WIDE * p).astype(jnp.int32)
-    inside = column - 3 * WIDE * pair
-    kind = inside >> log2(WIDE)
-    head = 2 * pair + (inside >> log2(HEAD) & 1)
-    index = (2 * head + (kind >> 1)) * HEAD + (inside & (HEAD - 1))
-    index = jnp.where(kind == 1, -1, index)
+    column = lax.broadcasted_iota(jnp.int32, (1, width), 1)
+    if row > 0:
+        column += (row - 1) * width
+        head = 2 * (column >> log2(2 * WIDE)) + (column >> log2(HEAD) & 1)
+        index = (2 * head + 1) * HEAD + (column & (HEAD - 1))
+        index = jnp.where(column & WIDE == 0, -1, index)
+    else:
+        index = 2 * (column >> log2(HEAD)) * HEAD + (column & (HEAD - 1))
     here = (index >> shift == device) & (index & (size - 1) == entry)
     return dot(vector.astype(BF), here.astype(F32).astype(BF))
+
+
+def joint_columns():
+    blocks = [3 * head for head in range(H)]
+    for pair in range(PAIRS):
+        blocks += [3 * head + kind for kind in (1, 2) for head in (2 * pair, 2 * pair + 1)]
+    return blocks
 
 
 def begin_kernel(bits_dp, bits_seq, parts, packed, *refs):
@@ -242,106 +251,140 @@
     ]
     start(loads)
     joint = joint_wide[...]
-    turned = []
-    for head in range(0, H, 2):
-        for kind in range(3):
-            for at in (head, head + 1):
-                turned.append(joint[:, (3 * at + kind) * HEAD : (3 * at + kind + 1) * HEAD])
+    turned = [joint[:, b * HEAD : (b + 1) * HEAD] for b in joint_columns()]
     joint_shard[...] = jnp.concatenate(turned, axis=1).astype(BF)
     start(placed[:1])
-    up_shard[...] = up_wide[...].astype(BF)
-    down_shard[...] = down_wide[...].astype(BF)
-    out_shard[...] = out_wide[...].astype(BF)
-    start(placed[1:])
-    device = net.dp * parts + net.seq
-    vec[...] = jnp.zeros_like(vec)
-    lines = (out_bias, gain_one, shift_one, down_bias, gain_two, shift_two)
-    for row, vector in enumerate(lines):
-        vec[row : row + 1] = owned_row(vector[...], 0, device)
-    for row in range(4):
-        vec[6 + row : 7 + row] = owned_row(up_bias[...], row, device)
-    for row in range(3):
-        vec[10 + row : 11 + row] = owned_pair(pair_bias[...], row, device)
-    wait(placed)
     pl.semaphore_wait(pltpu.get_barrier_semaphore(), due)
+
+    def prepare():
+        up_shard[...] = up_wide[...].astype(BF)
+        down_shard[...] = down_wide[...].astype(BF)
+        out_shard[...] = out_wide[...].astype(BF)
+        start(placed[1:])
+        device = net.dp * parts + net.seq
+        vec[...] = jnp.zeros_like(vec)
+        lines = (out_bias, gain_one, shift_one, down_bias, gain_two, shift_two)
+        for row, vector in enumerate(lines):
+            vec[row : row + 1] = owned_row(vector[...], 0, device)
+        for row in range(4):
+            vec[6 + row : 7 + row] = owned_row(up_bias[...], row, device)
+        for row in range(3):
+            vec[10 + row : 11 + row] = owned_pair(pair_bias[...], row, device)
+        wait(placed)
 
     def narrowed(g):
         wait(loads[g : g + 1])
         narrow[g] = wide[g].astype(BF)
         start(stores[g : g + 1])
 
-    late = []
-    exchange = []
-    for stage, group in enumerate(order):
-        done = flat(order[:stage])
-        joint = links.spread(joint_w, done, group)
-        vec_sent[stage] = vec[...]
-        small = [
+    cut = width + 2 * WIDE
+    columns = (slice(0, cut), slice(cut, 3 * width))
+    dones = [flat(order[:stage]) for stage in range(len(order))]
+    ahead, behind = [
+        [
+            links.spread(joint_w, done, group, c, None if done else joint_shard)
+            for done, group in zip(dones, order)
+        ]
+        for c in columns
+    ]
+    small = [
+        [
             links.copy(vec_sent.at[stage], vec_landing.at[stage, i], net.partner(flips))
             for i, flips in enumerate(subsets(group))
         ]
-        start(joint)
-        start(small)
+        for stage, group in enumerate(order)
+    ]
+
+    def small_start(stage):
+        vec_sent[stage] = vec[...]
+        start(small[stage])
+
+    def small_add(stage):
+        wait(small[stage])
+        for i in range(len(small[stage])):
+            vec[...] += vec_landing[stage, i]
+
+    exchange = [
+        links.copy(narrow.at[0], tokens_rest.at[other - 1, 0], ring(net, parts, other))
+        for other in range(1, parts)
+    ]
+    some = slice(0, local // AHEAD)
+    exchange_next = [
+        links.copy(narrow.at[1, some], tokens_rest.at[other - 1, 1, some], ring(net, parts, other))
+        for other in range(1, parts)
+    ]
+
+    def projected(part):
+        bias = jnp.concatenate([vec[10 + i : 11 + i] for i in range(3)], axis=1)[:, columns[part]]
+        block = min(256, local)
+        for g in range(groups):
+
+            def rows_of(b, carry):
+                rows = pl.ds(pl.multiple_of(b * block, block), block)
+                full = joint_w[..., columns[part]].reshape(width, -1)
+                joint = (dot(narrow[g, rows], full) + bias).astype(BF)
+                if part == 0:
+                    query_here[g, rows] = joint[:, :width]
+                    pair_here[g, rows, : cut - width] = joint[:, width:]
+                else:
+                    pair_here[g, rows, cut - width :] = joint
+                return carry
+
+            lax.fori_loop(0, local // block, rows_of, 0)
+
+    late, rest = [], []
+    last = len(order) - 1
+    start(ahead[0])
+    start(behind[0])
+    prepare()
+    small_start(0)
+    for stage in range(last):
+        done, group = dones[stage], order[stage]
         if stage < len(beside):
             rest = [links.spread(full, done, group) for full in (up_w, down_w, out_w)]
             for copies in rest:
                 start(copies)
         if stage == len(beside) - 1:
             narrowed(0)
-            exchange = [
-                links.copy(narrow.at[0], tokens_rest.at[other - 1, 0], ring(net, parts, other))
-                for other in range(1, parts)
-            ]
             start(exchange)
         elif stage == len(beside):
             for g in range(1, groups):
                 narrowed(g)
-        wait(joint)
-        wait(small)
-        for i in range(len(small)):
-            vec[...] += vec_landing[stage, i]
-        if stage < len(beside):
-            for copies in rest:
-                wait(copies)
-        elif stage < len(beside) + len(upper):
+            start(exchange_next)
+        wait(ahead[stage])
+        small_add(stage)
+        start(ahead[stage + 1])
+        small_start(stage + 1)
+        if stage + 1 < last:
+            wait(behind[stage])
+            start(behind[stage + 1])
+        for copies in rest:
+            wait(copies)
+        rest = []
+        if len(beside) <= stage < len(beside) + len(upper):
             wait(late)
             late = links.spread(up_w, done, group)
             start(late)
+    wait(ahead[last])
+    small_add(last)
+    if packed:
+        projected(0)
+    wait(behind[last - 1])
+    start(behind[last])
+    wait(behind[last])
+    if packed:
+        results = [
+            pltpu.make_async_copy(joint_here, joint_out, own_sem.at[4 * groups + 4]),
+            pltpu.make_async_copy(query_here, query, own_sem.at[4 * groups + 5]),
+        ]
+        start(results)
+        projected(1)
+        results.append(pltpu.make_async_copy(pair_here, pair_own, own_sem.at[4 * groups + 6]))
+        start(results[2:])
+        wait(results)
     wait(late)
-    if packed:
-        whole = pltpu.make_async_copy(joint_here, joint_out, own_sem.at[4 * groups + 4])
-        whole.start()
-        weight = joint_w.shape[-1]
-        bias = jnp.concatenate([vec[10 + i : 11 + i] for i in range(3)], axis=1)
-        block = min(256, local)
-        results = []
-        for g in range(groups):
-
-            def rows_of(b, carry):
-                rows = pl.ds(pl.multiple_of(b * block, block), block)
-                full = joint_w[...].reshape(width, weight)
-                joint = (dot(narrow[g, rows], full) + bias).astype(BF)
-                for p in range(PAIRS):
-                    at = 3 * WIDE * p
-                    query_here[g, rows, p * WIDE : (p + 1) * WIDE] = joint[:, at : at + WIDE]
-                    pair_here[g, rows, 2 * p * WIDE : 2 * (p + 1) * WIDE] = joint[
-                        :, at + WIDE : at + 3 * WIDE
-                    ]
-                return carry
-
-            lax.fori_loop(0, local // block, rows_of, 0)
-            results.append(
-                pltpu.make_async_copy(query_here.at[g], query.at[g], own_sem.at[2 * groups + 4 + g])
-            )
-            results.append(
-                pltpu.make_async_copy(
-                    pair_here.at[g], pair_own.at[g], own_sem.at[3 * groups + 4 + g]
-                )
-            )
-            start(results[-2:])
-        wait(results)
-        whole.wait()
     wait(exchange)
+    wait(exchange_next)
     wait(stores)
 
 
@@ -353,7 +396,7 @@
     beside, upper, next_to, cores = stages_of(bits_dp, bits_seq)
     order = beside + upper + next_to + cores
     sends = sum(2 ** len(group) - 1 for group in order)
-    copies = 2 * sends + 4 * sends + parts
+    copies = 3 * sends + 4 * sends + 2 * parts
     split = (2,) * bits
     hbm = pl.BlockSpec(memory_space=pl.ANY)
     vmem = pl.BlockSpec(memory_space=pltpu.VMEM)
@@ -384,7 +427,7 @@
             pltpu.VMEM((len(order), 3, 16, width), F32),
             pltpu.VMEM((groups, local, width), BF),
             pltpu.VMEM((groups, local, 2 * width), BF),
-            pltpu.SemaphoreType.DMA((4 * groups + 5,)),
+            pltpu.SemaphoreType.DMA((4 * groups + 7,)),
             pltpu.SemaphoreType.DMA((copies,)),
             pltpu.SemaphoreType.DMA((copies,)),
         ],
@@ -521,11 +564,9 @@
 
 def project_kernel(tokens, weight, bias, query, pair):
     x = tokens[...]
-    for p in range(PAIRS):
-        columns = slice(3 * WIDE * p, 3 * WIDE * (p + 1))
-        joint = (dot(x, weight[:, columns]) + bias[:, columns]).astype(BF)
-        query[:, p * WIDE : (p + 1) * WIDE] = joint[:, :WIDE]
-        pair[:, 2 * p * WIDE : 2 * (p + 1) * WIDE] = joint[:, WIDE:]
+    width = x.shape[1]
+    query[...] = (dot(x, weight[:, :width]) + bias[:, :width]).astype(BF)
+    pair[...] = (dot(x, weight[:, width:]) + bias[:, width:]).astype(BF)
 
 
 def project(tokens, weight, bias):
@@ -574,7 +615,7 @@
         up_w,
         down_w,
         out_w,
-        k_ext,
+        k_mask,
         v_ext,
         kept,
         tops,
@@ -604,20 +645,23 @@
         if ahead < last:
             copies += links.spread(up_w, flat(order[:ahead]), order[ahead])
         rounds.append(copies)
-    times = [0, 7, 12, 14, 15, 16]
     if len(rounds) > 3:
         times = [i * steps // (len(rounds) + 1) for i in range(len(rounds) + 1)]
     else:
-        times = [0, steps * 7 // 16, steps * 12 // 16, steps * 14 // 16]
-    exchange = [
-        [
-            links.copy(
-                tokens_low.at[g], tokens_rest.at[other - 1, g], ring(net, parts, other)
-            )
-            for other in range(1, parts)
-        ]
-        for g in range(1, groups)
-    ]
+        times = [0, steps * 6 // 16, steps * 12 // 16, steps * 14 // 16]
+    exchange = []
+    for g in range(1, groups):
+        left = slice(local // AHEAD if g == 1 else 0, local)
+        exchange.append(
+            [
+                links.copy(
+                    tokens_low.at[g, left],
+                    tokens_rest.at[other - 1, g, left],
+                    ring(net, parts, other),
+                )
+                for other in range(1, parts)
+            ]
+        )
 
     @pl.when(step == 0)
     def enter():
@@ -637,48 +681,58 @@
             if i + 1 < len(rounds):
                 start(rounds[i + 1])
 
+    stores = [
+        pltpu.make_async_copy(pair_here.at[:, g], pair_rest.at[:, g], own_sem.at[groups + g])
+        for g in range(groups)
+    ]
+    for group in range(groups):
+        @pl.when(step == group * blocks * PAIRS)
+        def other_keys():
+            if group > 0:
+                wait(exchange[group - 1])
+            copy = pltpu.make_async_copy(tokens_rest.at[:, group], rest_here, own_sem.at[group])
+            copy.start()
+            width = weight.shape[0]
+            bias = jnp.concatenate([vec[11:12], vec[12:13]], axis=1)
+            for part in range(parts):
+                rows = slice(part * local, (part + 1) * local)
+                first_key = lax.rem(net.seq + part, parts) * local
+                place = lax.broadcasted_iota(jnp.int32, (local, WIDE), 0) + first_key
+                k_mask[rows] = jnp.where(place < lengths[group], 0.0, -1e30).astype(BF)
+            copy.wait()
+            for part in range(1, parts):
+                for p in range(PAIRS):
+                    columns = slice(2 * WIDE * p, 2 * WIDE * (p + 1))
+                    both = dot(rest_here[part - 1], weight[:, width:][:, columns])
+                    pair_here[part - 1, group, p] = (both + bias[:, columns]).astype(BF)
+            start(stores[group : group + 1])
+
+    @pl.when(step == steps)
+    def leave():
+        wait(stores)
+
+    def decode(t):
+        return t // (PAIRS * blocks), lax.rem(t // blocks, PAIRS)
+
+    group_then, pair_then = decode(jnp.maximum(step - 1, 0))
+
     @pl.when(step % blocks == 1 % blocks)
     def prepare_values():
         for part in range(parts):
             rows = slice(part * local, (part + 1) * local)
-            values = values_own[0] if part == 0 else pair_here[part - 1, :, WIDE:]
+            if part == 0:
+                values = values_own[0]
+            else:
+                values = pair_here[part - 1, group_then, pair_then, :, WIDE:]
             turned = values.T
             v_ext[0, :HEAD, rows] = turned[:HEAD]
             v_ext[1, :HEAD, rows] = turned[HEAD:]
-            v_ext[:, HEAD:, rows] = jnp.ones((2, HEAD, local), BF)
-
-    for group in range(groups):
-        @pl.when(step == group * blocks * PAIRS)
-        def fetch():
-            if group > 0:
-                wait(exchange[group - 1])
-            copy = pltpu.make_async_copy(tokens_rest.at[:, group], rest_here, own_sem.at[group])
-            copy.start()
-            copy.wait()
-
-    @pl.when(jnp.logical_and(step % blocks == 0, step < steps))
-    def prepare_keys():
-        pair = lax.rem(step // blocks, PAIRS)
-        columns = pl.ds(pl.multiple_of(pair * (3 * WIDE) + WIDE, WIDE), 2 * WIDE)
-        bias = jnp.zeros((1, 2 * WIDE), F32)
-        flat_bias = jnp.concatenate([vec[10 + i : 11 + i] for i in range(3)], axis=1)
-        for p in range(PAIRS):
-            at = 3 * WIDE * p + WIDE
-            bias = jnp.where(pair == p, flat_bias[:, at : at + 2 * WIDE], bias)
-        for part in range(1, parts):
-            both = (dot(rest_here[part - 1], weight[:, columns]) + bias).astype(BF)
-            pair_here[part - 1] = both
-            pair_rest[part - 1, 0] = both
-        for group in range(groups):
-            @pl.when(step // (blocks * PAIRS) == group)
-            def fill():
-                length = lengths[group]
-                for part in range(parts):
-                    rows = slice(part * local, (part + 1) * local)
-                    k_ext[rows, :WIDE] = keys_own[0] if part == 0 else pair_here[part - 1, :, :WIDE]
-                    first_key = lax.rem(net.seq + part, parts) * local
-                    place = lax.broadcasted_iota(jnp.int32, (local, WIDE), 0) + first_key
-                    k_ext[rows, WIDE:] = jnp.where(place < length, 0.0, -1e30).astype(BF)
+
+    @pl.when(step == 0)
+    def ones():
+        v_ext[:, HEAD:] = jnp.ones((2, HEAD, parts * local), BF)
+
+    group_now, pair_now = decode(jnp.minimum(step, steps - 1))
 
     turned = query[0].T
     zero = jnp.zeros((HEAD, block), BF)
@@ -699,7 +753,11 @@
             e_out[at // local, 0, head, inside] = e
             add = dot(v_ext[head, :, rows], e)
             out = add if out is None else out + add
-            scores = dot(k_ext[rows], picked)
+            if at < local:
+                keys = keys_own[0, inside]
+            else:
+                keys = pair_here[at // local - 1, group_now, pair_now, inside, :WIDE]
+            scores = dot(jnp.concatenate([keys, k_mask[rows]], axis=1), picked)
             kept[head, rows] = scores
             most = jnp.max(scores.reshape(chunk // 8, 8, block), axis=0)
             largest = most if largest is None else jnp.maximum(largest, most)
@@ -755,7 +813,7 @@
             pl.BlockSpec((1, block, WIDE), before(lambda g, p, b: (g, b, p))),
             pl.BlockSpec((1, WIDE, block), before(lambda g, p, b: (g, p, b))),
             pl.BlockSpec((1, 1, 2, block), before(lambda g, p, b: (g, p, 0, b))),
-            pl.BlockSpec((others, 1, local, 2 * WIDE), now(lambda g, p, b: (0, g, 0, p))),
+            hbm,
         ]
         + [hbm] * 4,
         out_shape=[
@@ -763,18 +821,18 @@
             jax.ShapeDtypeStruct((groups, local, width), BF),
             jax.ShapeDtypeStruct((groups, width, local), BF),
             jax.ShapeDtypeStruct((groups, PAIRS, 2, local), F32),
-            jax.ShapeDtypeStruct((others, groups, local, 2 * width), BF),
+            jax.ShapeDtypeStruct((others, groups, PAIRS, local, 2 * WIDE), BF),
         ]
         + [jax.ShapeDtypeStruct(v.shape, v.dtype) for v in passed],
         input_output_aliases={7: 5, 8: 6, 9: 7, 10: 8},
         scratch_shapes=[
-            pltpu.VMEM((parts * local, 2 * WIDE), BF),
+            pltpu.VMEM((parts * local, WIDE), BF),
             pltpu.VMEM((2, WIDE, parts * local), BF),
             pltpu.VMEM((2, parts * local, block), F32),
             pltpu.VMEM((8, block), F32),
             pltpu.VMEM((others, local, width), BF),
-            pltpu.VMEM((others, local, 2 * WIDE), BF),
-            pltpu.SemaphoreType.DMA((groups,)),
+            pltpu.VMEM((others, groups, PAIRS, local, 2 * WIDE), BF),
+            pltpu.SemaphoreType.DMA((2 * groups,)),
             pltpu.SemaphoreType.DMA((copies,)),
             pltpu.SemaphoreType.DMA((copies,)),
         ],
@@ -910,7 +968,7 @@
 def middle(tokens, cotangent, mixed, out_w, up_w, down_w, rows, owners):
     count, width = tokens.shape
     hidden = up_w.shape[1]
-    block = min(256, count)
+    block = min(512, count)
     packed = whole_tiles(width, owners)
 
     def moving(columns=width):
@@ -993,7 +1051,8 @@
     orders = sum_orders(bits_dp, bits_seq)
     streams, loads = [], []
     if packed:
-        upper_held, lower_held, early_held, late_held = take(4)
+        upper_held, lower_held = take(2)
+        joint_helds = take(len(JOINT_PARTS))
         vec_sent, vec_landing, bias_sent, bias_landing = take(4)
         send_sem, recv_sem = take(2)
         links = Links(net, send_sem, recv_sem)
@@ -1001,10 +1060,7 @@
             Halving(net, links, orders[i], held, take(len(orders[i])), sources[i])
             for i, held in enumerate((upper_held, lower_held))
         ]
-        early, late = [
-            Halving(net, links, orders[2], held, take(len(orders[2])))
-            for held in (early_held, late_held)
-        ]
+        joint = [Halving(net, links, orders[2], h, take(len(orders[2]))) for h in joint_helds]
         early_vec = Everywhere(net, links, orders[2], vec_out.at[0:16], vec_sent, vec_landing)
         late_vec = Everywhere(net, links, orders[2], bias_grad, bias_sent, bias_landing)
         for i, stream in enumerate(streams):
@@ -1014,6 +1070,10 @@
         pltpu.make_async_copy(total.at[g], share_own.at[g], own_sem.at[2 + g])
         for g in range(groups)
     ]
+    partials = [
+        pltpu.make_async_copy(partial.at[g], total.at[g], own_sem.at[2 + groups + g])
+        for g in range(groups)
+    ]
 
     def share_copy(other, g):
         return pltpu.make_async_remote_copy(
@@ -1033,6 +1093,7 @@
         if packed:
             due += net.greet(orders[0]) + net.greet(orders[2])
         start(loads)
+        start(partials)
         pl.semaphore_wait(pltpu.get_barrier_semaphore(), due)
         for stream in streams:
             stream.start(0)
@@ -1043,19 +1104,30 @@
             if stage < count - 1:
                 stream.start(stage + 1)
 
-    def pack(held, first, columns):
-        rows_each = weight_grad.shape[0] // 2**bits
+    def pack(index):
+        first, count = JOINT_PARTS[index]
+        held = joint[index].held
+        rows_each, width = weight_grad.shape[0] // 2**bits, weight_grad.shape[0]
+        columns = slice(first * WIDE, (first + count) * WIDE)
+        doubled = slice(width + 2 * first * WIDE, width + 2 * (first + count) * WIDE)
 
         def one(flat_index, carry):
             place = tuple(lax.rem(flat_index // 2 ** (bits - 1 - i), 2) for i in range(bits))
             near = pl.ds(pl.multiple_of(flat_index * rows_each, rows_each), rows_each)
-            held[place] = weight_grad[near, first : first + columns].astype(BF)
+            held[place + (slice(None), slice(0, count * WIDE))] = weight_grad[near, columns].astype(BF)
+            held[place + (slice(None), slice(count * WIDE, 3 * count * WIDE))] = weight_grad[
+                near, doubled
+            ].astype(BF)
             return carry
 
         lax.fori_loop(0, 2**bits, one, 0)
 
-    split_at = 3 * WIDE * (PAIRS - 1)
+    def joint_place(index):
+        first, count = JOINT_PARTS[index]
+        return joint_out.at[:, 3 * first * WIDE : 3 * (first + count) * WIDE]
+
     if packed:
+        last = len(orders[2])
         for stage, when in enumerate((1, 5, 9, 12)):
             @pl.when(step == when)
             def ffn():
@@ -1063,25 +1135,33 @@
                     wait(loads)
                 advance(streams, stage, owned, len(orders[0]))
 
-        joint_early = joint_out.at[:, :split_at]
+        @pl.when(step == steps - 2 * groups)
+        def joint_early():
+            pack(0)
+            vec_out[...] = vec_in[...]
+            joint[0].start(0)
+            early_vec.start(0)
+
+        @pl.when(step == steps - 2 * groups + 1)
+        def joint_early_near():
+            advance((joint[0], early_vec), 0, (None, None), last)
 
         @pl.when(step == steps - groups)
-        def joint_first():
-            pack(early.held, 0, split_at)
-            vec_out[...] = vec_in[...]
-            for stream in (early, early_vec):
-                stream.start(0)
+        def joint_middle():
+            pack(1)
+            joint[1].start(0)
 
         @pl.when(step == steps - 1)
-        def joint_second():
-            advance((early, early_vec), 0, (joint_early, None), len(orders[2]))
+        def joint_middle_near():
+            advance((joint[0], early_vec), 1, (None, None), last)
+            advance((joint[1],), 0, (None,), last)
 
     local = query.shape[1]
     chunk = min(256, local)
     turned = mixed_grad[0].astype(F32).T
     mixed = mixed_t[0].astype(F32)
-    values = jnp.where(own, pair_own[0, :, WIDE:], pair_rest[0, 0, :, WIDE:])
-    keys_t = jnp.where(own, pair_own[0, :, :WIDE], pair_rest[0, 0, :, :WIDE]).T
+    values = jnp.where(own, pair_own[0, :, WIDE:], pair_rest[0, 0, 0, :, WIDE:])
+    keys_t = jnp.where(own, pair_own[0, :, :WIDE], pair_rest[0, 0, 0, :, :WIDE]).T
     query_now = query[0]
     lane = lax.broadcasted_iota(jnp.int32, (local, WIDE), 1)
     zero = jnp.zeros((HEAD, local), BF)
@@ -1096,11 +1176,18 @@
         kept = lane < HEAD if head == 0 else lane >= HEAD
         picked.append(jnp.where(kept, query_now, jnp.zeros_like(query_now)))
 
+    width = weight.shape[0]
+    at_queries = pl.ds(pl.multiple_of(pair * WIDE, WIDE), WIDE)
+    start_at = width + pair * (2 * WIDE)
+    at_keys = pl.ds(pl.multiple_of(start_at, WIDE), WIDE)
+    at_values = pl.ds(pl.multiple_of(start_at + WIDE, WIDE), WIDE)
+    at_both = pl.ds(pl.multiple_of(start_at, WIDE), 2 * WIDE)
+
     def key_grad(rows):
         sums = dot(d_scores[0, rows], picked[0]) + dot(d_scores[1, rows], picked[1])
-        joint_grad[rows, WIDE : 2 * WIDE] = (sums * SCALE).astype(BF)
-
-    last = None
+        joint_grad[group, rows, at_keys] = (sums * SCALE).astype(BF)
+
+    last_rows = None
     for at in range(0, local, chunk):
         rows = slice(at, at + chunk)
         for head in range(2):
@@ -1108,12 +1195,11 @@
             e = e_part[0, 0, head, rows].astype(F32)
             d_scores[head, rows] = (e * (pulled - centre[head])).astype(BF)
         sums = dot(e_part[0, 0, 0, rows], grad[0]) + dot(e_part[0, 0, 1, rows], grad[1])
-        joint_grad[rows, 2 * WIDE :] = sums.astype(BF)
-        if last is not None:
-            key_grad(last)
-        last = rows
-    key_grad(last)
-    first_part = part == 1 % parts
+        joint_grad[group, rows, at_values] = sums.astype(BF)
+        if last_rows is not None:
+            key_grad(last_rows)
+        last_rows = rows
+    key_grad(last_rows)
     for head in range(2):
         side = slice(head * HEAD, (head + 1) * HEAD)
         dq = dot(keys_t, d_scores[head])[side]
@@ -1125,65 +1211,64 @@
         bias_grad[...] = jnp.zeros_like(bias_grad)
         dq_sums[...] = jnp.zeros_like(dq_sums)
 
-    @pl.when(jnp.logical_and(pair == 0, own))
-    def start_near():
-        total[group] = partial[0]
-
-    @pl.when(jnp.logical_and(pair == 0, jnp.logical_not(own)))
-    def start_far():
-        total[group] = jnp.zeros(total.shape[1:], F32)
-
-    side = pl.ds(pl.multiple_of(pair * WIDE, WIDE), WIDE)
-    start_at = pair * (3 * WIDE)
-    wide = pl.ds(pl.multiple_of(start_at, WIDE), 3 * WIDE)
-    last_two = pl.ds(pl.multiple_of(start_at + WIDE, WIDE), 2 * WIDE)
     column = group * PAIRS + pair
 
     @pl.when(own)
     def near():
         dq = (dq_sums[column] + dq_turned[...]) * SCALE
         dq = dq.T.astype(BF)
-        joint_grad[:, :WIDE] = dq
-        bias_grad[0:1, side] += jnp.sum(dq.astype(F32), axis=0, keepdims=True)
-        total[group] += dot(joint_grad[...], weight[:, wide], "nt")
-        weight_grad[:, wide] += dot(tokens_own[group], joint_grad[...], "tn")
+        joint_grad[group, :, at_queries] = dq
+        bias_grad[0:1, at_queries] += jnp.sum(dq.astype(F32), axis=0, keepdims=True)
+        weight_grad[:, at_queries] += dot(tokens_own[group], dq, "tn")
+        weight_grad[:, at_both] += dot(tokens_own[group], joint_grad[group, :, at_both], "tn")
 
     @pl.when(jnp.logical_not(own))
     def far():
         dq_sums[column] += dq_turned[...]
-        total[group] += dot(joint_grad[:, WIDE:], weight[:, last_two], "nt")
-        weight_grad[:, last_two] += dot(tokens_rest[0, 0], joint_grad[:, WIDE:], "tn")
-
-    bias_grad[1:2, side] += jnp.sum(joint_grad[:, 2 * WIDE :].astype(F32), axis=0, keepdims=True)
+        weight_grad[:, at_both] += dot(tokens_rest[0, 0], joint_grad[group, :, at_both], "tn")
+
+    value_sums = jnp.sum(joint_grad[group, :, at_values].astype(F32), axis=0, keepdims=True)
+    bias_grad[1:2, at_queries] += value_sums
 
     for other in range(1, parts):
         for g in range(groups):
             @pl.when(step == ((other - 1) * groups + g + 1) * PAIRS - 1)
             def finish_far():
-                shares[other - 1, g] = total[g].astype(BF)
+                for at in range(0, local, chunk):
+                    rows = slice(at, at + chunk)
+                    part_share = dot(joint_grad[g, rows, width:], weight[:, width:], "nt")
+                    shares[other - 1, g, rows] = part_share.astype(BF)
                 share_copy(other, g).start()
 
-    for g in range(groups):
-        @pl.when(step == steps - groups + g)
-        def finish_near():
-            start(stores[g : g + 1])
+    def input_grads(g):
+        for at in range(0, local, chunk):
+            rows = slice(at, at + chunk)
+            total[g, rows] += dot(joint_grad[g, rows], weight[...], "nt")
+        start(stores[g : g + 1])
 
     @pl.when(step == steps - 1)
     def finish():
+        work = list(range(groups))
         if packed:
-            last = len(orders[2])
-            pack(late.held, split_at, 3 * WIDE)
-            pairs = ((early, early_vec), (late, late_vec))
-            outs = (joint_early, None), (joint_out.at[:, split_at:], None)
-            for stream in pairs[1]:
-                stream.start(0)
+            pack(2)
+            joint[2].start(0)
+            late_vec.start(0)
+            advance((joint[1],), 1, (None,), last)
+        wait(partials)
+        if packed:
             for stage in range(last):
-                if stage + 1 < last:
-                    advance(pairs[0], stage + 1, outs[0], last)
-                advance(pairs[1], stage, outs[1], last)
+                if work:
+                    input_grads(work.pop(0))
+                outs = (joint_place(2), None)
+                advance((joint[2], late_vec), stage, outs, last)
+                if stage == 0:
+                    advance((joint[0], early_vec), last - 1, (joint_place(0), None), last)
+            joint[1].add(last - 1, joint_place(1))
         else:
             vec_out[...] = vec_in[...]
             joint_out[...] = weight_grad[...]
+        for g in work:
+            input_grads(g)
         vec_out[12:14] = bias_grad[0:2]
         for g in range(groups):
             for other in range(1, parts):
@@ -1221,16 +1306,16 @@
         rows_joint = width // 2**bits
         sums = [v.reshape(split + v.shape[1:]) for v in (upper_sums, lower_sums)]
         out_blocks = [(rows_joint, 3 * width), (16, width), (rows_upper, width), (rows_lower, width)]
-        early = 3 * WIDE * (PAIRS - 1)
-        late = 3 * WIDE
+        joint_widths = [3 * count * WIDE for _, count in JOINT_PARTS]
         last = len(orders[2])
         sends = sum(2 ** len(g) - 1 for order in orders for g in order)
-        sends += 3 * sum(2 ** len(g) - 1 for g in orders[2])
+        sends += 4 * sum(2 ** len(g) - 1 for g in orders[2])
         extra = [
             pltpu.VMEM((2,) * (bits - 1) + (rows_upper, width), BF),
             pltpu.VMEM((2,) * (bits - 1) + (rows_lower, width), BF),
-            pltpu.VMEM(split + (rows_joint, early), BF),
-            pltpu.VMEM(split + (rows_joint, late), BF),
+        ]
+        extra += [pltpu.VMEM(split + (rows_joint, columns), BF) for columns in joint_widths]
+        extra += [
             pltpu.VMEM((last, 16, width), F32),
             pltpu.VMEM((last, 3, 16, width), F32),
             pltpu.VMEM((last, 8, width), F32),
@@ -1240,8 +1325,8 @@
         ]
         extra += landing_shapes(orders[0], bits, rows_upper, width)
         extra += landing_shapes(orders[1], bits, rows_lower, width)
-        extra += landing_shapes(orders[2], bits, rows_joint, early)
-        extra += landing_shapes(orders[2], bits, rows_joint, late)
+        for columns in joint_widths:
+            extra += landing_shapes(orders[2], bits, rows_joint, columns)
     else:
         out_blocks = [(width, 3 * width), (16, width)]
 
@@ -1261,9 +1346,6 @@
             return place(jnp.where(part == 0, group, 0), jnp.where(part == 0, pair, 0))
 
         return index
-
-    def once_at(t):
-        return jnp.clip(t - (parts - 1) * each, 0, groups - 1), 0, 0
 
     def rest_at(place):
         def index(t):
@@ -1283,7 +1365,7 @@
             pl.BlockSpec((1, 1, 2, local, local), at(lambda j, g, p: (j, g, p, 0, 0))),
             pl.BlockSpec((1, local, WIDE), at(lambda j, g, p: (g, 0, p))),
             pl.BlockSpec((1, local, 2 * WIDE), own_at(lambda g, p: (g, 0, p))),
-            pl.BlockSpec((1, 1, local, 2 * WIDE), rest_at(lambda j, g, p: (j, g, 0, p))),
+            pl.BlockSpec((1, 1, 1, local, 2 * WIDE), rest_at(lambda j, g, p: (j, g, p, 0, 0))),
             pl.BlockSpec((1, local, WIDE), at(lambda j, g, p: (g, 0, p))),
             pl.BlockSpec((1, WIDE, local), at(lambda j, g, p: (g, p, 0))),
             pl.BlockSpec((1, 1, 2, local), at(lambda j, g, p: (g, p, 0, 0))),
@@ -1292,7 +1374,7 @@
                 (1, 1, local, width), rest_at(lambda j, g, p: (j, g, 0, 0)), pipeline_mode=once
             ),
             still(width, 3 * width),
-            pl.BlockSpec((1, local, width), once_at, pipeline_mode=once),
+            pl.BlockSpec(memory_space=pl.ANY),
         ]
         + [pl.BlockSpec(memory_space=pl.ANY)] * len(sums)
         + [still(16, width)],
@@ -1308,7 +1390,7 @@
         + [jax.ShapeDtypeStruct(shape, F32) for shape in out_blocks],
         scratch_shapes=[
             pltpu.VMEM((2, local, local), BF),
-            pltpu.VMEM((local, 3 * WIDE), BF),
+            pltpu.VMEM((groups, local, 3 * width), BF),
             pltpu.VMEM((groups, local, width), F32),
             pltpu.VMEM((each, WIDE, local), F32),
             pltpu.VMEM((WIDE, local), F32),
@@ -1317,7 +1399,7 @@
             pltpu.VMEM((parts - 1, groups, local, width), BF),
             pltpu.SemaphoreType.DMA((parts - 1, groups)),
             pltpu.SemaphoreType.DMA((parts - 1, groups)),
-            pltpu.SemaphoreType.DMA((2 + groups,)),
+            pltpu.SemaphoreType.DMA((2 + 2 * groups,)),
         ]
         + extra,
         compiler_params=pltpu.CompilerParams(
@@ -1373,9 +1455,13 @@
         summed = joint[...]
         turned = []
         for head in range(H):
-            for kind in range(3):
-                at = ((head // 2 * 3 + kind) * 2 + head % 2) * HEAD
-                turned.append(summed[:, at : at + HEAD])
+            pair = head // 2
+            for first, count in JOINT_PARTS:
+                if first <= pair < first + count:
+                    base = 3 * first * WIDE + head % 2 * HEAD
+                    both = base + (count + 2 * (pair - first)) * WIDE
+                    for at in (base + (pair - first) * WIDE, both, both + WIDE):
+                        turned.append(summed[:, at : at + HEAD])
         joint_sum[...] = jnp.concatenate(turned, axis=1)
         out_sum[...] = upper[:rows]
         for piece in range(up_sum.shape[1] // width):
@@ -1546,8 +1632,9 @@
     out_sum, up_sum = upper[:, :width], upper[:, width:]
     vec = lax.psum(vec, ("dp", "seq"))
     device = lax.axis_index("dp") * parts + me
-    joint_sum = joint_sum.reshape(own_rows, PAIRS, 3, 2, HEAD).transpose(0, 1, 3, 2, 4)
-    joint_sum = joint_sum.reshape(own_rows, 3 * width)
+    back = [joint_columns().index(block) for block in range(3 * H)]
+    joint_sum = joint_sum.reshape(own_rows, 3 * H, HEAD)
+    joint_sum = jnp.stack([joint_sum[:, b] for b in back], axis=1).reshape(own_rows, 3 * width)
     pair_grad = jnp.stack(
         [vec[12].reshape(H, HEAD), vec[13].reshape(H, HEAD)], axis=1
     ).reshape(2 * width)

time: 281 us -> 263 us (0.936)
  Pallas kernels: 280 us -> 262 us
    pallas_call x1, Pallas kernels: 44.8 us -> 38.9 us  [begin(): pl.pallas_call(functools.partial(begin_kernel, bits_dp, bits_seq, parts,...]
    pallas_call x1, Pallas kernels: 120 us -> 115 us  [pull(): pl.pallas_call(functools.partial(pull_kernel, parts, groups, bits_dp, bit...]
    pallas_call x1, Pallas kernels: 50.8 us -> 46.8 us  [middle(): pl.pallas_call(functools.partial(middle_kernel, packed), grid=(count // b...]
    pallas_call x1, Pallas kernels: 58.8 us -> 55.3 us  [attend(): pl.pallas_call(functools.partial(attend_kernel, parts, groups, steps, blo...]
where the time goes in v5:
time: 263 us
  Pallas kernels  262 us (100%)
    pallas_call x1, Pallas kernels, pull(): pl.pallas_call(functools.partial(pull_kernel, parts, groups, bits_dp, bit...  115 us
    pallas_call x1, Pallas kernels, attend(): pl.pallas_call(functools.partial(attend_kernel, parts, groups, steps, blo...  55.3 us
    pallas_call x1, Pallas kernels, middle(): pl.pallas_call(functools.partial(middle_kernel, packed), grid=(count // b...  46.8 us
    pallas_call x1, Pallas kernels, begin(): pl.pallas_call(functools.partial(begin_kernel, bits_dp, bits_seq, parts,...  38.9 us
    pallas_call x1, Pallas kernels, finish(): pl.pallas_call(functools.partial(finish_kernel, bits_dp, bits_seq), grid=...  5.56 us

profile of v5, /device:TPU:0, one launch (start us, length us, event | category | flops | bytes accessed | tf_op | source)
XLA Modules:
  0.0 262.6 jit_solution(5183194182076269244)
XLA Ops:
  0.6 38.9 %begin.1 = (bf16[2,1024,512]{2,1,0:T(8,128)(2,1)}, bf16[1,2,1024,512]{3,2,1,0:T(8,128)(2,1)}, bf16[2,2,2,2,2,16,1536]{6,5,4,3,2,1,0:T(8,128)(2,1)}, f32[16,512]{...) custom-call(f32[2,1024,512]{2,1,0:T(8,128)} %refs_0_.2, ...), custom_call_target="tpu_custom_call" | custom-call | tf_op jit(solution)/shard_map/begin/pallas_call | solution.py:403
  39.5 55.3 %attend.1 = (bf16[2,2,8,1024,1024]{4,3,2,1,0:T(8,128)(2,1)}, bf16[2,1024,512]{2,1,0:T(8,128)(2,1)}, bf16[2,512,1024]{2,1,0:T(8,128)(2,1)}, f32[2,4,2,1024]{3,2,1...) custom-call(s32[2]{0:T(128)} %refs_0_.3, ...), custom_call_target="tpu_custom_call", output_to_operand_aliasing={{5}: (7, {}), {6}: (8, {}), {7}: (9, {}), {8}: (10, {})} | custom-call | tf_op jit(solution)/shard_map/attend/pallas_call | solution.py:799
  94.8 46.8 %middle.1 = (f32[2048,512]{1,0:T(8,128)}, f32[2048,512]{1,0:T(8,128)}, bf16[2048,512]{1,0:T(8,128)(2,1)}, bf16[32,80,512]{2,1,0:T(8,128)(2,1)}, bf16[32,64,512]{2,1,0:T(8,128)(2,1)}, /*index=5*/f32[16,512]{1,0:T(8,128)}) custom-call(f32[2048,512]{1,0:T(8,128)} %bitcast.28, f32[2048,512]{1,0:T(8,128)} %bitcast.34, bf16[2048,512]{1,0:T(8,128)(2,1)} %bitcast.38, ...), custom_call_target="tpu_custom_call" | custom-call | tf_op jit(solution)/shard_map/middle/pallas_call | solution.py:986
  141.6 115.3 %pull.1 = (f32[2,1024,512]{2,1,0:T(8,128)}, bf16[1,2,1024,512]{3,2,1,0:T(8,128)(2,1)}, f32[16,1536]{1,0:T(8,128)}, f32[16,512]{1,0:T(8,128)}, f32[80,512]{1,0:T(8,128)}, /*index=5*/f32[64,512]{1,0:T(8,128)}) custom-call(bf16[2,2,8,1024,1024]{4,3,2,1,0:T(8,128)(2,1)} %get-tuple-element.71.refs_0_, bf16[2,1024,512]{2,1,0:T(8,128)(2,1)} %get-tuple-element.57.refs_1_, ...), custom_call_target="tpu_custom_call" | custom-call | tf_op jit(solution)/shard_map/pull/pallas_call | solution.py:1361
  256.9 5.6 %finish.1 = (f32[2,1024,512]{2,1,0:T(8,128)}, f32[16,1536]{1,0:T(8,128)}, f32[1,32]{1,0:T(1,128)}, f32[16,512]{1,0:T(8,128)}, f32[1,16]{1,0:T(1,128)}, /*index=5...) custom-call(f32[2,1024,512]{2,1,0:T(8,128)} %get-tuple-element.81.sh, ...), custom_call_target="tpu_custom_call" | custom-call | tf_op jit(solution)/shard_map/finish/pallas_call | solution.py:1506

commit v6 on v5

--- a/solution.py
+++ b/solution.py
@@ -53,8 +53,8 @@
         self.bits_dp, self.bits_seq = bits_dp, bits_seq
         self.bits = bits_dp + bits_seq
         self.dp, self.seq = lax.axis_index("dp"), lax.axis_index("seq")
-        self.mine = [lax.rem(self.dp // 2 ** (bits_dp - 1 - b), 2) for b in range(bits_dp)]
-        self.mine += [lax.rem(self.seq // 2 ** (bits_seq - 1 - b), 2) for b in range(bits_seq)]
+        self.mine = [lax.rem(lax.div(self.dp, 2 ** (bits_dp - 1 - b)), 2) for b in range(bits_dp)]
+        self.mine += [lax.rem(lax.div(self.seq, 2 ** (bits_seq - 1 - b)), 2) for b in range(bits_seq)]
 
     def partner(self, flips):
         dp, seq = self.dp, self.seq
@@ -111,6 +111,17 @@
     return log2(lax.axis_size("dp")), log2(lax.axis_size("seq"))
 
 
+class Later:
+    def __init__(self, make):
+        self.make = make
+
+    def start(self):
+        self.make().start()
+
+    def wait(self):
+        self.make().wait()
+
+
 class Links:
     def __init__(self, net, send_sem, recv_sem):
         self.net, self.send_sem, self.recv_sem, self.used = net, send_sem, recv_sem, 0
@@ -118,20 +129,26 @@
     def copy(self, source, target, device):
         at = self.used
         self.used += 1
-        return pltpu.make_async_remote_copy(
-            src_ref=source,
-            dst_ref=target,
-            send_sem=self.send_sem.at[at],
-            recv_sem=self.recv_sem.at[at],
-            device_id=device,
-            device_id_type=MESH,
+        return Later(
+            lambda: pltpu.make_async_remote_copy(
+                src_ref=source(),
+                dst_ref=target(),
+                send_sem=self.send_sem.at[at],
+                recv_sem=self.recv_sem.at[at],
+                device_id=device(),
+                device_id_type=MESH,
+            )
         )
 
     def spread(self, full, done, group, columns=slice(None), shard=None):
-        place = self.net.place(done) + (slice(None), columns)
-        source = full.at[place] if shard is None else shard.at[:, columns]
+        def target():
+            return full.at[self.net.place(done) + (slice(None), columns)]
+
+        def source():
+            return target() if shard is None else shard.at[:, columns]
+
         return [
-            self.copy(source, full.at[place], self.net.partner(flips))
+            self.copy(source, target, functools.partial(self.net.partner, flips))
             for flips in subsets(group)
         ]
 
@@ -202,6 +219,7 @@
         gain_two,
         shift_two,
         tokens_low,
+        tokens_t,
         tokens_rest,
         joint_out,
         vec,
@@ -212,6 +230,7 @@
         pair_own,
         wide,
         narrow,
+        narrow_t,
         joint_here,
         joint_shard,
         up_shard,
@@ -242,6 +261,7 @@
         pltpu.make_async_copy(narrow.at[g], tokens_low.at[g], own_sem.at[groups + g])
         for g in range(groups)
     ]
+    turned_stores = [pltpu.make_async_copy(narrow_t, tokens_t, own_sem.at[4 * groups + 7])]
     mine = net.place(())
     placed = [
         pltpu.make_async_copy(shard, full.at[mine], own_sem.at[2 * groups + i])
@@ -277,6 +297,14 @@
         narrow[g] = wide[g].astype(BF)
         start(stores[g : g + 1])
 
+    def turned_tokens():
+        block = min(256, local)
+        for g in range(groups):
+            for at in range(0, local, block):
+                rows = slice(at, at + block)
+                narrow_t[g, :, rows] = narrow[g, rows].T
+        start(turned_stores)
+
     cut = width + 2 * WIDE
     columns = (slice(0, cut), slice(cut, 3 * width))
     dones = [flat(order[:stage]) for stage in range(len(order))]
@@ -289,7 +317,11 @@
     ]
     small = [
         [
-            links.copy(vec_sent.at[stage], vec_landing.at[stage, i], net.partner(flips))
+            links.copy(
+                functools.partial(Everywhere.line, vec_sent, stage),
+                functools.partial(Everywhere.line, vec_landing, stage, i),
+                functools.partial(net.partner, flips),
+            )
             for i, flips in enumerate(subsets(group))
         ]
         for stage, group in enumerate(order)
@@ -305,12 +337,20 @@
             vec[...] += vec_landing[stage, i]
 
     exchange = [
-        links.copy(narrow.at[0], tokens_rest.at[other - 1, 0], ring(net, parts, other))
+        links.copy(
+            functools.partial(Everywhere.line, narrow, 0),
+            functools.partial(Everywhere.line, tokens_rest, other - 1, 0),
+            functools.partial(ring, net, parts, other),
+        )
         for other in range(1, parts)
     ]
     some = slice(0, local // AHEAD)
     exchange_next = [
-        links.copy(narrow.at[1, some], tokens_rest.at[other - 1, 1, some], ring(net, parts, other))
+        links.copy(
+            functools.partial(Everywhere.line, narrow, 1, some),
+            functools.partial(Everywhere.line, tokens_rest, other - 1, 1, some),
+            functools.partial(ring, net, parts, other),
+        )
         for other in range(1, parts)
     ]
 
@@ -351,6 +391,7 @@
             for g in range(1, groups):
                 narrowed(g)
             start(exchange_next)
+            turned_tokens()
         wait(ahead[stage])
         small_add(stage)
         start(ahead[stage + 1])
@@ -386,6 +427,7 @@
     wait(exchange)
     wait(exchange_next)
     wait(stores)
+    wait(turned_stores)
 
 
 def begin(tokens, joint, up, down, out, vectors, parts):
@@ -403,9 +445,10 @@
     return pl.pallas_call(
         functools.partial(begin_kernel, bits_dp, bits_seq, parts, packed),
         in_specs=[hbm] + [vmem] * (4 + len(vectors)),
-        out_specs=[hbm, hbm, hbm, vmem] + [hbm] * 5,
+        out_specs=[hbm, hbm, hbm, hbm, vmem] + [hbm] * 5,
         out_shape=[
             jax.ShapeDtypeStruct((groups, local, width), BF),
+            jax.ShapeDtypeStruct((groups, width, local), BF),
             jax.ShapeDtypeStruct((parts - 1, groups, local, width), BF),
             jax.ShapeDtypeStruct(split + joint.shape, BF),
             jax.ShapeDtypeStruct((16, width), F32),
@@ -418,6 +461,7 @@
         scratch_shapes=[
             pltpu.VMEM((groups, local, width), F32),
             pltpu.VMEM((groups, local, width), BF),
+            pltpu.VMEM((groups, width, local), BF),
             pltpu.VMEM(split + joint.shape if packed else (16, 128), BF),
             pltpu.VMEM(joint.shape, BF),
             pltpu.VMEM(up.shape, BF),
@@ -427,7 +471,7 @@
             pltpu.VMEM((len(order), 3, 16, width), F32),
             pltpu.VMEM((groups, local, width), BF),
             pltpu.VMEM((groups, local, 2 * width), BF),
-            pltpu.SemaphoreType.DMA((4 * groups + 7,)),
+            pltpu.SemaphoreType.DMA((4 * groups + 8,)),
             pltpu.SemaphoreType.DMA((copies,)),
             pltpu.SemaphoreType.DMA((copies,)),
         ],
@@ -475,9 +519,13 @@
         for stage, group in enumerate(groups):
             copies = []
             for i, flips in enumerate(subsets(group)):
-                at = self.place(stage, flips)
-                part = source.at[at] if stage == 0 and source is not None else held.at[self.cut(at)]
-                copies.append(links.copy(part, landing[stage].at[i], net.partner(flips)))
+                copies.append(
+                    links.copy(
+                        functools.partial(self.part, stage, flips, source),
+                        functools.partial(self.slot, stage, i),
+                        functools.partial(net.partner, flips),
+                    )
+                )
             self.rounds.append(copies)
 
     def place(self, stage, turned):
@@ -489,6 +537,13 @@
             else:
                 at.append(slice(None))
         return tuple(at)
+
+    def part(self, stage, flips, source):
+        at = self.place(stage, flips)
+        return source.at[at] if stage == 0 and source is not None else self.held.at[self.cut(at)]
+
+    def slot(self, stage, i):
+        return self.landing[stage].at[i]
 
     def cut(self, at):
         return tuple(a for bit, a in enumerate(at) if bit not in self.gone)
@@ -528,11 +583,19 @@
         self.value, self.sent, self.landing = value, sent, landing
         self.rounds = [
             [
-                links.copy(sent.at[stage], landing.at[stage, i], net.partner(flips))
+                links.copy(
+                    functools.partial(self.line, sent, stage),
+                    functools.partial(self.line, landing, stage, i),
+                    functools.partial(net.partner, flips),
+                )
                 for i, flips in enumerate(subsets(group))
             ]
             for stage, group in enumerate(groups)
         ]
+
+    @staticmethod
+    def line(ref, *at):
+        return ref.at[at]
 
     def start(self, stage):
         self.sent[stage] = self.value[...]
@@ -655,9 +718,9 @@
         exchange.append(
             [
                 links.copy(
-                    tokens_low.at[g, left],
-                    tokens_rest.at[other - 1, g, left],
-                    ring(net, parts, other),
+                    functools.partial(Everywhere.line, tokens_low, g, left),
+                    functools.partial(Everywhere.line, tokens_rest, other - 1, g, left),
+                    functools.partial(ring, net, parts, other),
                 )
                 for other in range(1, parts)
             ]
@@ -712,11 +775,11 @@
         wait(stores)
 
     def decode(t):
-        return t // (PAIRS * blocks), lax.rem(t // blocks, PAIRS)
+        return lax.div(t, PAIRS * blocks), lax.rem(lax.div(t, blocks), PAIRS)
 
     group_then, pair_then = decode(jnp.maximum(step - 1, 0))
 
-    @pl.when(step % blocks == 1 % blocks)
+    @pl.when(lax.rem(step, blocks) == 1 % blocks)
     def prepare_values():
         for part in range(parts):
             rows = slice(part * local, (part + 1) * local)
@@ -783,7 +846,9 @@
     copies = 3 * sends + groups * others
 
     def decode(t, place):
-        return place(t // (PAIRS * blocks), t // blocks % PAIRS, t % blocks)
+        return place(
+            lax.div(t, PAIRS * blocks), lax.rem(lax.div(t, blocks), PAIRS), lax.rem(t, blocks)
+        )
 
     def now(place):
         return lambda t: decode(jnp.minimum(t, steps - 1), place)
@@ -1030,7 +1095,7 @@
         return refs[taken - count : taken]
 
     e_part, query, pair_own, pair_rest, mixed_grad, mixed_t, inverse = take(7)
-    tokens_own, tokens_rest, weight, partial = take(4)
+    tokens_t, tokens_rest, weight, partial = take(4)
     sources = take(2) if packed else ()
     (vec_in,) = take(1)
     share_own, arrived, joint_out, vec_out = take(4)
@@ -1040,11 +1105,11 @@
     step = pl.program_id(0)
     steps = pl.num_programs(0)
     each = groups * PAIRS
-    part = lax.rem(step // each + 1, parts)
+    part = lax.rem(lax.div(step, each) + 1, parts)
     own = part == 0
     inside = lax.rem(step, each)
-    group = jnp.where(own, lax.rem(inside, groups), inside // PAIRS)
-    pair = jnp.where(own, inside // groups, lax.rem(inside, PAIRS))
+    group = jnp.where(own, lax.rem(inside, groups), lax.div(inside, PAIRS))
+    pair = jnp.where(own, lax.div(inside, groups), lax.rem(inside, PAIRS))
 
     net = Net(bits_dp, bits_seq)
     bits = net.bits
@@ -1219,13 +1284,12 @@
         dq = dq.T.astype(BF)
         joint_grad[group, :, at_queries] = dq
         bias_grad[0:1, at_queries] += jnp.sum(dq.astype(F32), axis=0, keepdims=True)
-        weight_grad[:, at_queries] += dot(tokens_own[group], dq, "tn")
-        weight_grad[:, at_both] += dot(tokens_own[group], joint_grad[group, :, at_both], "tn")
+        weight_grad[:, at_queries] += dot(tokens_t[group], dq)
+        weight_grad[:, at_both] += dot(tokens_t[group], joint_grad[group, :, at_both])
 
     @pl.when(jnp.logical_not(own))
     def far():
         dq_sums[column] += dq_turned[...]
-        weight_grad[:, at_both] += dot(tokens_rest[0, 0], joint_grad[group, :, at_both], "tn")
 
     value_sums = jnp.sum(joint_grad[group, :, at_values].astype(F32), axis=0, keepdims=True)
     bias_grad[1:2, at_queries] += value_sums
@@ -1239,6 +1303,7 @@
                     part_share = dot(joint_grad[g, rows, width:], weight[:, width:], "nt")
                     shares[other - 1, g, rows] = part_share.astype(BF)
                 share_copy(other, g).start()
+                weight_grad[:, width:] += dot(tokens_rest[0, 0], joint_grad[g, :, width:], "tn")
 
     def input_grads(g):
         for at in range(0, local, chunk):
@@ -1331,10 +1396,10 @@
         out_blocks = [(width, 3 * width), (16, width)]
 
     def decode(t):
-        part, inside = (t // each + 1) % parts, t % each
+        part, inside = lax.rem(lax.div(t, each) + 1, parts), lax.rem(t, each)
         own = part == 0
-        group = jnp.where(own, inside % groups, inside // PAIRS)
-        pair = jnp.where(own, inside // groups, inside % PAIRS)
+        group = jnp.where(own, lax.rem(inside, groups), lax.div(inside, PAIRS))
+        pair = jnp.where(own, lax.div(inside, groups), lax.rem(inside, PAIRS))
         return part, group, pair
 
     def at(place):
@@ -1350,7 +1415,9 @@
     def rest_at(place):
         def index(t):
             t = jnp.minimum(t, (parts - 1) * each - 1)
-            return place(t // each, t // PAIRS % groups, t % PAIRS)
+            return place(
+                lax.div(t, each), lax.rem(lax.div(t, PAIRS), groups), lax.rem(t, PAIRS)
+            )
 
         return index
 
@@ -1369,7 +1436,7 @@
             pl.BlockSpec((1, local, WIDE), at(lambda j, g, p: (g, 0, p))),
             pl.BlockSpec((1, WIDE, local), at(lambda j, g, p: (g, p, 0))),
             pl.BlockSpec((1, 1, 2, local), at(lambda j, g, p: (g, p, 0, 0))),
-            still(groups, local, width),
+            still(groups, width, local),
             pl.BlockSpec(
                 (1, 1, local, width), rest_at(lambda j, g, p: (j, g, 0, 0)), pipeline_mode=once
             ),
@@ -1556,7 +1623,7 @@
         shift_second,
     ]
     lens = [v.shape[0] for v in vectors]
-    tokens_low, tokens_rest, joint_w, vec, up_w, down_w, out_w, query, pair_own = begin(
+    tokens_low, tokens_t, tokens_rest, joint_w, vec, up_w, down_w, out_w, query, pair_own = begin(
         tokens,
         joint_weight,
         up_weight,
@@ -1598,7 +1665,7 @@
         mixed_grad,
         mixed_t,
         inverse,
-        tokens_low,
+        tokens_t,
         tokens_rest,
         joint_w,
         partial.reshape(groups, local, width),

time: 263 us -> 260 us (0.989)
  Pallas kernels: 262 us -> 259 us
    pallas_call x1, Pallas kernels: 115 us -> 112 us  [pull(): pl.pallas_call(functools.partial(pull_kernel, parts, groups, bits_dp, bit...]
where the time goes in v6:
time: 260 us
  Pallas kernels  259 us (100%)
    pallas_call x1, Pallas kernels, pull(): pl.pallas_call(functools.partial(pull_kernel, parts, groups, bits_dp, bit...  112 us
    pallas_call x1, Pallas kernels, attend(): pl.pallas_call(functools.partial(attend_kernel, parts, groups, steps, blo...  55.2 us
    pallas_call x1, Pallas kernels, middle(): pl.pallas_call(functools.partial(middle_kernel, packed), grid=(count // b...  46.7 us
    pallas_call x1, Pallas kernels, begin(): pl.pallas_call(functools.partial(begin_kernel, bits_dp, bits_seq, parts,...  38.9 us
    pallas_call x1, Pallas kernels, finish(): pl.pallas_call(functools.partial(finish_kernel, bits_dp, bits_seq), grid=...  5.56 us

profile of v6, /device:TPU:0, one launch (start us, length us, event | category | flops | bytes accessed | tf_op | source)
XLA Modules:
  0.0 259.7 jit_solution(12902827425463678798)
XLA Ops:
  0.6 38.9 %begin.1 = (bf16[2,1024,512]{2,1,0:T(8,128)(2,1)}, bf16[2,512,1024]{2,1,0:T(8,128)(2,1)}, bf16[1,2,1024,512]{3,2,1,0:T(8,128)(2,1)}, bf16[2,2,2,2,2,16,1536]{6,5...) custom-call(f32[2,1024,512]{2,1,0:T(8,128)} %refs_0_.2, ...), custom_call_target="tpu_custom_call" | custom-call | tf_op jit(solution)/shard_map/begin/pallas_call | solution.py:445
  39.6 55.2 %attend.1 = (bf16[2,2,8,1024,1024]{4,3,2,1,0:T(8,128)(2,1)}, bf16[2,1024,512]{2,1,0:T(8,128)(2,1)}, bf16[2,512,1024]{2,1,0:T(8,128)(2,1)}, f32[2,4,2,1024]{3,2,1...) custom-call(s32[2]{0:T(128)} %refs_0_.3, ...), custom_call_target="tpu_custom_call", output_to_operand_aliasing={{5}: (7, {}), {6}: (8, {}), {7}: (9, {}), {8}: (10, {})} | custom-call | tf_op jit(solution)/shard_map/attend/pallas_call | solution.py:864
  94.7 46.7 %middle.1 = (f32[2048,512]{1,0:T(8,128)}, f32[2048,512]{1,0:T(8,128)}, bf16[2048,512]{1,0:T(8,128)(2,1)}, bf16[32,80,512]{2,1,0:T(8,128)(2,1)}, bf16[32,64,512]{2,1,0:T(8,128)(2,1)}, /*index=5*/f32[16,512]{1,0:T(8,128)}) custom-call(f32[2048,512]{1,0:T(8,128)} %bitcast.28, f32[2048,512]{1,0:T(8,128)} %bitcast.34, bf16[2048,512]{1,0:T(8,128)(2,1)} %bitcast.38, ...), custom_call_target="tpu_custom_call" | custom-call | tf_op jit(solution)/shard_map/middle/pallas_call | solution.py:1051
  141.5 112.5 %pull.1 = (f32[2,1024,512]{2,1,0:T(8,128)}, bf16[1,2,1024,512]{3,2,1,0:T(8,128)(2,1)}, f32[16,1536]{1,0:T(8,128)}, f32[16,512]{1,0:T(8,128)}, f32[80,512]{1,0:T(8,128)}, /*index=5*/f32[64,512]{1,0:T(8,128)}) custom-call(bf16[2,2,8,1024,1024]{4,3,2,1,0:T(8,128)(2,1)} %get-tuple-element.72.refs_0_, bf16[2,1024,512]{2,1,0:T(8,128)(2,1)} %get-tuple-element.58.refs_1_, ...), custom_call_target="tpu_custom_call" | custom-call | tf_op jit(solution)/shard_map/pull/pallas_call | solution.py:1428
  254.0 5.6 %finish.1 = (f32[2,1024,512]{2,1,0:T(8,128)}, f32[16,1536]{1,0:T(8,128)}, f32[1,32]{1,0:T(1,128)}, f32[16,512]{1,0:T(8,128)}, f32[1,16]{1,0:T(1,128)}, /*index=5...) custom-call(f32[2,1024,512]{2,1,0:T(8,128)} %get-tuple-element.83.sh, ...), custom_call_target="tpu_custom_call" | custom-call | tf_op jit(solution)/shard_map/finish/pallas_call | solution.py:1573

commit v7 on v6

--- a/solution.py
+++ b/solution.py
@@ -328,13 +328,13 @@
     ]
 
     def small_start(stage):
-        vec_sent[stage] = vec[...]
+        vec_sent[stage] = vec[...].astype(BF)
         start(small[stage])
 
     def small_add(stage):
         wait(small[stage])
         for i in range(len(small[stage])):
-            vec[...] += vec_landing[stage, i]
+            vec[...] += vec_landing[stage, i].astype(F32)
 
     exchange = [
         links.copy(
@@ -467,8 +467,8 @@
             pltpu.VMEM(up.shape, BF),
             pltpu.VMEM(down.shape, BF),
             pltpu.VMEM(out.shape, BF),
-            pltpu.VMEM((len(order), 16, width), F32),
-            pltpu.VMEM((len(order), 3, 16, width), F32),
+            pltpu.VMEM((len(order), 16, width), BF),
+            pltpu.VMEM((len(order), 3, 16, width), BF),
             pltpu.VMEM((groups, local, width), BF),
             pltpu.VMEM((groups, local, 2 * width), BF),
             pltpu.SemaphoreType.DMA((4 * groups + 8,)),
@@ -1100,7 +1100,7 @@
     (vec_in,) = take(1)
     share_own, arrived, joint_out, vec_out = take(4)
     owned = take(2) if packed else ()
-    d_scores, joint_grad, total, dq_sums, dq_turned, weight_grad, bias_grad, shares = take(8)
+    d_scores, joint_grad, total, dq_sums, weight_grad, bias_grad, shares = take(7)
     share_send, share_recv, own_sem = take(3)
     step = pl.program_id(0)
     steps = pl.num_programs(0)
@@ -1252,6 +1252,14 @@
         sums = dot(d_scores[0, rows], picked[0]) + dot(d_scores[1, rows], picked[1])
         joint_grad[group, rows, at_keys] = (sums * SCALE).astype(BF)
 
+    @pl.when(step == 0)
+    def clear():
+        weight_grad[...] = jnp.zeros_like(weight_grad)
+        bias_grad[...] = jnp.zeros_like(bias_grad)
+        dq_sums[...] = jnp.zeros_like(dq_sums)
+
+    column = group * PAIRS + pair
+    value_sums = jnp.zeros((1, WIDE), F32)
     last_rows = None
     for at in range(0, local, chunk):
         rows = slice(at, at + chunk)
@@ -1260,39 +1268,25 @@
             e = e_part[0, 0, head, rows].astype(F32)
             d_scores[head, rows] = (e * (pulled - centre[head])).astype(BF)
         sums = dot(e_part[0, 0, 0, rows], grad[0]) + dot(e_part[0, 0, 1, rows], grad[1])
-        joint_grad[group, rows, at_values] = sums.astype(BF)
+        sums = sums.astype(BF)
+        joint_grad[group, rows, at_values] = sums
+        value_sums += jnp.sum(sums.astype(F32), axis=0, keepdims=True)
         if last_rows is not None:
             key_grad(last_rows)
         last_rows = rows
     key_grad(last_rows)
     for head in range(2):
         side = slice(head * HEAD, (head + 1) * HEAD)
-        dq = dot(keys_t, d_scores[head])[side]
-        dq_turned[side] = dq
-
-    @pl.when(step == 0)
-    def clear():
-        weight_grad[...] = jnp.zeros_like(weight_grad)
-        bias_grad[...] = jnp.zeros_like(bias_grad)
-        dq_sums[...] = jnp.zeros_like(dq_sums)
-
-    column = group * PAIRS + pair
+        dq_sums[column, side] += dot(keys_t, d_scores[head])[side]
+    bias_grad[1:2, at_queries] += value_sums
 
     @pl.when(own)
     def near():
-        dq = (dq_sums[column] + dq_turned[...]) * SCALE
-        dq = dq.T.astype(BF)
+        dq = (dq_sums[column] * SCALE).astype(BF).T
         joint_grad[group, :, at_queries] = dq
         bias_grad[0:1, at_queries] += jnp.sum(dq.astype(F32), axis=0, keepdims=True)
         weight_grad[:, at_queries] += dot(tokens_t[group], dq)
         weight_grad[:, at_both] += dot(tokens_t[group], joint_grad[group, :, at_both])
-
-    @pl.when(jnp.logical_not(own))
-    def far():
-        dq_sums[column] += dq_turned[...]
-
-    value_sums = jnp.sum(joint_grad[group, :, at_values].astype(F32), axis=0, keepdims=True)
-    bias_grad[1:2, at_queries] += value_sums
 
     for other in range(1, parts):
         for g in range(groups):
@@ -1460,7 +1454,6 @@
             pltpu.VMEM((groups, local, 3 * width), BF),
             pltpu.VMEM((groups, local, width), F32),
             pltpu.VMEM((each, WIDE, local), F32),
-            pltpu.VMEM((WIDE, local), F32),
             pltpu.VMEM((width, 3 * width), F32),
             pltpu.VMEM((8, width), F32),
             pltpu.VMEM((parts - 1, groups, local, width), BF),
@@ -1556,7 +1549,7 @@
 
 def finish(share, arrived, joint, vec, upper, lower, shards):
     groups, local, width = share.shape
-    block = min(512, local)
+    block = min(1024, local)
     each = local // block
 
     def moving(*lead):

time: 260 us -> 257 us (0.988)
  Pallas kernels: 259 us -> 256 us
where the time goes in v7:
time: 257 us
  Pallas kernels  256 us (100%)
    pallas_call x1, Pallas kernels, pull(): pl.pallas_call(functools.partial(pull_kernel, parts, groups, bits_dp, bit...  113 us
    pallas_call x1, Pallas kernels, attend(): pl.pallas_call(functools.partial(attend_kernel, parts, groups, steps, blo...  53.1 us
    pallas_call x1, Pallas kernels, middle(): pl.pallas_call(functools.partial(middle_kernel, packed), grid=(count // b...  46.7 us
    pallas_call x1, Pallas kernels, begin(): pl.pallas_call(functools.partial(begin_kernel, bits_dp, bits_seq, parts,...  38.6 us

profile of v7, /device:TPU:0, one launch (start us, length us, event | category | flops | bytes accessed | tf_op | source)
XLA Modules:
  0.0 256.6 jit_solution(3322220946728443943)
XLA Ops:
  0.6 38.6 %begin.1 = (bf16[2,1024,512]{2,1,0:T(8,128)(2,1)}, bf16[2,512,1024]{2,1,0:T(8,128)(2,1)}, bf16[1,2,1024,512]{3,2,1,0:T(8,128)(2,1)}, bf16[2,2,2,2,2,16,1536]{6,5...) custom-call(f32[2,1024,512]{2,1,0:T(8,128)} %refs_0_.2, ...), custom_call_target="tpu_custom_call" | custom-call | tf_op jit(solution)/shard_map/begin/pallas_call | solution.py:445
  39.3 53.1 %attend.1 = (bf16[2,2,8,1024,1024]{4,3,2,1,0:T(8,128)(2,1)}, bf16[2,1024,512]{2,1,0:T(8,128)(2,1)}, bf16[2,512,1024]{2,1,0:T(8,128)(2,1)}, f32[2,4,2,1024]{3,2,1...) custom-call(s32[2]{0:T(128)} %refs_0_.3, ...), custom_call_target="tpu_custom_call", output_to_operand_aliasing={{5}: (7, {}), {6}: (8, {}), {7}: (9, {}), {8}: (10, {})} | custom-call | tf_op jit(solution)/shard_map/attend/pallas_call | solution.py:864
  92.3 46.7 %middle.1 = (f32[2048,512]{1,0:T(8,128)}, f32[2048,512]{1,0:T(8,128)}, bf16[2048,512]{1,0:T(8,128)(2,1)}, bf16[32,80,512]{2,1,0:T(8,128)(2,1)}, bf16[32,64,512]{2,1,0:T(8,128)(2,1)}, /*index=5*/f32[16,512]{1,0:T(8,128)}) custom-call(f32[2048,512]{1,0:T(8,128)} %bitcast.28, f32[2048,512]{1,0:T(8,128)} %bitcast.34, bf16[2048,512]{1,0:T(8,128)(2,1)} %bitcast.38, ...), custom_call_target="tpu_custom_call" | custom-call | tf_op jit(solution)/shard_map/middle/pallas_call | solution.py:1051
  139.1 112.7 %pull.1 = (f32[2,1024,512]{2,1,0:T(8,128)}, bf16[1,2,1024,512]{3,2,1,0:T(8,128)(2,1)}, f32[16,1536]{1,0:T(8,128)}, f32[16,512]{1,0:T(8,128)}, f32[80,512]{1,0:T(8,128)}, /*index=5*/f32[64,512]{1,0:T(8,128)}) custom-call(bf16[2,2,8,1024,1024]{4,3,2,1,0:T(8,128)(2,1)} %get-tuple-element.72.refs_0_, bf16[2,1024,512]{2,1,0:T(8,128)(2,1)} %get-tuple-element.58.refs_1_, ...), custom_call_target="tpu_custom_call" | custom-call | tf_op jit(solution)/shard_map/pull/pallas_call | solution.py:1422
  251.8 4.6 %finish.1 = (f32[2,1024,512]{2,1,0:T(8,128)}, f32[16,1536]{1,0:T(8,128)}, f32[1,32]{1,0:T(1,128)}, f32[16,512]{1,0:T(8,128)}, f32[1,16]{1,0:T(1,128)}, /*index=5...) custom-call(f32[2,1024,512]{2,1,0:T(8,128)} %get-tuple-element.83.sh, ...), custom_call_target="tpu_custom_call" | custom-call | tf_op jit(solution)/shard_map/finish/pallas_call | solution.py:1566

commit v8 on v7

--- a/solution.py
+++ b/solution.py
@@ -356,7 +356,7 @@
 
     def projected(part):
         bias = jnp.concatenate([vec[10 + i : 11 + i] for i in range(3)], axis=1)[:, columns[part]]
-        block = min(256, local)
+        block = min(512, local)
         for g in range(groups):
 
             def rows_of(b, carry):
@@ -381,6 +381,8 @@
     for stage in range(last):
         done, group = dones[stage], order[stage]
         if stage < len(beside):
+            for copies in rest:
+                wait(copies)
             rest = [links.spread(full, done, group) for full in (up_w, down_w, out_w)]
             for copies in rest:
                 start(copies)
@@ -399,10 +401,10 @@
         if stage + 1 < last:
             wait(behind[stage])
             start(behind[stage + 1])
-        for copies in rest:
-            wait(copies)
-        rest = []
         if len(beside) <= stage < len(beside) + len(upper):
+            for copies in rest:
+                wait(copies)
+            rest = []
             wait(late)
             late = links.spread(up_w, done, group)
             start(late)

time: 257 us -> 256 us (level)
  no operation moved by 1% of the time
where the time goes in v8:
time: 256 us
  Pallas kernels  255 us (100%)
    pallas_call x1, Pallas kernels, pull(): pl.pallas_call(functools.partial(pull_kernel, parts, groups, bits_dp, bit...  112 us
    pallas_call x1, Pallas kernels, attend(): pl.pallas_call(functools.partial(attend_kernel, parts, groups, steps, blo...  52.9 us
    pallas_call x1, Pallas kernels, middle(): pl.pallas_call(functools.partial(middle_kernel, packed), grid=(count // b...  46.7 us
    pallas_call x1, Pallas kernels, begin(): pl.pallas_call(functools.partial(begin_kernel, bits_dp, bits_seq, parts,...  38.6 us

profile of v8, /device:TPU:0, one launch (start us, length us, event | category | flops | bytes accessed | tf_op | source)
XLA Modules:
  0.0 256.1 jit_solution(13870222449224094197)
XLA Ops:
  0.6 38.6 %begin.1 = (bf16[2,1024,512]{2,1,0:T(8,128)(2,1)}, bf16[2,512,1024]{2,1,0:T(8,128)(2,1)}, bf16[1,2,1024,512]{3,2,1,0:T(8,128)(2,1)}, bf16[2,2,2,2,2,16,1536]{6,5...) custom-call(f32[2,1024,512]{2,1,0:T(8,128)} %refs_0_.2, ...), custom_call_target="tpu_custom_call" | custom-call | tf_op jit(solution)/shard_map/begin/pallas_call | solution.py:447
  39.3 52.9 %attend.1 = (bf16[2,2,8,1024,1024]{4,3,2,1,0:T(8,128)(2,1)}, bf16[2,1024,512]{2,1,0:T(8,128)(2,1)}, bf16[2,512,1024]{2,1,0:T(8,128)(2,1)}, f32[2,4,2,1024]{3,2,1...) custom-call(s32[2]{0:T(128)} %refs_0_.3, ...), custom_call_target="tpu_custom_call", output_to_operand_aliasing={{5}: (7, {}), {6}: (8, {}), {7}: (9, {}), {8}: (10, {})} | custom-call | tf_op jit(solution)/shard_map/attend/pallas_call | solution.py:866
  92.1 46.7 %middle.1 = (f32[2048,512]{1,0:T(8,128)}, f32[2048,512]{1,0:T(8,128)}, bf16[2048,512]{1,0:T(8,128)(2,1)}, bf16[32,80,512]{2,1,0:T(8,128)(2,1)}, bf16[32,64,512]{2,1,0:T(8,128)(2,1)}, /*index=5*/f32[16,512]{1,0:T(8,128)}) custom-call(f32[2048,512]{1,0:T(8,128)} %bitcast.28, f32[2048,512]{1,0:T(8,128)} %bitcast.34, bf16[2048,512]{1,0:T(8,128)(2,1)} %bitcast.38, ...), custom_call_target="tpu_custom_call" | custom-call | tf_op jit(solution)/shard_map/middle/pallas_call | solution.py:1053
  138.9 112.5 %pull.1 = (f32[2,1024,512]{2,1,0:T(8,128)}, bf16[1,2,1024,512]{3,2,1,0:T(8,128)(2,1)}, f32[16,1536]{1,0:T(8,128)}, f32[16,512]{1,0:T(8,128)}, f32[80,512]{1,0:T(8,128)}, /*index=5*/f32[64,512]{1,0:T(8,128)}) custom-call(bf16[2,2,8,1024,1024]{4,3,2,1,0:T(8,128)(2,1)} %get-tuple-element.72.refs_0_, bf16[2,1024,512]{2,1,0:T(8,128)(2,1)} %get-tuple-element.58.refs_1_, ...), custom_call_target="tpu_custom_call" | custom-call | tf_op jit(solution)/shard_map/pull/pallas_call | solution.py:1424
  251.3 4.6 %finish.1 = (f32[2,1024,512]{2,1,0:T(8,128)}, f32[16,1536]{1,0:T(8,128)}, f32[1,32]{1,0:T(1,128)}, f32[16,512]{1,0:T(8,128)}, f32[1,16]{1,0:T(1,128)}, /*index=5...) custom-call(f32[2,1024,512]{2,1,0:T(8,128)} %get-tuple-element.83.sh, ...), custom_call_target="tpu_custom_call" | custom-call | tf_op jit(solution)/shard_map/finish/pallas_call | solution.py:1568
